TPU v7x, 32 devices: a whole 2x2x4 slice. The times are simulated.
32 devices in a mesh: depth: 32 (over z, y, x, core).
Axes of the slice: x: 2, y: 2, z: 4, core: 2. Of those that a mesh axis runs over, the one named last changes fastest.
Arguments:
- initial: bfloat16 [2, 256, 1536], replicated, may hold values from -6 to 6
- weights: bfloat16 [64, 1536, 1536], P('depth'), may hold values from -0.15625 to 0.15625
- biases: float32 [64, 1536], P('depth'), may hold values from -3 to 3
- step_sizes: float32 [64], P('depth'), may hold values from 0.02 to 0.2
Outputs:
- states: bfloat16 [64, 2, 256, 1536], P('depth')
All inputs are finite; a program needn't handle non-finite values.
Results may differ from a plain program's by a relative error of at most 0.013.
The roundings to bfloat16 on the way count: a program that leaves them out, or rounds other values in their place, can miss the bound.
Values may be sent and summed in bfloat16 or wider, within the bound.
No kernel may reach another device: no remote copies, remote signals or barrier semaphores. Data moves between devices by JAX's collectives and lax.ppermute only.
A program may use at most 64 MiB of HBM per device.

v0:
```python
import jax
import jax.numpy as jnp
from jax import lax
from jax.sharding import PartitionSpec as P

LAY_DEV = 2
INTERVAL = 8


row_blocks = 8


def passed_along(value, axis, steps):
    count = lax.axis_size(axis)
    leading, last = (max(0, -steps), min(count, count - steps))
    return lax.ppermute(value, axis, [(source, source + steps) for source in range(leading, last)])


def advance(entering, weights, biases, step_sizes):
    state = entering.astype(jnp.float32)
    outputs = []
    for layer in range(LAY_DEV):
        pre = (
            jnp.dot(state.astype(jnp.bfloat16), weights[layer], preferred_element_type=jnp.float32)
            + biases[layer]
        )
        state = state + step_sizes[layer] * jnp.tanh(pre)
        outputs.append(state)
    return jnp.stack(outputs)


def local(initial, weights, biases, step_sizes):
    device = lax.axis_index("depth")
    count = lax.axis_size("depth")
    groups = count // INTERVAL
    interval_index = device // INTERVAL
    width = initial.shape[2]
    start_state = initial.reshape(-1, width)
    entering = start_state
    passes = []
    for relax_pass in range(3):
        leaving = advance(entering, weights, biases, step_sizes)[-1].astype(jnp.bfloat16)
        arrived = passed_along(leaving, "depth", 1)
        entering = jnp.where(device == 0, start_state, arrived)
        passes.append(entering)
    entry_state = passes[1]
    fresh_state = passes[2]
    anchor = entry_state.astype(jnp.float32)
    residual_local = fresh_state.astype(jnp.float32) - anchor
    residual_ahead = passed_along(residual_local.astype(jnp.bfloat16), "depth", -INTERVAL).astype(
        residual_local.dtype
    )
    coarse_step = INTERVAL * LAY_DEV * step_sizes[0]

    def coarse_update(correction, base, residual):
        rows_here = base.shape[0]
        stacked = jnp.concatenate([base + correction.astype(jnp.float32), base], axis=0)
        pre = (
            jnp.dot(stacked.astype(jnp.bfloat16), weights[0], preferred_element_type=jnp.float32)
            + biases[0]
        )
        mapped = stacked + coarse_step * jnp.tanh(pre)
        return (mapped[:rows_here] - mapped[rows_here:] + residual).astype(jnp.bfloat16)

    def silent(correction, base, residual):
        return jnp.zeros_like(correction)

    zero_block = jnp.zeros_like(start_state)
    piece_rows = start_state.shape[0] // row_blocks

    def blocked_link(step_index, correction):
        send_block = step_index - interval_index
        sending = (send_block >= 0) & (send_block < row_blocks) & (interval_index < groups - 1)
        send_start = jnp.clip(send_block, 0, row_blocks - 1) * piece_rows
        part_correction = lax.dynamic_slice_in_dim(correction, send_start, piece_rows, 0)
        part_anchor = lax.dynamic_slice_in_dim(anchor, send_start, piece_rows, 0)
        part_residual = lax.dynamic_slice_in_dim(residual_ahead, send_start, piece_rows, 0)
        message = lax.cond(
            sending, coarse_update, silent, part_correction, part_anchor, part_residual
        )
        arrived = passed_along(message, "depth", INTERVAL)
        take_block = step_index - interval_index + 1
        taking = (interval_index >= 1) & (take_block >= 0) & (take_block < row_blocks)
        take_start = jnp.clip(take_block, 0, row_blocks - 1) * piece_rows
        current = lax.dynamic_slice_in_dim(correction, take_start, piece_rows, 0)
        updated = jnp.where(taking, arrived, current)
        return lax.dynamic_update_slice_in_dim(correction, updated, take_start, 0)

    correction = lax.fori_loop(0, groups - 2 + row_blocks, blocked_link, zero_block)
    corrected = anchor + correction.astype(jnp.float32)
    states = advance(corrected, weights, biases, step_sizes).astype(jnp.bfloat16)
    return states.reshape(states.shape[0], 2, -1, width)


def solution(mesh):
    placed = (P(), P("depth", None, None), P("depth", None), P("depth"))
    return jax.shard_map(
        local, mesh=mesh, in_specs=placed, out_specs=P("depth", None, None, None), check_vma=False
    )
```

profile of v0, /device:TPU:22, one launch (start us, length us, event | category | flops | bytes accessed | tf_op | source)
XLA Modules:
  0.0 292.7 jit_solution(15214031203499212147)
XLA Ops:
  2.2 6.8 %fusion.45 = f32[512,1536]{1,0:T(8,128)S(1)} fusion(bf16[512,1536]{1,0:T(8,128)(2,1)} %bitcast.114, bf16[2,1536,1536]{2,1,0:T(8,128)(2,1)} %param.9, f32[1536]{0:T(1024)S(1)} %get-tuple-element.294, f32[]{:T(128)} %bitcast.2), kind=kOutput, calls=%fused_computation.36 | convolution fusion | flops 2419064832 | bytes 11016704 | tf_op jit(solution)/shard_map/dot_general | solution.py:24
  14.6 19.9 %collective-permute-done.1 = bf16[512,1536]{1,0:T(8,128)(2,1)} collective-permute-done((bf16[512,1536]{1,0:T(8,128)(2,1)S(1)}, bf16[512,1536]{1,0:T(8,128)(2,1)}, u32[]{:S(2)}, u32[]{:S(2)}) %collective-permute-start.1) | collective-permute-done | bytes 1572896 | tf_op jit(solution)/shard_map/ppermute | solution.py:16
  34.5 7.2 %convert_add_fusion.2 = f32[512,1536]{1,0:T(8,128)S(1)} fusion(bf16[2,1536,1536]{2,1,0:T(8,128)(2,1)} %param.9, bf16[512,1536]{1,0:T(8,128)(2,1)S(1)} %bitcast.115, bf16[512,1536]{1,0:T(8,128)(2,1)} %collective-permute-done.1, f32[1536]{0:T(1024)S(1)} %get-tuple-element.294, f32[]{:T(128)} %bitcast.2, pred[]{:T(512)S(6)} %eq.2), kind=kOutput, calls=%fused_computation.67 | convolution fusion | flops 2420637696 | bytes 14165504 | tf_op jit(solution)/shard_map/dot_general | solution.py:24
  41.7 5.8 %fusion.145 = bf16[512,1536]{1,0:T(8,128)(2,1)S(1)} fusion(f32[512,1536]{1,0:T(8,128)S(1)} %convert_add_fusion.2, bf16[2,1536,1536]{2,1,0:T(8,128)(2,1)} %param.9, f32[1536]{0:T(1024)S(1)} %get-tuple-element.293, f32[]{:T(128)} %bitcast.4), kind=kOutput, calls=%fused_computation.78 | convolution fusion | flops 2419851264 | bytes 12591616 | tf_op jit(solution)/shard_map/dot_general | solution.py:24
  49.4 19.8 %collective-permute-done.2 = bf16[512,1536]{1,0:T(8,128)(2,1)S(1)} collective-permute-done((bf16[512,1536]{1,0:T(8,128)(2,1)S(1)}, bf16[512,1536]{1,0:T(8,128)(2,1)S(1)}, u32[]{:S(2)}, u32[]{:S(2)}) %collective-permute-start.2) | collective-permute-done | bytes 1572896 | tf_op jit(solution)/shard_map/ppermute | solution.py:16
  81.1 18.7 %collective-permute-done.3 = bf16[512,1536]{1,0:T(8,128)(2,1)S(1)} collective-permute-done((bf16[512,1536]{1,0:T(8,128)(2,1)S(1)}, bf16[512,1536]{1,0:T(8,128)(2,1)S(1)}, u32[]{:S(2)}, u32[]{:S(2)}) %collective-permute-start.3) | collective-permute-done | bytes 1572896 | tf_op jit(solution)/shard_map/ppermute | solution.py:16
  103.5 34.4 %collective-permute-done.4 = bf16[512,1536]{1,0:T(8,128)(2,1)} collective-permute-done((bf16[512,1536]{1,0:T(8,128)(2,1)S(1)}, bf16[512,1536]{1,0:T(8,128)(2,1)}, u32[]{:S(2)}, u32[]{:S(2)}) %collective-permute-start.4) | collective-permute-done | bytes 1572896 | tf_op jit(solution)/shard_map/ppermute | solution.py:16
  141.0 138.5 %while.14 = (s32[]{:T(128)}, bf16[512,1536]{1,0:T(8,128)(2,1)}, s32[]{:T(128)}, pred[]{:T(512)}, pred[]{:T(512)}, /*index=5*/f32[512,1536]{1,0:T(8,128)}, f32[]{...) while((s32[]{:T(128)}, bf16[512,1536]{1,0:T(8,128)(2,1)}, ...), condition=%wide.region_3.4_spmd, body=%wide.region_0.3_spmd.sunk | while | flops 605749248 | bytes 11228131 | solution.py:89
  143.0 7.1 %collective-permute-done = bf16[64,1536]{1,0:T(8,128)(2,1)S(1)} collective-permute-done((bf16[64,1536]{1,0:T(8,128)(2,1)S(1)}, bf16[64,1536]{1,0:T(8,128)(2,1)S(1)}, u32[]{:S(2)}, u32[]{:S(2)}) %collective-permute-start) | collective-permute-done | bytes 196640 | tf_op jit(solution)/shard_map/while/body/eval_jaxpr/ppermute | solution.py:16
  153.7 12.5 %collective-permute-done = bf16[64,1536]{1,0:T(8,128)(2,1)S(1)} collective-permute-done((bf16[64,1536]{1,0:T(8,128)(2,1)S(1)}, bf16[64,1536]{1,0:T(8,128)(2,1)S(1)}, u32[]{:S(2)}, u32[]{:S(2)}) %collective-permute-start) | collective-permute-done | bytes 196640 | tf_op jit(solution)/shard_map/while/body/eval_jaxpr/ppermute | solution.py:16
  167.9 4.5 %conditional.2 = (bf16[64,1536]{1,0:T(8,128)(2,1)S(1)}) conditional(s32[]{:T(128)} %convert_element_type.130, () %tuple.52, (s32[]{:T(128)}, f32[512,1536]{1,0:T(8,128)}, bf16[512,1536]{1,0:T(8,128)(2,1)}, f32[]{:T(128)}, bf16[2,1536,1536]{2,1,0:T(8,128)(2,1)}, /*index=5*/f32[2,1536]{1,0:T(2,128)S(1)}, f32[512,1536]{1,0:T(8,128)S(1)}) %tuple.53), branch_computations={%region_1.1_spmd, %region_2.2_spmd} | conditional | flops 605650944 | bytes 9851478 | solution.py:78
  174.4 6.9 %collective-permute-done = bf16[64,1536]{1,0:T(8,128)(2,1)S(1)} collective-permute-done((bf16[64,1536]{1,0:T(8,128)(2,1)S(1)}, bf16[64,1536]{1,0:T(8,128)(2,1)S(1)}, u32[]{:S(2)}, u32[]{:S(2)}) %collective-permute-start) | collective-permute-done | bytes 196640 | tf_op jit(solution)/shard_map/while/body/eval_jaxpr/ppermute | solution.py:16
  189.4 6.0 %collective-permute-done = bf16[64,1536]{1,0:T(8,128)(2,1)S(1)} collective-permute-done((bf16[64,1536]{1,0:T(8,128)(2,1)S(1)}, bf16[64,1536]{1,0:T(8,128)(2,1)S(1)}, u32[]{:S(2)}, u32[]{:S(2)}) %collective-permute-start) | collective-permute-done | bytes 196640 | tf_op jit(solution)/shard_map/while/body/eval_jaxpr/ppermute | solution.py:16
  197.1 4.5 %conditional.2 = (bf16[64,1536]{1,0:T(8,128)(2,1)S(1)}) conditional(s32[]{:T(128)} %convert_element_type.130, () %tuple.52, (s32[]{:T(128)}, f32[512,1536]{1,0:T(8,128)}, bf16[512,1536]{1,0:T(8,128)(2,1)}, f32[]{:T(128)}, bf16[2,1536,1536]{2,1,0:T(8,128)(2,1)}, /*index=5*/f32[2,1536]{1,0:T(2,128)S(1)}, f32[512,1536]{1,0:T(8,128)S(1)}) %tuple.53), branch_computations={%region_1.1_spmd, %region_2.2_spmd} | conditional | flops 605650944 | bytes 9851478 | solution.py:78
  203.5 5.6 %collective-permute-done = bf16[64,1536]{1,0:T(8,128)(2,1)S(1)} collective-permute-done((bf16[64,1536]{1,0:T(8,128)(2,1)S(1)}, bf16[64,1536]{1,0:T(8,128)(2,1)S(1)}, u32[]{:S(2)}, u32[]{:S(2)}) %collective-permute-start) | collective-permute-done | bytes 196640 | tf_op jit(solution)/shard_map/while/body/eval_jaxpr/ppermute | solution.py:16
  210.8 4.5 %conditional.2 = (bf16[64,1536]{1,0:T(8,128)(2,1)S(1)}) conditional(s32[]{:T(128)} %convert_element_type.130, () %tuple.52, (s32[]{:T(128)}, f32[512,1536]{1,0:T(8,128)}, bf16[512,1536]{1,0:T(8,128)(2,1)}, f32[]{:T(128)}, bf16[2,1536,1536]{2,1,0:T(8,128)(2,1)}, /*index=5*/f32[2,1536]{1,0:T(2,128)S(1)}, f32[512,1536]{1,0:T(8,128)S(1)}) %tuple.53), branch_computations={%region_1.1_spmd, %region_2.2_spmd} | conditional | flops 605650944 | bytes 9851478 | solution.py:78
  217.3 5.6 %collective-permute-done = bf16[64,1536]{1,0:T(8,128)(2,1)S(1)} collective-permute-done((bf16[64,1536]{1,0:T(8,128)(2,1)S(1)}, bf16[64,1536]{1,0:T(8,128)(2,1)S(1)}, u32[]{:S(2)}, u32[]{:S(2)}) %collective-permute-start) | collective-permute-done | bytes 196640 | tf_op jit(solution)/shard_map/while/body/eval_jaxpr/ppermute | solution.py:16
  224.5 4.5 %conditional.2 = (bf16[64,1536]{1,0:T(8,128)(2,1)S(1)}) conditional(s32[]{:T(128)} %convert_element_type.130, () %tuple.52, (s32[]{:T(128)}, f32[512,1536]{1,0:T(8,128)}, bf16[512,1536]{1,0:T(8,128)(2,1)}, f32[]{:T(128)}, bf16[2,1536,1536]{2,1,0:T(8,128)(2,1)}, /*index=5*/f32[2,1536]{1,0:T(2,128)S(1)}, f32[512,1536]{1,0:T(8,128)S(1)}) %tuple.53), branch_computations={%region_1.1_spmd, %region_2.2_spmd} | conditional | flops 605650944 | bytes 9851478 | solution.py:78
  231.0 5.6 %collective-permute-done = bf16[64,1536]{1,0:T(8,128)(2,1)S(1)} collective-permute-done((bf16[64,1536]{1,0:T(8,128)(2,1)S(1)}, bf16[64,1536]{1,0:T(8,128)(2,1)S(1)}, u32[]{:S(2)}, u32[]{:S(2)}) %collective-permute-start) | collective-permute-done | bytes 196640 | tf_op jit(solution)/shard_map/while/body/eval_jaxpr/ppermute | solution.py:16
  244.7 5.6 %collective-permute-done = bf16[64,1536]{1,0:T(8,128)(2,1)S(1)} collective-permute-done((bf16[64,1536]{1,0:T(8,128)(2,1)S(1)}, bf16[64,1536]{1,0:T(8,128)(2,1)S(1)}, u32[]{:S(2)}, u32[]{:S(2)}) %collective-permute-start) | collective-permute-done | bytes 196640 | tf_op jit(solution)/shard_map/while/body/eval_jaxpr/ppermute | solution.py:16
  258.5 5.6 %collective-permute-done = bf16[64,1536]{1,0:T(8,128)(2,1)S(1)} collective-permute-done((bf16[64,1536]{1,0:T(8,128)(2,1)S(1)}, bf16[64,1536]{1,0:T(8,128)(2,1)S(1)}, u32[]{:S(2)}, u32[]{:S(2)}) %collective-permute-start) | collective-permute-done | bytes 196640 | tf_op jit(solution)/shard_map/while/body/eval_jaxpr/ppermute | solution.py:16
  265.7 4.5 %conditional.2 = (bf16[64,1536]{1,0:T(8,128)(2,1)S(1)}) conditional(s32[]{:T(128)} %convert_element_type.130, () %tuple.52, (s32[]{:T(128)}, f32[512,1536]{1,0:T(8,128)}, bf16[512,1536]{1,0:T(8,128)(2,1)}, f32[]{:T(128)}, bf16[2,1536,1536]{2,1,0:T(8,128)(2,1)}, /*index=5*/f32[2,1536]{1,0:T(2,128)S(1)}, f32[512,1536]{1,0:T(8,128)S(1)}) %tuple.53), branch_computations={%region_1.1_spmd, %region_2.2_spmd} | conditional | flops 605650944 | bytes 9851478 | solution.py:78
  272.2 5.6 %collective-permute-done = bf16[64,1536]{1,0:T(8,128)(2,1)S(1)} collective-permute-done((bf16[64,1536]{1,0:T(8,128)(2,1)S(1)}, bf16[64,1536]{1,0:T(8,128)(2,1)S(1)}, u32[]{:S(2)}, u32[]{:S(2)}) %collective-permute-start) | collective-permute-done | bytes 196640 | tf_op jit(solution)/shard_map/while/body/eval_jaxpr/ppermute | solution.py:16
  279.5 8.0 %fusion.160 = (bf16[512,1536]{1,0:T(8,128)(2,1)S(1)}, f32[512,1536]{1,0:T(8,128)S(1)}) fusion(f32[1536]{0:T(1024)} %copy-done.5, bf16[2,1536,1536]{2,1,0:T(8,128)(2,1)} %get-tuple-element.438, bf16[512,1536]{1,0:T(8,128)(2,1)} %get-tuple-element.292, bf16[512,1536]{1,0:T(8,128)(2,1)} %copy-done.1, f32[]{:T(128)} %bitcast.2), kind=kOutput, calls=%fused_computation.91 | convolution fusion | flops 2424569856 | bytes 15737344 | tf_op jit(solution)/shard_map/dot_general | solution.py:24
  (97 shorter events, 118.0 us)
Async XLA Ops:
  2.2 69.1 %copy-start.5 = (f32[1536]{0:T(1024)}, f32[1536]{0:T(1024)S(1)}, u32[]{:S(2)}) copy-start(f32[1536]{0:T(1024)S(1)} %get-tuple-element.294) | copy-start | bytes 18436
  2.2 72.5 %copy-start.3 = (f32[1536]{0:T(1024)}, f32[1536]{0:T(1024)S(1)}, u32[]{:S(2)}) copy-start(f32[1536]{0:T(1024)S(1)} %get-tuple-element.293) | copy-start | bytes 18436
  9.1 25.3 %copy-start = (bf16[2,256,1536]{2,1,0:T(8,128)(2,1)S(1)}, bf16[2,256,1536]{2,1,0:T(8,128)(2,1)}, u32[]{:S(2)}) copy-start(bf16[2,256,1536]{2,1,0:T(8,128)(2,1)} %param.8) | copy-start | bytes 4718596
  12.6 21.8 %collective-permute-start.1 = (bf16[512,1536]{1,0:T(8,128)(2,1)S(1)}, bf16[512,1536]{1,0:T(8,128)(2,1)}, u32[]{:S(2)}, u32[]{:S(2)}) collective-permute-start(bf16[512,1536]{1,0:T(8,128)(2,1)S(1)} %fusion.148), channel_id=1, source_target_pairs={{0,1},{1,2},{2,3},{3,4},{4,5},{5,6},{6,7},{7,8},{8,9},{9,10},{10,1... | collective-permute-start | bytes 4718600 | tf_op jit(solution)/shard_map/ppermute | solution.py:16
  34.5 36.9 %slice-start = ((s8[9437184]{0:T(1024)(128)(4,1)}), s8[4194304]{0:T(1024)(128)(4,1)S(1)}, s32[]{:S(2)}) async-start(s8[9437184]{0:T(1024)(128)(4,1)} %bitcast.118), calls=%async_computation | async-start | bytes 8388608
  34.5 36.9 %slice-start.1 = ((s8[9437184]{0:T(1024)(128)(4,1)}), s8[4194304]{0:T(1024)(128)(4,1)S(1)}, s32[]{:S(2)}) async-start(s8[9437184]{0:T(1024)(128)(4,1)} %bitcast.118), calls=%async_computation.1 | async-start | bytes 8388608
  41.7 29.7 %slice-start.2 = ((s8[9437184]{0:T(1024)(128)(4,1)}), s8[1048576]{0:T(1024)(128)(4,1)S(1)}, s32[]{:S(2)}) async-start(s8[9437184]{0:T(1024)(128)(4,1)} %bitcast.118), calls=%async_computation.2 | async-start | bytes 2097152
  47.5 21.7 %collective-permute-start.2 = (bf16[512,1536]{1,0:T(8,128)(2,1)S(1)}, bf16[512,1536]{1,0:T(8,128)(2,1)S(1)}, u32[]{:S(2)}, u32[]{:S(2)}) collective-permute-start(bf16[512,1536]{1,0:T(8,128)(2,1)S(1)} %fusion.145), channel_id=1, source_target_pairs={{0,1},{1,2},{2,3},{3,4},{4,5},{5,6},{6,7},{7,8},{8,9},{9,10},{10,1... | collective-permute-start | bytes 4718600 | tf_op jit(solution)/shard_map/ppermute | solution.py:16
  71.3 28.5 %copy-start.1 = (bf16[512,1536]{1,0:T(8,128)(2,1)}, bf16[512,1536]{1,0:T(8,128)(2,1)S(1)}, u32[]{:S(2)}) copy-start(bf16[512,1536]{1,0:T(8,128)(2,1)S(1)} %get-tuple-element.316) | copy-start | bytes 4718596
  78.1 21.7 %collective-permute-start.3 = (bf16[512,1536]{1,0:T(8,128)(2,1)S(1)}, bf16[512,1536]{1,0:T(8,128)(2,1)S(1)}, u32[]{:S(2)}, u32[]{:S(2)}) collective-permute-start(bf16[512,1536]{1,0:T(8,128)(2,1)S(1)} %fusion.142), channel_id=1, source_target_pairs={{0,1},{1,2},{2,3},{3,4},{4,5},{5,6},{6,7},{7,8},{8,9},{9,10},{10,1... | collective-permute-start | bytes 4718600 | tf_op jit(solution)/shard_map/ppermute | solution.py:16
  100.5 37.4 %collective-permute-start.4 = (bf16[512,1536]{1,0:T(8,128)(2,1)S(1)}, bf16[512,1536]{1,0:T(8,128)(2,1)}, u32[]{:S(2)}, u32[]{:S(2)}) collective-permute-start(bf16[512,1536]{1,0:T(8,128)(2,1)S(1)} %subtract_convert_fusion), channel_id=1, source_target_pairs={{8,0},{9,1},{10,2},{11,3},{12,4},{13,5},{14,6},{15,7},{16,8},{17,9... | collective-permute-start | bytes 4718600 | tf_op jit(solution)/shard_map/ppermute | solution.py:16
  103.5 37.5 %copy-start.2 = (f32[2,1536]{1,0:T(2,128)S(1)}, f32[2,1536]{1,0:T(2,128)}, u32[]{:S(2)}) copy-start(f32[2,1536]{1,0:T(2,128)} %param.10) | copy-start | bytes 36868
  141.0 9.0 %collective-permute-start = (bf16[64,1536]{1,0:T(8,128)(2,1)S(1)}, bf16[64,1536]{1,0:T(8,128)(2,1)S(1)}, u32[]{:S(2)}, u32[]{:S(2)}) collective-permute-start(bf16[64,1536]{1,0:T(8,128)(2,1)S(1)} %get-tuple-element.432), channel_id=1, source_target_pairs={{0,8},{1,9},{2,10},{3,11},{4,12},{5,13},{6,14},{7,15},{8,16},{9,17... | collective-permute-start | bytes 589832 | tf_op jit(solution)/shard_map/while/body/eval_jaxpr/ppermute | solution.py:16
  151.8 14.5 %collective-permute-start = (bf16[64,1536]{1,0:T(8,128)(2,1)S(1)}, bf16[64,1536]{1,0:T(8,128)(2,1)S(1)}, u32[]{:S(2)}, u32[]{:S(2)}) collective-permute-start(bf16[64,1536]{1,0:T(8,128)(2,1)S(1)} %get-tuple-element.432), channel_id=1, source_target_pairs={{0,8},{1,9},{2,10},{3,11},{4,12},{5,13},{6,14},{7,15},{8,16},{9,17... | collective-permute-start | bytes 589832 | tf_op jit(solution)/shard_map/while/body/eval_jaxpr/ppermute | solution.py:16
  172.4 8.8 %collective-permute-start = (bf16[64,1536]{1,0:T(8,128)(2,1)S(1)}, bf16[64,1536]{1,0:T(8,128)(2,1)S(1)}, u32[]{:S(2)}, u32[]{:S(2)}) collective-permute-start(bf16[64,1536]{1,0:T(8,128)(2,1)S(1)} %get-tuple-element.432), channel_id=1, source_target_pairs={{0,8},{1,9},{2,10},{3,11},{4,12},{5,13},{6,14},{7,15},{8,16},{9,17... | collective-permute-start | bytes 589832 | tf_op jit(solution)/shard_map/while/body/eval_jaxpr/ppermute | solution.py:16
  187.4 8.0 %collective-permute-start = (bf16[64,1536]{1,0:T(8,128)(2,1)S(1)}, bf16[64,1536]{1,0:T(8,128)(2,1)S(1)}, u32[]{:S(2)}, u32[]{:S(2)}) collective-permute-start(bf16[64,1536]{1,0:T(8,128)(2,1)S(1)} %get-tuple-element.432), channel_id=1, source_target_pairs={{0,8},{1,9},{2,10},{3,11},{4,12},{5,13},{6,14},{7,15},{8,16},{9,17... | collective-permute-start | bytes 589832 | tf_op jit(solution)/shard_map/while/body/eval_jaxpr/ppermute | solution.py:16
  201.6 7.6 %collective-permute-start = (bf16[64,1536]{1,0:T(8,128)(2,1)S(1)}, bf16[64,1536]{1,0:T(8,128)(2,1)S(1)}, u32[]{:S(2)}, u32[]{:S(2)}) collective-permute-start(bf16[64,1536]{1,0:T(8,128)(2,1)S(1)} %get-tuple-element.432), channel_id=1, source_target_pairs={{0,8},{1,9},{2,10},{3,11},{4,12},{5,13},{6,14},{7,15},{8,16},{9,17... | collective-permute-start | bytes 589832 | tf_op jit(solution)/shard_map/while/body/eval_jaxpr/ppermute | solution.py:16
  215.3 7.6 %collective-permute-start = (bf16[64,1536]{1,0:T(8,128)(2,1)S(1)}, bf16[64,1536]{1,0:T(8,128)(2,1)S(1)}, u32[]{:S(2)}, u32[]{:S(2)}) collective-permute-start(bf16[64,1536]{1,0:T(8,128)(2,1)S(1)} %get-tuple-element.432), channel_id=1, source_target_pairs={{0,8},{1,9},{2,10},{3,11},{4,12},{5,13},{6,14},{7,15},{8,16},{9,17... | collective-permute-start | bytes 589832 | tf_op jit(solution)/shard_map/while/body/eval_jaxpr/ppermute | solution.py:16
  229.0 7.6 %collective-permute-start = (bf16[64,1536]{1,0:T(8,128)(2,1)S(1)}, bf16[64,1536]{1,0:T(8,128)(2,1)S(1)}, u32[]{:S(2)}, u32[]{:S(2)}) collective-permute-start(bf16[64,1536]{1,0:T(8,128)(2,1)S(1)} %get-tuple-element.432), channel_id=1, source_target_pairs={{0,8},{1,9},{2,10},{3,11},{4,12},{5,13},{6,14},{7,15},{8,16},{9,17... | collective-permute-start | bytes 589832 | tf_op jit(solution)/shard_map/while/body/eval_jaxpr/ppermute | solution.py:16
  242.8 7.6 %collective-permute-start = (bf16[64,1536]{1,0:T(8,128)(2,1)S(1)}, bf16[64,1536]{1,0:T(8,128)(2,1)S(1)}, u32[]{:S(2)}, u32[]{:S(2)}) collective-permute-start(bf16[64,1536]{1,0:T(8,128)(2,1)S(1)} %get-tuple-element.432), channel_id=1, source_target_pairs={{0,8},{1,9},{2,10},{3,11},{4,12},{5,13},{6,14},{7,15},{8,16},{9,17... | collective-permute-start | bytes 589832 | tf_op jit(solution)/shard_map/while/body/eval_jaxpr/ppermute | solution.py:16
  256.5 7.6 %collective-permute-start = (bf16[64,1536]{1,0:T(8,128)(2,1)S(1)}, bf16[64,1536]{1,0:T(8,128)(2,1)S(1)}, u32[]{:S(2)}, u32[]{:S(2)}) collective-permute-start(bf16[64,1536]{1,0:T(8,128)(2,1)S(1)} %get-tuple-element.432), channel_id=1, source_target_pairs={{0,8},{1,9},{2,10},{3,11},{4,12},{5,13},{6,14},{7,15},{8,16},{9,17... | collective-permute-start | bytes 589832 | tf_op jit(solution)/shard_map/while/body/eval_jaxpr/ppermute | solution.py:16
  270.2 7.6 %collective-permute-start = (bf16[64,1536]{1,0:T(8,128)(2,1)S(1)}, bf16[64,1536]{1,0:T(8,128)(2,1)S(1)}, u32[]{:S(2)}, u32[]{:S(2)}) collective-permute-start(bf16[64,1536]{1,0:T(8,128)(2,1)S(1)} %get-tuple-element.432), channel_id=1, source_target_pairs={{0,8},{1,9},{2,10},{3,11},{4,12},{5,13},{6,14},{7,15},{8,16},{9,17... | collective-permute-start | bytes 589832 | tf_op jit(solution)/shard_map/while/body/eval_jaxpr/ppermute | solution.py:16
  279.5 8.0 %copy-start.4 = (f32[1536]{0:T(1024)S(1)}, f32[1536]{0:T(1024)}, u32[]{:S(2)}) copy-start(f32[1536]{0:T(1024)} %copy-done.3) | copy-start | bytes 18436
  279.5 8.0 %copy-start.7 = (bf16[2,1536,1536]{2,1,0:T(8,128)(2,1)S(1)}, bf16[2,1536,1536]{2,1,0:T(8,128)(2,1)}, u32[]{:S(2)}) copy-start(bf16[2,1536,1536]{2,1,0:T(8,128)(2,1)} %get-tuple-element.438) | copy-start | bytes 28311556
  (1 other events, 6.9 us)
where the time goes:
time: 294 us; the launch traced here: 293 us
  waiting for transfers between devices  159 us (54%)
  matrix products  67.1 us (23%)
  other arithmetic  33.1 us (11%)
  starting transfers between devices  28.4 us (10%)
  local copies, waits for them, and re-layouts  3.72 us (1%)
    ppermute x14, waiting for transfers between devices, passed_along(): lax.ppermute(value, axis, [(source, source + steps) for source in range(l...  159 us
    dot_general x8, matrix products, advance(): jnp.dot(state.astype(jnp.bfloat16), weights[layer], preferred_element_typ...  41.3 us
    ppermute x14, starting transfers between devices, passed_along(): lax.ppermute(value, axis, [(source, source + steps) for source in range(l...  28.4 us
    dot_general x8, matrix products, coarse_update(): jnp.dot(stacked.astype(jnp.bfloat16), weights[0], preferred_element_type=...  25.7 us
    dynamic_update_slice x10, other arithmetic, blocked_link(): return lax.dynamic_update_slice_in_dim(correction, updated, take_start, 0)  16.6 us
    add x8, other arithmetic, coarse_update(): base + correction.astype(jnp.float32)  9.28 us
  transfers between devices with their start and end apart: 14, of which 14 were waited for; matrix products, arithmetic and copies ran while one was open for 0% of the time, Pallas kernels for 0%

commit v1 on v0

v1 whole, which is shorter than its diff:
```python
import functools

import jax
import jax.numpy as jnp
from jax import lax
from jax.experimental import pallas as pl
from jax.experimental.pallas import tpu as pltpu
from jax.sharding import PartitionSpec as P

LAY_DEV = 2
INTERVAL = 8

CHUNKS = 4
TILE = 512
VMEM_BYTES = 20 << 20
VMEM = pl.BlockSpec(memory_space=pltpu.VMEM)
ANY = pl.BlockSpec(memory_space=pl.ANY)


def held(value):
    return pltpu.with_memory_space_constraint(value, pltpu.VMEM)


def kept(shape, kind):
    return pltpu.VMEM(shape, kind)


def in_hbm(value):
    return pltpu.with_memory_space_constraint(value, pltpu.HBM)


def passed_along(value, pairs):
    return lax.ppermute(value, "depth", pairs)


def tiles(width):
    tile = TILE if width % TILE == 0 else width
    return [slice(low, low + tile) for low in range(0, width, tile)]


def product(state, weight):
    return jnp.dot(state, weight, preferred_element_type=jnp.float32)


def block_layers(entering, w_ref, p_ref, out_ref, t_ref, state, rounded):
    width = w_ref.shape[2]
    for cols in tiles(width):
        bent = jnp.tanh(product(rounded[...], w_ref[0, :, cols]) + p_ref[0:1, cols])
        if t_ref is not None:
            t_ref[:, cols] = bent
        state[:, cols] = entering[:, cols].astype(jnp.float32) + p_ref[2:3, cols] * bent


def second_layer(w_ref, p_ref, out_ref, state, rounded):
    for cols in tiles(w_ref.shape[2]):
        bent = jnp.tanh(product(rounded[...], w_ref[1, :, cols]) + p_ref[1:2, cols])
        out_ref[:, cols] = (state[:, cols] + p_ref[3:4, cols] * bent).astype(jnp.bfloat16)


def opening_kernel(start_ref, w_hbm, b_ref, h_ref, out_ref, w_ref, p_ref, state, rounded, sems):
    width = w_hbm.shape[2]
    copies = []
    for layer in range(2):
        for cols in tiles(width):
            copy = pltpu.make_async_copy(
                w_hbm.at[layer, :, cols], w_ref.at[layer, :, cols], sems.at[len(copies)]
            )
            copy.start()
            copies.append(copy)
    p_ref[0:2, :] = b_ref[...]
    for layer in range(2):
        p_ref[2 + layer : 3 + layer, :] = jnp.full((1, width), h_ref[layer], jnp.float32)
    p_ref[4:8, :] = jnp.zeros((4, width), jnp.float32)
    for index, cols in enumerate(tiles(width)):
        copies[index].wait()
        bent = jnp.tanh(product(start_ref[...], w_ref[0, :, cols]) + p_ref[0:1, cols])
        state[:, cols] = start_ref[:, cols].astype(jnp.float32) + p_ref[2:3, cols] * bent
    rounded[...] = state[...].astype(jnp.bfloat16)
    for index, cols in enumerate(tiles(width)):
        copies[len(tiles(width)) + index].wait()
        bent = jnp.tanh(product(rounded[...], w_ref[1, :, cols]) + p_ref[1:2, cols])
        out_ref[:, cols] = (state[:, cols] + p_ref[3:4, cols] * bent).astype(jnp.bfloat16)


def pass_kernel(keep, start_ref, arrived_ref, w_ref, p_ref, out_ref, *rest):
    if keep:
        t_ref, entering, state, rounded = rest
    else:
        t_ref, (entering, state, rounded) = None, rest
    first = lax.axis_index("depth") == 0
    entering[...] = jnp.where(first, start_ref[...], arrived_ref[...])
    block_layers(entering, w_ref, p_ref, out_ref, t_ref, state, entering)
    rounded[...] = state[...].astype(jnp.bfloat16)
    second_layer(w_ref, p_ref, out_ref, state, rounded)


def correction_of(start_ref, entry_ref, fresh_ref, moved_ref, entry, correction):
    device = lax.axis_index("depth")
    entry[...] = jnp.where(device == 0, start_ref[...], entry_ref[...])
    anchor = entry[...].astype(jnp.float32)
    residual = fresh_ref[...].astype(jnp.float32) - anchor
    total = residual if moved_ref is None else moved_ref[...].astype(jnp.float32) + residual
    total = jnp.where(device < INTERVAL, 0.0, total)
    correction[...] = total.astype(jnp.bfloat16)


def coarse_kernel(group, *refs):
    if group == 1:
        start_ref, entry_ref, fresh_ref, t_ref, w_ref, p_ref, out_ref, entry, correction, rounded = refs
        moved_ref = None
    else:
        (start_ref, entry_ref, fresh_ref, moved_ref, t_ref, w_ref, p_ref, out_ref, entry, correction, rounded) = refs

    @pl.when(lax.axis_index("depth") // INTERVAL == group)
    def _():
        correction_of(start_ref, entry_ref, fresh_ref, moved_ref, entry, correction)
        rounded[...] = (entry[...].astype(jnp.float32) + correction[...].astype(jnp.float32)).astype(jnp.bfloat16)
        for cols in tiles(w_ref.shape[2]):
            bent = jnp.tanh(product(rounded[...], w_ref[0, :, cols]) + p_ref[0:1, cols])
            change = (INTERVAL * LAY_DEV) * p_ref[2:3, cols] * (bent - t_ref[:, cols])
            out_ref[:, cols] = (correction[:, cols].astype(jnp.float32) + change).astype(jnp.bfloat16)


def final_kernel(start_ref, entry_ref, fresh_ref, moved_ref, w_ref, p_ref, out_ref, entry, correction, state, rounded):
    correction_of(start_ref, entry_ref, fresh_ref, moved_ref, entry, correction)
    state[...] = entry[...].astype(jnp.float32) + correction[...].astype(jnp.float32)
    rounded[...] = state[...].astype(jnp.bfloat16)
    for cols in tiles(w_ref.shape[2]):
        bent = jnp.tanh(product(rounded[...], w_ref[0, :, cols]) + p_ref[0:1, cols])
        state[:, cols] = state[:, cols] + p_ref[2:3, cols] * bent
    rounded[...] = state[...].astype(jnp.bfloat16)
    out_ref[0] = rounded[...]
    second_layer(w_ref, p_ref, out_ref.at[1], state, rounded)


def local(initial, weights, biases, step_sizes):
    count = lax.axis_size("depth")
    groups = count // INTERVAL
    width = initial.shape[2]
    start = initial.reshape(-1, width)
    rows = start.shape[0] // CHUNKS
    one_on = [(source, source + 1) for source in range(count - 1)]

    def call(body, outs, scratch, *operands, specs=None, layers=2):
        flops = 2 * rows * width * width * layers
        return pl.pallas_call(
            body,
            out_shape=outs,
            in_specs=specs or [VMEM] * len(operands),
            out_specs=jax.tree.map(lambda _: VMEM, outs),
            scratch_shapes=scratch,
            compiler_params=pltpu.CompilerParams(vmem_limit_bytes=VMEM_BYTES),
            cost_estimate=pl.CostEstimate(flops=flops, bytes_accessed=rows * width * 8, transcendentals=rows * width * layers),
        )(*(operands if specs else [held(operand) for operand in operands]))

    wide = lambda kind: pltpu.VMEM((rows, width), kind)
    narrow = jax.ShapeDtypeStruct((rows, width), jnp.bfloat16)
    starts = [start[chunk * rows : (chunk + 1) * rows] for chunk in range(CHUNKS)]

    parts = len(tiles(width))
    leaving, w, p = call(
        opening_kernel,
        (narrow, kept(weights.shape, jnp.bfloat16), kept((8, width), jnp.float32)),
        [wide(jnp.float32), wide(jnp.bfloat16), pltpu.SemaphoreType.DMA((2 * parts,))],
        starts[0], in_hbm(weights), biases, step_sizes,
        specs=[VMEM, ANY, VMEM, pl.BlockSpec(memory_space=pltpu.SMEM)],
    )
    entry, fresh, bent = [None] * CHUNKS, [None] * CHUNKS, [None] * CHUNKS
    arrived = [passed_along(leaving, one_on)]
    plain = [wide(jnp.bfloat16), wide(jnp.float32), wide(jnp.bfloat16)]
    for chunk in range(1, CHUNKS):
        leaving = call(functools.partial(pass_kernel, False), narrow, plain, starts[chunk], starts[chunk], w, p)
        arrived.append(passed_along(leaving, one_on))
    for chunk in range(CHUNKS):
        leaving = call(functools.partial(pass_kernel, False), narrow, plain, starts[chunk], arrived[chunk], w, p)
        entry[chunk] = passed_along(leaving, one_on)
    for chunk in range(CHUNKS):
        leaving, bent[chunk] = call(
            functools.partial(pass_kernel, True),
            (narrow, kept((rows, width), jnp.float32)), plain, starts[chunk], entry[chunk], w, p,
        )
        fresh[chunk] = passed_along(leaving, one_on)
    moved = [None] * CHUNKS
    group_index = lax.axis_index("depth") // INTERVAL
    for group in range(1, groups - 1):
        ahead = [(source, source + INTERVAL) for source in range(group * INTERVAL, (group + 1) * INTERVAL)]
        for chunk in range(CHUNKS):
            operands = [starts[chunk], entry[chunk], fresh[chunk]]
            if group > 1:
                operands.append(moved[chunk])
            delta = call(
                functools.partial(coarse_kernel, group), narrow,
                [wide(jnp.bfloat16)] * 3, *operands, bent[chunk], w, p, layers=1,
            )
            sent = passed_along(delta, ahead)
            moved[chunk] = sent if group == 1 else jnp.where(group_index == group + 1, sent, moved[chunk])
    outs = []
    for chunk in range(CHUNKS):
        outs.append(
            call(
                final_kernel, jax.ShapeDtypeStruct((2, rows, width), jnp.bfloat16),
                [wide(jnp.bfloat16), wide(jnp.bfloat16), wide(jnp.float32), wide(jnp.bfloat16)],
                starts[chunk], entry[chunk], fresh[chunk], moved[chunk], w, p,
            )
        )
    states = jnp.concatenate(outs, axis=1)
    return states.reshape(states.shape[0], initial.shape[0], -1, width)


def solution(mesh):
    placed = (P(), P("depth", None, None), P("depth", None), P("depth"))
    return jax.shard_map(
        local, mesh=mesh, in_specs=placed, out_specs=P("depth", None, None, None), check_vma=False
    )
```

time: 294 us -> 120 us (0.41)
  the two profiles are of different devices: /device:TPU:22 before, /device:TPU:23 now
where the time goes in v1:
time: 120 us; the launch traced here: 119 us
  starting transfers between devices  41.2 us (34%)
  Pallas kernels  36.4 us (30%)
  waiting for transfers between devices  27.1 us (23%)
  local copies, waits for them, and re-layouts  8.7 us (7%)
  other arithmetic  4.97 us (4%)
    ppermute x20, starting transfers between devices, passed_along(): return lax.ppermute(value, 'depth', pairs)  41.2 us
    pallas_call x24, Pallas kernels, call(): pl.pallas_call(body, out_shape=outs, in_specs=specs or [VMEM] * len(opera...  36.4 us
    ppermute x20, waiting for transfers between devices, passed_along(): return lax.ppermute(value, 'depth', pairs)  27.1 us
    unnamed x48, local copies, waits for them, and re-layouts  7.25 us
    select_n x4, other arithmetic, local(): jnp.where(group_index == group + 1, sent, moved[chunk])  3.18 us
  transfers between devices with their start and end apart: 20, of which 7 were waited for; matrix products, arithmetic and copies ran while one was open for 2% of the time, Pallas kernels for 25%

profile of v1, /device:TPU:23, one launch (start us, length us, event | category | flops | bytes accessed | tf_op | source)
XLA Modules:
  0.0 119.1 jit_solution(6673789342647507904)
XLA Ops:
  2.8 4.8 %shard_map.46 = (bf16[128,1536]{1,0:T(8,128)(2,1)S(1)}, bf16[2,1536,1536]{2,1,0:T(8,128)(2,1)S(1)}, f32[8,1536]{1,0:T(8,128)S(1)}) custom-call(bf16[128,1536]{1,0:T(8,128)(2,1)S(1)} %get-tuple-element.30.start_ref.refs_0_, bf16[2,1536,1536]{2,1,0:T(8,128)(2,1)} %w_hbm.1, f32[2,1536]{1,0:T(2,128)S(1)} %copy-done.19, f32[2]{0:T(128)S(1)} %copy-done.20), custom_call_target="tpu_custom_call" | custom-call | flops 1207959552 | bytes 1572864 | tf_op jit(solution)/shard_map/pallas_call | solution.py:146
  7.6 3.7 %collective-permute-start = (bf16[128,1536]{1,0:T(8,128)(2,1)S(1)}, bf16[128,1536]{1,0:T(8,128)(2,1)S(1)}, u32[]{:S(2)}, u32[]{:S(2)}) collective-permute-start(bf16[128,1536]{1,0:T(8,128)(2,1)S(1)} %get-tuple-element.16), channel_id=1, source_target_pairs={{0,1},{1,2},{2,3},{3,4},{4,5},{5,6},{6,7},{7,8},{8,9},{9,10},{10,1... | collective-permute-start | bytes 1179656 | tf_op jit(solution)/shard_map/ppermute | solution.py:33
  12.7 1.9 %collective-permute-start.15 = (bf16[128,1536]{1,0:T(8,128)(2,1)S(1)}, bf16[128,1536]{1,0:T(8,128)(2,1)S(1)}, u32[]{:S(2)}, u32[]{:S(2)}) collective-permute-start(bf16[128,1536]{1,0:T(8,128)(2,1)S(1)} %shard_map.64), channel_id=1, source_target_pairs={{0,1},{1,2},{2,3},{3,4},{4,5},{5,6},{6,7},{7,8},{8,9},{9,10},{10,1... | collective-permute-start | bytes 1179656 | tf_op jit(solution)/shard_map/ppermute | solution.py:33
  16.1 3.5 %collective-permute-start.10 = (bf16[128,1536]{1,0:T(8,128)(2,1)S(1)}, bf16[128,1536]{1,0:T(8,128)(2,1)S(1)}, u32[]{:S(2)}, u32[]{:S(2)}) collective-permute-start(bf16[128,1536]{1,0:T(8,128)(2,1)S(1)} %shard_map.58), channel_id=1, source_target_pairs={{0,1},{1,2},{2,3},{3,4},{4,5},{5,6},{6,7},{7,8},{8,9},{9,10},{10,1... | collective-permute-start | bytes 1179656 | tf_op jit(solution)/shard_map/ppermute | solution.py:33
  21.0 1.9 %collective-permute-start.5 = (bf16[128,1536]{1,0:T(8,128)(2,1)S(1)}, bf16[128,1536]{1,0:T(8,128)(2,1)S(1)}, u32[]{:S(2)}, u32[]{:S(2)}) collective-permute-start(bf16[128,1536]{1,0:T(8,128)(2,1)S(1)} %shard_map.52), channel_id=1, source_target_pairs={{0,1},{1,2},{2,3},{3,4},{4,5},{5,6},{6,7},{7,8},{8,9},{9,10},{10,1... | collective-permute-start | bytes 1179656 | tf_op jit(solution)/shard_map/ppermute | solution.py:33
  24.4 3.5 %collective-permute-start.1 = (bf16[128,1536]{1,0:T(8,128)(2,1)S(1)}, bf16[128,1536]{1,0:T(8,128)(2,1)S(1)}, u32[]{:S(2)}, u32[]{:S(2)}) collective-permute-start(bf16[128,1536]{1,0:T(8,128)(2,1)S(1)} %shard_map.47), channel_id=1, source_target_pairs={{0,1},{1,2},{2,3},{3,4},{4,5},{5,6},{6,7},{7,8},{8,9},{9,10},{10,1... | collective-permute-start | bytes 1179656 | tf_op jit(solution)/shard_map/ppermute | solution.py:33
  29.4 1.9 %collective-permute-start.16 = (bf16[128,1536]{1,0:T(8,128)(2,1)S(1)}, bf16[128,1536]{1,0:T(8,128)(2,1)S(1)}, u32[]{:S(2)}, u32[]{:S(2)}) collective-permute-start(bf16[128,1536]{1,0:T(8,128)(2,1)S(1)} %shard_map.65), channel_id=1, source_target_pairs={{0,1},{1,2},{2,3},{3,4},{4,5},{5,6},{6,7},{7,8},{8,9},{9,10},{10,1... | collective-permute-start | bytes 1179656 | tf_op jit(solution)/shard_map/ppermute | solution.py:33
  32.8 3.5 %collective-permute-start.11 = (bf16[128,1536]{1,0:T(8,128)(2,1)S(1)}, bf16[128,1536]{1,0:T(8,128)(2,1)S(1)}, u32[]{:S(2)}, u32[]{:S(2)}) collective-permute-start(bf16[128,1536]{1,0:T(8,128)(2,1)S(1)} %shard_map.59), channel_id=1, source_target_pairs={{0,1},{1,2},{2,3},{3,4},{4,5},{5,6},{6,7},{7,8},{8,9},{9,10},{10,1... | collective-permute-start | bytes 1179656 | tf_op jit(solution)/shard_map/ppermute | solution.py:33
  37.7 2.1 %collective-permute-start.6 = (bf16[128,1536]{1,0:T(8,128)(2,1)S(1)}, bf16[128,1536]{1,0:T(8,128)(2,1)S(1)}, u32[]{:S(2)}, u32[]{:S(2)}) collective-permute-start(bf16[128,1536]{1,0:T(8,128)(2,1)S(1)} %shard_map.53), channel_id=1, source_target_pairs={{0,1},{1,2},{2,3},{3,4},{4,5},{5,6},{6,7},{7,8},{8,9},{9,10},{10,1... | collective-permute-start | bytes 1179656 | tf_op jit(solution)/shard_map/ppermute | solution.py:33
  41.3 1.9 %collective-permute-start.2 = (bf16[128,1536]{1,0:T(8,128)(2,1)S(1)}, bf16[128,1536]{1,0:T(8,128)(2,1)S(1)}, u32[]{:S(2)}, u32[]{:S(2)}) collective-permute-start(bf16[128,1536]{1,0:T(8,128)(2,1)S(1)} %get-tuple-element.19), channel_id=1, source_target_pairs={{0,1},{1,2},{2,3},{3,4},{4,5},{5,6},{6,7},{7,8},{8,9},{9,10},{10,1... | collective-permute-start | bytes 1179656 | tf_op jit(solution)/shard_map/ppermute | solution.py:33
  44.7 1.9 %collective-permute-start.17 = (bf16[128,1536]{1,0:T(8,128)(2,1)S(1)}, bf16[128,1536]{1,0:T(8,128)(2,1)S(1)}, u32[]{:S(2)}, u32[]{:S(2)}) collective-permute-start(bf16[128,1536]{1,0:T(8,128)(2,1)S(1)} %get-tuple-element.25), channel_id=1, source_target_pairs={{0,1},{1,2},{2,3},{3,4},{4,5},{5,6},{6,7},{7,8},{8,9},{9,10},{10,1... | collective-permute-start | bytes 1179656 | tf_op jit(solution)/shard_map/ppermute | solution.py:33
  48.0 1.9 %collective-permute-start.12 = (bf16[128,1536]{1,0:T(8,128)(2,1)S(1)}, bf16[128,1536]{1,0:T(8,128)(2,1)S(1)}, u32[]{:S(2)}, u32[]{:S(2)}) collective-permute-start(bf16[128,1536]{1,0:T(8,128)(2,1)S(1)} %get-tuple-element.23), channel_id=1, source_target_pairs={{0,1},{1,2},{2,3},{3,4},{4,5},{5,6},{6,7},{7,8},{8,9},{9,10},{10,1... | collective-permute-start | bytes 1179656 | tf_op jit(solution)/shard_map/ppermute | solution.py:33
  51.4 1.9 %collective-permute-start.7 = (bf16[128,1536]{1,0:T(8,128)(2,1)S(1)}, bf16[128,1536]{1,0:T(8,128)(2,1)S(1)}, u32[]{:S(2)}, u32[]{:S(2)}) collective-permute-start(bf16[128,1536]{1,0:T(8,128)(2,1)S(1)} %get-tuple-element.21), channel_id=1, source_target_pairs={{0,1},{1,2},{2,3},{3,4},{4,5},{5,6},{6,7},{7,8},{8,9},{9,10},{10,1... | collective-permute-start | bytes 1179656 | tf_op jit(solution)/shard_map/ppermute | solution.py:33
  60.2 2.1 %collective-permute-done.7.refs_2_.fresh_ref = bf16[128,1536]{1,0:T(8,128)(2,1)S(1)} collective-permute-done((bf16[128,1536]{1,0:T(8,128)(2,1)S(1)}, bf16[128,1536]{1,0:T(8,128)(2,1)S(1)}, u32[]{:S(2)}, u32[]{:S(2)}) %collective-permute-start.7) | collective-permute-done | bytes 393248 | tf_op jit(solution)/shard_map/ppermute | solution.py:33
  64.4 9.8 %collective-permute-done.3.refs_3_ = bf16[128,1536]{1,0:T(8,128)(2,1)S(1)} collective-permute-done((bf16[128,1536]{1,0:T(8,128)(2,1)S(1)}, bf16[128,1536]{1,0:T(8,128)(2,1)S(1)}, u32[]{:S(2)}, u32[]{:S(2)}) %collective-permute-start.3) | collective-permute-done | bytes 393248 | tf_op jit(solution)/shard_map/ppermute | solution.py:33
  74.2 1.7 %shard_map.50 = bf16[128,1536]{1,0:T(8,128)(2,1)} custom-call(bf16[128,1536]{1,0:T(8,128)(2,1)S(1)} %get-tuple-element.30.start_ref.refs_0_, bf16[128,1536]{1,0:T(8,128)(2,1)S(1)} %collective-permute-done.1.arrived_ref.refs_1_.entry_ref, bf16[128,1536]{1,0:T(8,128)(2,1)S(1)} %collective-permute-done.2.refs_2_.fresh_ref, ...), custom_call_target="tpu_custom_call" | custom-call | flops 603979776 | bytes 1572864 | tf_op jit(solution)/shard_map/pallas_call | solution.py:146
  75.9 2.0 %collective-permute-start.4 = (bf16[128,1536]{1,0:T(8,128)(2,1)}, bf16[128,1536]{1,0:T(8,128)(2,1)}, u32[]{:S(2)}, u32[]{:S(2)}) collective-permute-start(bf16[128,1536]{1,0:T(8,128)(2,1)} %shard_map.50), channel_id=1, source_target_pairs={{16,24},{17,25},{18,26},{19,27},{20,28},{21,29},{22,30},{23,31}} | collective-permute-start | bytes 1179656 | tf_op jit(solution)/shard_map/ppermute | solution.py:33
  78.0 4.7 %collective-permute-done.18.refs_3_ = bf16[128,1536]{1,0:T(8,128)(2,1)} collective-permute-done((bf16[128,1536]{1,0:T(8,128)(2,1)}, bf16[128,1536]{1,0:T(8,128)(2,1)}, u32[]{:S(2)}, u32[]{:S(2)}) %collective-permute-start.18) | collective-permute-done | bytes 393248 | tf_op jit(solution)/shard_map/ppermute | solution.py:33
  82.7 3.7 %copy-done.1 = bf16[2,1536,1536]{2,1,0:T(8,128)(2,1)S(1)} copy-done((bf16[2,1536,1536]{2,1,0:T(8,128)(2,1)S(1)}, bf16[2,1536,1536]{2,1,0:T(8,128)(2,1)}, u32[]{:S(2)}) %copy-start.1) | copy-done | bytes 9437208
  88.5 2.0 %shard_map.68 = bf16[128,1536]{1,0:T(8,128)(2,1)S(1)} custom-call(bf16[128,1536]{1,0:T(8,128)(2,1)S(1)} %get-tuple-element.28.start_ref.arrived_ref.refs_0_, bf16[128,1536]{1,0:T(8,128)(2,1)S(1)} %collective-permute-done.16.arrived_ref.refs_1_.entry_ref, bf16[128,1536]{1,0:T(8,128)(2,1)S(1)} %copy-done.5, bf16[128,1536]{1,0:T(8,128)(2,1)} %collective-permute-done.18.refs_3_, ...), custom_call_target="tpu_custom_call" | custom-call | flops 603979776 | bytes 1572864 | tf_op jit(solution)/shard_map/pallas_call | solution.py:146
  92.0 2.0 %shard_map.62 = bf16[128,1536]{1,0:T(8,128)(2,1)S(1)} custom-call(bf16[128,1536]{1,0:T(8,128)(2,1)S(1)} %get-tuple-element.29.start_ref.arrived_ref.refs_0_, bf16[128,1536]{1,0:T(8,128)(2,1)S(1)} %collective-permute-done.11.arrived_ref.refs_1_.entry_ref, bf16[128,1536]{1,0:T(8,128)(2,1)S(1)} %copy-done.10, ...), custom_call_target="tpu_custom_call" | custom-call | flops 603979776 | bytes 1572864 | tf_op jit(solution)/shard_map/pallas_call | solution.py:146
  96.8 1.9 %shard_map.56 = bf16[128,1536]{1,0:T(8,128)(2,1)S(1)} custom-call(bf16[128,1536]{1,0:T(8,128)(2,1)S(1)} %get-tuple-element.27.start_ref.arrived_ref.refs_0_, bf16[128,1536]{1,0:T(8,128)(2,1)S(1)} %collective-permute-done.6.arrived_ref.refs_1_.entry_ref, bf16[128,1536]{1,0:T(8,128)(2,1)S(1)} %copy-done.8, bf16[128,1536]{1,0:T(8,128)(2,1)} %collective-permute-done.8.refs_3_, ...), custom_call_target="tpu_custom_call" | custom-call | flops 603979776 | bytes 1572864 | tf_op jit(solution)/shard_map/pallas_call | solution.py:146
  101.9 7.2 %collective-permute-done.14 = bf16[128,1536]{1,0:T(8,128)(2,1)S(1)} collective-permute-done((bf16[128,1536]{1,0:T(8,128)(2,1)S(1)}, bf16[128,1536]{1,0:T(8,128)(2,1)S(1)}, u32[]{:S(2)}, u32[]{:S(2)}) %collective-permute-start.14) | collective-permute-done | bytes 393248 | tf_op jit(solution)/shard_map/ppermute | solution.py:33
  117.3 1.8 %pad_maximum_fusion = bf16[2,512,1536]{2,1,0:T(8,128)(2,1)} fusion(bf16[2,128,1536]{2,1,0:T(8,128)(2,1)S(1)} %shard_map.69, bf16[2,128,1536]{2,1,0:T(8,128)(2,1)S(1)} %shard_map.63, bf16[2,128,1536]{2,1,0:T(8,128)(2,1)S(1)} %shard_map.57, bf16[2,128,1536]{2,1,0:T(8,128)(2,1)S(1)} %shard_map.51), kind=kLoop, calls=%fused_computation | loop fusion | flops 12582912 | bytes 6291456 | tf_op jit(solution)/shard_map/concatenate | solution.py:206
  (95 shorter events, 45.0 us)
Async XLA Ops:
  7.6 66.6 %copy-start = (bf16[2,1536,1536]{2,1,0:T(8,128)(2,1)}, bf16[2,1536,1536]{2,1,0:T(8,128)(2,1)S(1)}, u32[]{:S(2)}) copy-start(bf16[2,1536,1536]{2,1,0:T(8,128)(2,1)S(1)} %get-tuple-element.17.w_ref.refs_4_.refs_5_) | copy-start | bytes 28311556
  7.6 15.4 %collective-permute-start = (bf16[128,1536]{1,0:T(8,128)(2,1)S(1)}, bf16[128,1536]{1,0:T(8,128)(2,1)S(1)}, u32[]{:S(2)}, u32[]{:S(2)}) collective-permute-start(bf16[128,1536]{1,0:T(8,128)(2,1)S(1)} %get-tuple-element.16), channel_id=1, source_target_pairs={{0,1},{1,2},{2,3},{3,4},{4,5},{5,6},{6,7},{7,8},{8,9},{9,10},{10,1... | collective-permute-start | bytes 1179656 | tf_op jit(solution)/shard_map/ppermute | solution.py:33
  12.7 15.2 %collective-permute-start.15 = (bf16[128,1536]{1,0:T(8,128)(2,1)S(1)}, bf16[128,1536]{1,0:T(8,128)(2,1)S(1)}, u32[]{:S(2)}, u32[]{:S(2)}) collective-permute-start(bf16[128,1536]{1,0:T(8,128)(2,1)S(1)} %shard_map.64), channel_id=1, source_target_pairs={{0,1},{1,2},{2,3},{3,4},{4,5},{5,6},{6,7},{7,8},{8,9},{9,10},{10,1... | collective-permute-start | bytes 1179656 | tf_op jit(solution)/shard_map/ppermute | solution.py:33
  16.1 15.2 %collective-permute-start.10 = (bf16[128,1536]{1,0:T(8,128)(2,1)S(1)}, bf16[128,1536]{1,0:T(8,128)(2,1)S(1)}, u32[]{:S(2)}, u32[]{:S(2)}) collective-permute-start(bf16[128,1536]{1,0:T(8,128)(2,1)S(1)} %shard_map.58), channel_id=1, source_target_pairs={{0,1},{1,2},{2,3},{3,4},{4,5},{5,6},{6,7},{7,8},{8,9},{9,10},{10,1... | collective-permute-start | bytes 1179656 | tf_op jit(solution)/shard_map/ppermute | solution.py:33
  21.0 15.2 %collective-permute-start.5 = (bf16[128,1536]{1,0:T(8,128)(2,1)S(1)}, bf16[128,1536]{1,0:T(8,128)(2,1)S(1)}, u32[]{:S(2)}, u32[]{:S(2)}) collective-permute-start(bf16[128,1536]{1,0:T(8,128)(2,1)S(1)} %shard_map.52), channel_id=1, source_target_pairs={{0,1},{1,2},{2,3},{3,4},{4,5},{5,6},{6,7},{7,8},{8,9},{9,10},{10,1... | collective-permute-start | bytes 1179656 | tf_op jit(solution)/shard_map/ppermute | solution.py:33
  24.4 15.4 %collective-permute-start.1 = (bf16[128,1536]{1,0:T(8,128)(2,1)S(1)}, bf16[128,1536]{1,0:T(8,128)(2,1)S(1)}, u32[]{:S(2)}, u32[]{:S(2)}) collective-permute-start(bf16[128,1536]{1,0:T(8,128)(2,1)S(1)} %shard_map.47), channel_id=1, source_target_pairs={{0,1},{1,2},{2,3},{3,4},{4,5},{5,6},{6,7},{7,8},{8,9},{9,10},{10,1... | collective-permute-start | bytes 1179656 | tf_op jit(solution)/shard_map/ppermute | solution.py:33
  29.4 13.8 %collective-permute-start.16 = (bf16[128,1536]{1,0:T(8,128)(2,1)S(1)}, bf16[128,1536]{1,0:T(8,128)(2,1)S(1)}, u32[]{:S(2)}, u32[]{:S(2)}) collective-permute-start(bf16[128,1536]{1,0:T(8,128)(2,1)S(1)} %shard_map.65), channel_id=1, source_target_pairs={{0,1},{1,2},{2,3},{3,4},{4,5},{5,6},{6,7},{7,8},{8,9},{9,10},{10,1... | collective-permute-start | bytes 1179656 | tf_op jit(solution)/shard_map/ppermute | solution.py:33
  32.8 13.8 %collective-permute-start.11 = (bf16[128,1536]{1,0:T(8,128)(2,1)S(1)}, bf16[128,1536]{1,0:T(8,128)(2,1)S(1)}, u32[]{:S(2)}, u32[]{:S(2)}) collective-permute-start(bf16[128,1536]{1,0:T(8,128)(2,1)S(1)} %shard_map.59), channel_id=1, source_target_pairs={{0,1},{1,2},{2,3},{3,4},{4,5},{5,6},{6,7},{7,8},{8,9},{9,10},{10,1... | collective-permute-start | bytes 1179656 | tf_op jit(solution)/shard_map/ppermute | solution.py:33
  37.7 12.3 %collective-permute-start.6 = (bf16[128,1536]{1,0:T(8,128)(2,1)S(1)}, bf16[128,1536]{1,0:T(8,128)(2,1)S(1)}, u32[]{:S(2)}, u32[]{:S(2)}) collective-permute-start(bf16[128,1536]{1,0:T(8,128)(2,1)S(1)} %shard_map.53), channel_id=1, source_target_pairs={{0,1},{1,2},{2,3},{3,4},{4,5},{5,6},{6,7},{7,8},{8,9},{9,10},{10,1... | collective-permute-start | bytes 1179656 | tf_op jit(solution)/shard_map/ppermute | solution.py:33
  41.3 12.1 %collective-permute-start.2 = (bf16[128,1536]{1,0:T(8,128)(2,1)S(1)}, bf16[128,1536]{1,0:T(8,128)(2,1)S(1)}, u32[]{:S(2)}, u32[]{:S(2)}) collective-permute-start(bf16[128,1536]{1,0:T(8,128)(2,1)S(1)} %get-tuple-element.19), channel_id=1, source_target_pairs={{0,1},{1,2},{2,3},{3,4},{4,5},{5,6},{6,7},{7,8},{8,9},{9,10},{10,1... | collective-permute-start | bytes 1179656 | tf_op jit(solution)/shard_map/ppermute | solution.py:33
  44.7 10.1 %collective-permute-start.17 = (bf16[128,1536]{1,0:T(8,128)(2,1)S(1)}, bf16[128,1536]{1,0:T(8,128)(2,1)S(1)}, u32[]{:S(2)}, u32[]{:S(2)}) collective-permute-start(bf16[128,1536]{1,0:T(8,128)(2,1)S(1)} %get-tuple-element.25), channel_id=1, source_target_pairs={{0,1},{1,2},{2,3},{3,4},{4,5},{5,6},{6,7},{7,8},{8,9},{9,10},{10,1... | collective-permute-start | bytes 1179656 | tf_op jit(solution)/shard_map/ppermute | solution.py:33
  48.0 10.1 %collective-permute-start.12 = (bf16[128,1536]{1,0:T(8,128)(2,1)S(1)}, bf16[128,1536]{1,0:T(8,128)(2,1)S(1)}, u32[]{:S(2)}, u32[]{:S(2)}) collective-permute-start(bf16[128,1536]{1,0:T(8,128)(2,1)S(1)} %get-tuple-element.23), channel_id=1, source_target_pairs={{0,1},{1,2},{2,3},{3,4},{4,5},{5,6},{6,7},{7,8},{8,9},{9,10},{10,1... | collective-permute-start | bytes 1179656 | tf_op jit(solution)/shard_map/ppermute | solution.py:33
  51.4 10.9 %collective-permute-start.7 = (bf16[128,1536]{1,0:T(8,128)(2,1)S(1)}, bf16[128,1536]{1,0:T(8,128)(2,1)S(1)}, u32[]{:S(2)}, u32[]{:S(2)}) collective-permute-start(bf16[128,1536]{1,0:T(8,128)(2,1)S(1)} %get-tuple-element.21), channel_id=1, source_target_pairs={{0,1},{1,2},{2,3},{3,4},{4,5},{5,6},{6,7},{7,8},{8,9},{9,10},{10,1... | collective-permute-start | bytes 1179656 | tf_op jit(solution)/shard_map/ppermute | solution.py:33
  53.4 20.9 %copy-start.2 = (bf16[128,1536]{1,0:T(8,128)(2,1)}, bf16[128,1536]{1,0:T(8,128)(2,1)S(1)}, u32[]{:S(2)}) copy-start(bf16[128,1536]{1,0:T(8,128)(2,1)S(1)} %collective-permute-done.2.refs_2_.fresh_ref) | copy-start | bytes 1179652
  53.4 20.8 %collective-permute-start.3 = (bf16[128,1536]{1,0:T(8,128)(2,1)S(1)}, bf16[128,1536]{1,0:T(8,128)(2,1)S(1)}, u32[]{:S(2)}, u32[]{:S(2)}) collective-permute-start(bf16[128,1536]{1,0:T(8,128)(2,1)S(1)} %shard_map.49), channel_id=1, source_target_pairs={{8,16},{9,17},{10,18},{11,19},{12,20},{13,21},{14,22},{15,23}} | collective-permute-start | bytes 1179656 | tf_op jit(solution)/shard_map/ppermute | solution.py:33
  55.6 27.1 %collective-permute-start.18 = (bf16[128,1536]{1,0:T(8,128)(2,1)}, bf16[128,1536]{1,0:T(8,128)(2,1)}, u32[]{:S(2)}, u32[]{:S(2)}) collective-permute-start(bf16[128,1536]{1,0:T(8,128)(2,1)} %shard_map.67), channel_id=1, source_target_pairs={{8,16},{9,17},{10,18},{11,19},{12,20},{13,21},{14,22},{15,23}} | collective-permute-start | bytes 1179656 | tf_op jit(solution)/shard_map/ppermute | solution.py:33
  58.9 33.0 %collective-permute-start.13 = (bf16[128,1536]{1,0:T(8,128)(2,1)}, bf16[128,1536]{1,0:T(8,128)(2,1)}, u32[]{:S(2)}, u32[]{:S(2)}) collective-permute-start(bf16[128,1536]{1,0:T(8,128)(2,1)} %shard_map.61), channel_id=1, source_target_pairs={{8,16},{9,17},{10,18},{11,19},{12,20},{13,21},{14,22},{15,23}} | collective-permute-start | bytes 1179656 | tf_op jit(solution)/shard_map/ppermute | solution.py:33
  63.1 33.6 %collective-permute-start.8 = (bf16[128,1536]{1,0:T(8,128)(2,1)}, bf16[128,1536]{1,0:T(8,128)(2,1)}, u32[]{:S(2)}, u32[]{:S(2)}) collective-permute-start(bf16[128,1536]{1,0:T(8,128)(2,1)} %shard_map.55), channel_id=1, source_target_pairs={{8,16},{9,17},{10,18},{11,19},{12,20},{13,21},{14,22},{15,23}} | collective-permute-start | bytes 1179656 | tf_op jit(solution)/shard_map/ppermute | solution.py:33
  75.9 24.1 %collective-permute-start.4 = (bf16[128,1536]{1,0:T(8,128)(2,1)}, bf16[128,1536]{1,0:T(8,128)(2,1)}, u32[]{:S(2)}, u32[]{:S(2)}) collective-permute-start(bf16[128,1536]{1,0:T(8,128)(2,1)} %shard_map.50), channel_id=1, source_target_pairs={{16,24},{17,25},{18,26},{19,27},{20,28},{21,29},{22,30},{23,31}} | collective-permute-start | bytes 1179656 | tf_op jit(solution)/shard_map/ppermute | solution.py:33
  90.5 10.4 %collective-permute-start.19 = (bf16[128,1536]{1,0:T(8,128)(2,1)S(1)}, bf16[128,1536]{1,0:T(8,128)(2,1)S(1)}, u32[]{:S(2)}, u32[]{:S(2)}) collective-permute-start(bf16[128,1536]{1,0:T(8,128)(2,1)S(1)} %shard_map.68), channel_id=1, source_target_pairs={{16,24},{17,25},{18,26},{19,27},{20,28},{21,29},{22,30},{23,31}} | collective-permute-start | bytes 1179656 | tf_op jit(solution)/shard_map/ppermute | solution.py:33
  92.0 18.2 %slice-start = ((s8[9437184]{0:T(1024)(128)(4,1)}), s8[4194304]{0:T(1024)(128)(4,1)S(1)}, s32[]{:S(2)}) async-start(s8[9437184]{0:T(1024)(128)(4,1)} %bitcast.2), calls=%async_computation | async-start | bytes 8388608
  92.0 18.2 %slice-start.1 = ((s8[9437184]{0:T(1024)(128)(4,1)}), s8[4194304]{0:T(1024)(128)(4,1)S(1)}, s32[]{:S(2)}) async-start(s8[9437184]{0:T(1024)(128)(4,1)} %bitcast.2), calls=%async_computation.1 | async-start | bytes 8388608
  94.0 15.1 %collective-permute-start.14 = (bf16[128,1536]{1,0:T(8,128)(2,1)S(1)}, bf16[128,1536]{1,0:T(8,128)(2,1)S(1)}, u32[]{:S(2)}, u32[]{:S(2)}) collective-permute-start(bf16[128,1536]{1,0:T(8,128)(2,1)S(1)} %shard_map.62), channel_id=1, source_target_pairs={{16,24},{17,25},{18,26},{19,27},{20,28},{21,29},{22,30},{23,31}} | collective-permute-start | bytes 1179656 | tf_op jit(solution)/shard_map/ppermute | solution.py:33
  98.7 16.1 %collective-permute-start.9 = (bf16[128,1536]{1,0:T(8,128)(2,1)S(1)}, bf16[128,1536]{1,0:T(8,128)(2,1)S(1)}, u32[]{:S(2)}, u32[]{:S(2)}) collective-permute-start(bf16[128,1536]{1,0:T(8,128)(2,1)S(1)} %shard_map.56), channel_id=1, source_target_pairs={{16,24},{17,25},{18,26},{19,27},{20,28},{21,29},{22,30},{23,31}} | collective-permute-start | bytes 1179656 | tf_op jit(solution)/shard_map/ppermute | solution.py:33
  (20 other events, 132.5 us)

commit v2 on v0

v2 whole, which is shorter than its diff:
```python
import functools

import jax
import jax.numpy as jnp
from jax import lax
from jax.experimental import pallas as pl
from jax.experimental.pallas import tpu as pltpu
from jax.sharding import PartitionSpec as P

LAY_DEV = 2
INTERVAL = 8

SHARES = (4, 4, 4, 4)
PASSES = (0, 1, 0, 2, 1, 0, 3, 1, 2, 3, 2, 3)
FIRST_LAG = 2.5
NEXT_LAG = 3.2
TILE = 512
VMEM_BYTES = 20 << 20
VMEM = pl.BlockSpec(memory_space=pltpu.VMEM)
ANY = pl.BlockSpec(memory_space=pl.ANY)
DMA = pltpu.SemaphoreType.DMA


def held(value):
    return pltpu.with_memory_space_constraint(value, pltpu.VMEM)


def kept(shape, kind):
    return pltpu.VMEM(shape, kind)


def in_hbm(value):
    return pltpu.with_memory_space_constraint(value, pltpu.HBM)


def passed_along(value, pairs):
    return lax.ppermute(value, "depth", pairs)


def tiles(width):
    tile = TILE if width % TILE == 0 else width
    return [slice(low, low + tile) for low in range(0, width, tile)]


def bend(state, w_ref, p_ref, layer, cols):
    pre = jnp.dot(state, w_ref[layer, :, cols], preferred_element_type=jnp.float32)
    return jnp.tanh(pre + p_ref[layer : layer + 1, cols])


def opening_kernel(rows, start_hbm, w_hbm, b_hbm, h_hbm, out_ref, start_ref, w_ref, p_ref, state, rounded, b_ref, h_ref, w_sems, sems):
    width = w_hbm.shape[2]
    small = [
        pltpu.make_async_copy(start_hbm, start_ref, sems.at[0]),
        pltpu.make_async_copy(b_hbm, b_ref, sems.at[1]),
        pltpu.make_async_copy(h_hbm, h_ref, sems.at[2]),
    ]
    for copy in small:
        copy.start()
    copies = []
    for layer in range(LAY_DEV):
        for cols in tiles(width):
            copy = pltpu.make_async_copy(
                w_hbm.at[layer, :, cols], w_ref.at[layer, :, cols], w_sems.at[len(copies)]
            )
            copy.start()
            copies.append(copy)
    for copy in small:
        copy.wait()
    p_ref[0:2, :] = b_ref[...]
    for layer in range(LAY_DEV):
        p_ref[2 + layer : 3 + layer, :] = jnp.full((1, width), h_ref[layer], jnp.float32)
    p_ref[4:8, :] = jnp.zeros((4, width), jnp.float32)
    start = start_ref[rows, :]
    for index, cols in enumerate(tiles(width)):
        copies[index].wait()
        moved = start[:, cols].astype(jnp.float32) + p_ref[2:3, cols] * bend(start, w_ref, p_ref, 0, cols)
        state[:, cols] = moved
        rounded[:, cols] = moved.astype(jnp.bfloat16)
    for index, cols in enumerate(tiles(width)):
        copies[len(tiles(width)) + index].wait()
        bent = bend(rounded[...], w_ref, p_ref, 1, cols)
        out_ref[:, cols] = (state[:, cols] + p_ref[3:4, cols] * bent).astype(jnp.bfloat16)


def pass_kernel(rows, opening, keep, after_ref, start_ref, w_ref, p_ref, *rest):
    if opening:
        out_ref, state, rounded = rest
        entering = start_ref.at[rows, :]
    else:
        arrived_ref, *rest = rest
        if keep:
            out_ref, t_ref, entering, state, rounded = rest
        else:
            out_ref, entering, state, rounded = rest
        entering[...] = jnp.where(lax.axis_index("depth") == 0, start_ref[rows, :], arrived_ref[...])
    for cols in tiles(w_ref.shape[2]):
        bent = bend(entering[...], w_ref, p_ref, 0, cols)
        if keep:
            t_ref[:, cols] = bent
        moved = entering[:, cols].astype(jnp.float32) + p_ref[2:3, cols] * bent
        state[:, cols] = moved
        rounded[:, cols] = moved.astype(jnp.bfloat16)
    for cols in tiles(w_ref.shape[2]):
        bent = bend(rounded[...], w_ref, p_ref, 1, cols)
        out_ref[:, cols] = (state[:, cols] + p_ref[3:4, cols] * bent).astype(jnp.bfloat16)


def correction_of(entry_ref, fresh_ref, moved_ref):
    total = fresh_ref[...].astype(jnp.float32) - entry_ref[...].astype(jnp.float32)
    if moved_ref is not None:
        total = moved_ref[...].astype(jnp.float32) + total
    return total.astype(jnp.bfloat16)


def coarse_kernel(group, after_ref, entry_ref, fresh_ref, t_ref, w_ref, p_ref, *rest):
    moved_ref = None
    if group > 1:
        moved_ref, before_ref, *rest = rest
    out_ref, correction_ref, rounded = rest

    here = lax.axis_index("depth") // INTERVAL == group
    if group > 1:

        @pl.when(jnp.logical_not(here))
        def _():
            correction_ref[...] = before_ref[...]

    @pl.when(here)
    def _():
        correction = correction_of(entry_ref, fresh_ref, moved_ref)
        correction_ref[...] = correction
        rounded[...] = (entry_ref[...].astype(jnp.float32) + correction.astype(jnp.float32)).astype(jnp.bfloat16)
        for cols in tiles(w_ref.shape[2]):
            bent = bend(rounded[...], w_ref, p_ref, 0, cols)
            change = (INTERVAL * LAY_DEV) * p_ref[2:3, cols] * (bent - t_ref[:, cols])
            out_ref[:, cols] = (correction_ref[:, cols].astype(jnp.float32) + change).astype(jnp.bfloat16)


def final_kernel(rows, groups, aliased, after_ref, start_ref, w_ref, p_ref, entry_ref, fresh_ref, moved_ref, correction_ref, *rest):
    if aliased:
        _, *rest = rest
    states, state, first, second, sems = rest
    device = lax.axis_index("depth")
    group = device // INTERVAL
    width = w_ref.shape[2]

    @pl.when(group == 0)
    def _():
        entry = jnp.where(device == 0, start_ref[rows, :], entry_ref[...])
        state[...] = entry.astype(jnp.float32)

    @pl.when((group > 0) & (group < groups - 1))
    def _():
        state[...] = entry_ref[...].astype(jnp.float32) + correction_ref[...].astype(jnp.float32)

    @pl.when((group > 0) & (group == groups - 1))
    def _():
        correction = correction_of(entry_ref, fresh_ref, moved_ref)
        state[...] = entry_ref[...].astype(jnp.float32) + correction.astype(jnp.float32)

    second[...] = state[...].astype(jnp.bfloat16)
    copies = []
    for cols in tiles(width):
        moved = state[:, cols] + p_ref[2:3, cols] * bend(second[...], w_ref, p_ref, 0, cols)
        state[:, cols] = moved
        first[:, cols] = moved.astype(jnp.bfloat16)
        copy = pltpu.make_async_copy(first.at[:, cols], states.at[0, rows, cols], sems.at[len(copies)])
        copy.start()
        copies.append(copy)
    for cols in tiles(width):
        bent = bend(first[...], w_ref, p_ref, 1, cols)
        second[:, cols] = (state[:, cols] + p_ref[3:4, cols] * bent).astype(jnp.bfloat16)
        copy = pltpu.make_async_copy(second.at[:, cols], states.at[1, rows, cols], sems.at[len(copies)])
        copy.start()
        copies.append(copy)
    for copy in copies:
        copy.wait()


def order_of(groups):
    chunks = len(SHARES)
    times, done = [], [0] * chunks
    for place, chunk in enumerate(PASSES):
        done[chunk] += 1
        times.append((place, 0, "pass", chunk, done[chunk] - 1))
        if done[chunk] == 3:
            due = place + FIRST_LAG
            for group in range(1, groups - 1):
                times.append((due, 1, "coarse", chunk, group))
                due += NEXT_LAG
            times.append((due, 2, "final", chunk, 0))
    return [item[2:] for item in sorted(times)]


def local(initial, weights, biases, step_sizes):
    count = lax.axis_size("depth")
    groups = count // INTERVAL
    width = initial.shape[2]
    start_hbm = initial.reshape(-1, width)
    total = start_hbm.shape[0]
    bounds = [0]
    for share in SHARES:
        bounds.append(bounds[-1] + share * total // sum(SHARES))
    spans = [slice(low, high) for low, high in zip(bounds, bounds[1:])]
    sizes = [span.stop - span.start for span in spans]
    parts = len(tiles(width))
    one_on = [(source, source + 1) for source in range(count - 1)]

    def narrow(size):
        return kept((size, width), jnp.bfloat16)

    def call(body, size, layers, outs, out_specs, scratch, operands, specs, aliases=None):
        return pl.pallas_call(
            body,
            out_shape=outs,
            in_specs=specs,
            out_specs=out_specs,
            scratch_shapes=scratch,
            input_output_aliases=aliases or {},
            compiler_params=pltpu.CompilerParams(vmem_limit_bytes=VMEM_BYTES),
            cost_estimate=pl.CostEstimate(
                flops=2 * size * width * width * layers,
                bytes_accessed=size * width * 8,
                transcendentals=size * width * layers,
            ),
        )(*[held(value) if spec is VMEM else in_hbm(value) for value, spec in zip(operands, specs)])

    first = sizes[0]
    leaving, start, w, p = call(
        functools.partial(opening_kernel, spans[0]), first, LAY_DEV,
        (narrow(first), narrow(total), kept(weights.shape, jnp.bfloat16), kept((8, width), jnp.float32)),
        (VMEM,) * 4,
        [
            pltpu.VMEM((first, width), jnp.float32), pltpu.VMEM((first, width), jnp.bfloat16),
            pltpu.VMEM(biases.shape, jnp.float32), pltpu.SMEM(step_sizes.shape, jnp.float32),
            DMA((LAY_DEV * parts,)), DMA((3,)),
        ],
        [start_hbm, weights, biases, step_sizes], [ANY] * 4,
    )
    chunks = len(SHARES)
    bent, correction, moved = [None] * chunks, [None] * chunks, [None] * chunks
    arrived = [[] for _ in range(chunks)]
    arrived[0].append(passed_along(leaving, one_on))
    after, after_spec, states = leaving, VMEM, None
    for kind, chunk, step in order_of(groups)[1:]:
        size = sizes[chunk]
        wide = pltpu.VMEM((size, width), jnp.float32)
        thin = pltpu.VMEM((size, width), jnp.bfloat16)
        if kind == "pass":
            keep = step == 2
            operands = [after, start, w, p] + ([arrived[chunk][-1]] if step else [])
            result = call(
                functools.partial(pass_kernel, spans[chunk], step == 0, keep), size, LAY_DEV,
                (narrow(size), kept((size, width), jnp.float32)) if keep else narrow(size),
                (VMEM, VMEM) if keep else VMEM,
                [thin, wide, thin] if step else [wide, thin],
                operands, [after_spec] + [VMEM] * (len(operands) - 1),
            )
            if keep:
                leaving, bent[chunk] = result
            else:
                leaving = result
            arrived[chunk].append(passed_along(leaving, one_on))
            after, after_spec = leaving, VMEM
        elif kind == "coarse":
            _, entry, fresh = arrived[chunk]
            operands = [after, entry, fresh, bent[chunk], w, p]
            if step > 1:
                operands += [moved[chunk], correction[chunk]]
            delta, correction[chunk] = call(
                functools.partial(coarse_kernel, step), size, 1,
                (narrow(size), narrow(size)), (VMEM, VMEM), [thin],
                operands, [after_spec] + [VMEM] * (len(operands) - 1),
            )
            ahead = [(source, source + INTERVAL) for source in range(step * INTERVAL, (step + 1) * INTERVAL)]
            moved[chunk] = passed_along(delta, ahead)
            after, after_spec = delta, VMEM
        else:
            _, entry, fresh = arrived[chunk]
            operands = [after, start, w, p, entry, fresh, moved[chunk], correction[chunk]]
            specs = [after_spec] + [VMEM] * (len(operands) - 1)
            aliases = None
            if states is not None:
                aliases = {len(operands): 0}
                operands.append(states)
                specs.append(ANY)
                if after_spec is ANY:
                    operands[0], specs[0] = start, VMEM
            states = call(
                functools.partial(final_kernel, spans[chunk], groups, states is not None), size, LAY_DEV,
                jax.ShapeDtypeStruct((LAY_DEV, total, width), jnp.bfloat16), ANY,
                [wide, thin, thin, DMA((LAY_DEV * parts,))], operands, specs, aliases,
            )
            after, after_spec = states, ANY
    return states.reshape(LAY_DEV, initial.shape[0], -1, width)


def solution(mesh):
    placed = (P(), P("depth", None, None), P("depth", None), P("depth"))
    return jax.shard_map(
        local, mesh=mesh, in_specs=placed, out_specs=P("depth", None, None, None), check_vma=False
    )
```

time: 294 us -> 117 us (0.40)
  the two profiles are of different devices: /device:TPU:22 before, /device:TPU:23 now
where the time goes in v2:
time: 117 us; the launch traced here: 116 us
  starting transfers between devices  51.2 us (44%)
  Pallas kernels  34.1 us (29%)
  waiting for transfers between devices  30.1 us (26%)
    ppermute x20, starting transfers between devices, passed_along(): return lax.ppermute(value, 'depth', pairs)  51.2 us
    pallas_call x24, Pallas kernels, call(): pl.pallas_call(body, out_shape=outs, in_specs=specs, out_specs=out_specs,...  34.1 us
    ppermute x20, waiting for transfers between devices, passed_along(): return lax.ppermute(value, 'depth', pairs)  30.1 us
  transfers between devices with their start and end apart: 20, of which 7 were waited for; matrix products, arithmetic and copies ran while one was open for 0% of the time, Pallas kernels for 23%

profile of v2, /device:TPU:23, one launch (start us, length us, event | category | flops | bytes accessed | tf_op | source)
XLA Modules:
  0.0 115.9 jit_solution(3989508714117574900)
XLA Ops:
  0.0 5.7 %shard_map.46 = (bf16[128,1536]{1,0:T(8,128)(2,1)S(1)}, bf16[512,1536]{1,0:T(8,128)(2,1)S(1)}, bf16[2,1536,1536]{2,1,0:T(8,128)(2,1)S(1)}, f32[8,1536]{1,0:T(8,128)S(1)}) custom-call(bf16[512,1536]{1,0:T(8,128)(2,1)} %bitcast.2, bf16[2,1536,1536]{2,1,0:T(8,128)(2,1)} %w_hbm.1, f32[2,1536]{1,0:T(2,128)} %b_hbm.1, f32[2]{0:T(128)} %h_hbm.1), custom_call_target="tpu_custom_call" | custom-call | flops 1207959552 | bytes 1572864 | tf_op jit(solution)/shard_map/pallas_call | solution.py:213
  5.7 3.7 %collective-permute-start = (bf16[128,1536]{1,0:T(8,128)(2,1)S(1)}, bf16[128,1536]{1,0:T(8,128)(2,1)S(1)}, u32[]{:S(2)}, u32[]{:S(2)}) collective-permute-start(bf16[128,1536]{1,0:T(8,128)(2,1)S(1)} %get-tuple-element.36.after_ref), channel_id=1, source_target_pairs={{0,1},{1,2},{2,3},{3,4},{4,5},{5,6},{6,7},{7,8},{8,9},{9,10},{10,1... | collective-permute-start | bytes 1179656 | tf_op jit(solution)/shard_map/ppermute | solution.py:37
  10.8 1.9 %collective-permute-start.1 = (bf16[128,1536]{1,0:T(8,128)(2,1)S(1)}, bf16[128,1536]{1,0:T(8,128)(2,1)S(1)}, u32[]{:S(2)}, u32[]{:S(2)}) collective-permute-start(bf16[128,1536]{1,0:T(8,128)(2,1)S(1)} %shard_map.47.after_ref), channel_id=1, source_target_pairs={{0,1},{1,2},{2,3},{3,4},{4,5},{5,6},{6,7},{7,8},{8,9},{9,10},{10,1... | collective-permute-start | bytes 1179656 | tf_op jit(solution)/shard_map/ppermute | solution.py:37
  15.5 6.2 %collective-permute-start.2 = (bf16[128,1536]{1,0:T(8,128)(2,1)S(1)}, bf16[128,1536]{1,0:T(8,128)(2,1)S(1)}, u32[]{:S(2)}, u32[]{:S(2)}) collective-permute-start(bf16[128,1536]{1,0:T(8,128)(2,1)S(1)} %shard_map.48.after_ref), channel_id=1, source_target_pairs={{0,1},{1,2},{2,3},{3,4},{4,5},{5,6},{6,7},{7,8},{8,9},{9,10},{10,1... | collective-permute-start | bytes 1179656 | tf_op jit(solution)/shard_map/ppermute | solution.py:37
  24.6 1.9 %collective-permute-start.3 = (bf16[128,1536]{1,0:T(8,128)(2,1)S(1)}, bf16[128,1536]{1,0:T(8,128)(2,1)S(1)}, u32[]{:S(2)}, u32[]{:S(2)}) collective-permute-start(bf16[128,1536]{1,0:T(8,128)(2,1)S(1)} %shard_map.50.after_ref), channel_id=1, source_target_pairs={{0,1},{1,2},{2,3},{3,4},{4,5},{5,6},{6,7},{7,8},{8,9},{9,10},{10,1... | collective-permute-start | bytes 1179656 | tf_op jit(solution)/shard_map/ppermute | solution.py:37
  26.5 1.4 %shard_map.51 = (bf16[128,1536]{1,0:T(8,128)(2,1)S(1)}, f32[128,1536]{1,0:T(8,128)S(1)}) custom-call(bf16[128,1536]{1,0:T(8,128)(2,1)S(1)} %shard_map.50.after_ref, bf16[512,1536]{1,0:T(8,128)(2,1)S(1)} %get-tuple-element.33.start_ref.after_ref, bf16[2,1536,1536]{2,1,0:T(8,128)(2,1)S(1)} %get-tuple-element.34.w_ref, f32[8,1536]{1,0:T(8,128)S(1)} %get-tuple-element.35.p_ref, ...), custom_call_target="tpu_custom_call" | custom-call | flops 1207959552 | bytes 1572864 | tf_op jit(solution)/shard_map/pallas_call | solution.py:213
  28.0 6.1 %collective-permute-start.4 = (bf16[128,1536]{1,0:T(8,128)(2,1)S(1)}, bf16[128,1536]{1,0:T(8,128)(2,1)S(1)}, u32[]{:S(2)}, u32[]{:S(2)}) collective-permute-start(bf16[128,1536]{1,0:T(8,128)(2,1)S(1)} %get-tuple-element.37.after_ref), channel_id=1, source_target_pairs={{0,1},{1,2},{2,3},{3,4},{4,5},{5,6},{6,7},{7,8},{8,9},{9,10},{10,1... | collective-permute-start | bytes 1179656 | tf_op jit(solution)/shard_map/ppermute | solution.py:37
  34.0 1.9 %collective-permute-start.5 = (bf16[128,1536]{1,0:T(8,128)(2,1)S(1)}, bf16[128,1536]{1,0:T(8,128)(2,1)S(1)}, u32[]{:S(2)}, u32[]{:S(2)}) collective-permute-start(bf16[128,1536]{1,0:T(8,128)(2,1)S(1)} %shard_map.49.after_ref), channel_id=1, source_target_pairs={{0,1},{1,2},{2,3},{3,4},{4,5},{5,6},{6,7},{7,8},{8,9},{9,10},{10,1... | collective-permute-start | bytes 1179656 | tf_op jit(solution)/shard_map/ppermute | solution.py:37
  37.4 1.9 %collective-permute-start.6 = (bf16[128,1536]{1,0:T(8,128)(2,1)S(1)}, bf16[128,1536]{1,0:T(8,128)(2,1)S(1)}, u32[]{:S(2)}, u32[]{:S(2)}) collective-permute-start(bf16[128,1536]{1,0:T(8,128)(2,1)S(1)} %shard_map.52.after_ref), channel_id=1, source_target_pairs={{0,1},{1,2},{2,3},{3,4},{4,5},{5,6},{6,7},{7,8},{8,9},{9,10},{10,1... | collective-permute-start | bytes 1179656 | tf_op jit(solution)/shard_map/ppermute | solution.py:37
  40.8 1.9 %collective-permute-start.8 = (bf16[128,1536]{1,0:T(8,128)(2,1)S(1)}, bf16[128,1536]{1,0:T(8,128)(2,1)S(1)}, u32[]{:S(2)}, u32[]{:S(2)}) collective-permute-start(bf16[128,1536]{1,0:T(8,128)(2,1)S(1)} %get-tuple-element.38.after_ref), channel_id=1, source_target_pairs={{0,1},{1,2},{2,3},{3,4},{4,5},{5,6},{6,7},{7,8},{8,9},{9,10},{10,1... | collective-permute-start | bytes 1179656 | tf_op jit(solution)/shard_map/ppermute | solution.py:37
  44.4 6.2 %collective-permute-start.9 = (bf16[128,1536]{1,0:T(8,128)(2,1)S(1)}, bf16[128,1536]{1,0:T(8,128)(2,1)S(1)}, u32[]{:S(2)}, u32[]{:S(2)}) collective-permute-start(bf16[128,1536]{1,0:T(8,128)(2,1)S(1)} %shard_map.55.after_ref), channel_id=1, source_target_pairs={{0,1},{1,2},{2,3},{3,4},{4,5},{5,6},{6,7},{7,8},{8,9},{9,10},{10,1... | collective-permute-start | bytes 1179656 | tf_op jit(solution)/shard_map/ppermute | solution.py:37
  53.3 1.9 %collective-permute-start.7 = (bf16[128,1536]{1,0:T(8,128)(2,1)S(1)}, bf16[128,1536]{1,0:T(8,128)(2,1)S(1)}, u32[]{:S(2)}, u32[]{:S(2)}) collective-permute-start(bf16[128,1536]{1,0:T(8,128)(2,1)S(1)} %shard_map.56.after_ref), channel_id=1, source_target_pairs={{0,1},{1,2},{2,3},{3,4},{4,5},{5,6},{6,7},{7,8},{8,9},{9,10},{10,1... | collective-permute-start | bytes 1179656 | tf_op jit(solution)/shard_map/ppermute | solution.py:37
  58.0 5.2 %collective-permute-start.12 = (bf16[128,1536]{1,0:T(8,128)(2,1)S(1)}, bf16[128,1536]{1,0:T(8,128)(2,1)S(1)}, u32[]{:S(2)}, u32[]{:S(2)}) collective-permute-start(bf16[128,1536]{1,0:T(8,128)(2,1)S(1)} %get-tuple-element.43.after_ref), channel_id=1, source_target_pairs={{0,1},{1,2},{2,3},{3,4},{4,5},{5,6},{6,7},{7,8},{8,9},{9,10},{10,1... | collective-permute-start | bytes 1179656 | tf_op jit(solution)/shard_map/ppermute | solution.py:37
  63.2 5.1 %collective-permute-done.10.rest_0_ = bf16[128,1536]{1,0:T(8,128)(2,1)S(1)} collective-permute-done((bf16[128,1536]{1,0:T(8,128)(2,1)S(1)}, bf16[128,1536]{1,0:T(8,128)(2,1)S(1)}, u32[]{:S(2)}, u32[]{:S(2)}) %collective-permute-start.10) | collective-permute-done | bytes 393248 | tf_op jit(solution)/shard_map/ppermute | solution.py:37
  70.6 1.9 %collective-permute-start.11 = (bf16[128,1536]{1,0:T(8,128)(2,1)S(1)}, bf16[128,1536]{1,0:T(8,128)(2,1)S(1)}, u32[]{:S(2)}, u32[]{:S(2)}) collective-permute-start(bf16[128,1536]{1,0:T(8,128)(2,1)S(1)} %get-tuple-element.46.after_ref), channel_id=1, source_target_pairs={{0,1},{1,2},{2,3},{3,4},{4,5},{5,6},{6,7},{7,8},{8,9},{9,10},{10,1... | collective-permute-start | bytes 1179656 | tf_op jit(solution)/shard_map/ppermute | solution.py:37
  75.2 2.0 %collective-permute-done.13.rest_0_ = bf16[128,1536]{1,0:T(8,128)(2,1)S(1)} collective-permute-done((bf16[128,1536]{1,0:T(8,128)(2,1)S(1)}, bf16[128,1536]{1,0:T(8,128)(2,1)S(1)}, u32[]{:S(2)}, u32[]{:S(2)}) %collective-permute-start.13) | collective-permute-done | bytes 393248 | tf_op jit(solution)/shard_map/ppermute | solution.py:37
  80.8 7.1 %collective-permute-done.14.moved_ref = bf16[128,1536]{1,0:T(8,128)(2,1)S(1)} collective-permute-done((bf16[128,1536]{1,0:T(8,128)(2,1)S(1)}, bf16[128,1536]{1,0:T(8,128)(2,1)S(1)}, u32[]{:S(2)}, u32[]{:S(2)}) %collective-permute-start.14) | collective-permute-done | bytes 393248 | tf_op jit(solution)/shard_map/ppermute | solution.py:37
  87.9 2.2 %shard_map.64.after_ref.rest_0_ = bf16[2,512,1536]{2,1,0:T(8,128)(2,1)} custom-call(bf16[128,1536]{1,0:T(8,128)(2,1)S(1)} %get-tuple-element.52.after_ref, bf16[512,1536]{1,0:T(8,128)(2,1)S(1)} %get-tuple-element.33.start_ref.after_ref, bf16[2,1536,1536]{2,1,0:T(8,128)(2,1)S(1)} %get-tuple-element.34.w_ref, f32[8,1536]{1,0:T(8,128)S(1)} %get-tuple-element.35.p_ref, ...), custom_call_target="tpu_custom_call" | custom-call | flops 1207959552 | bytes 1572864 | tf_op jit(solution)/shard_map/pallas_call | solution.py:213
  90.1 8.2 %collective-permute-done.15.rest_0_ = bf16[128,1536]{1,0:T(8,128)(2,1)S(1)} collective-permute-done((bf16[128,1536]{1,0:T(8,128)(2,1)S(1)}, bf16[128,1536]{1,0:T(8,128)(2,1)S(1)}, u32[]{:S(2)}, u32[]{:S(2)}) %collective-permute-start.15) | collective-permute-done | bytes 393248 | tf_op jit(solution)/shard_map/ppermute | solution.py:37
  100.5 2.3 %shard_map.66.after_ref.rest_0_ = bf16[2,512,1536]{2,1,0:T(8,128)(2,1)} custom-call(bf16[128,1536]{1,0:T(8,128)(2,1)S(1)} %get-tuple-element.55.after_ref, bf16[512,1536]{1,0:T(8,128)(2,1)S(1)} %get-tuple-element.33.start_ref.after_ref, bf16[2,1536,1536]{2,1,0:T(8,128)(2,1)S(1)} %get-tuple-element.34.w_ref, ...), custom_call_target="tpu_custom_call", output_to_operand_aliasing={{}: (8, {})} | custom-call | flops 1207959552 | bytes 1572864 | tf_op jit(solution)/shard_map/pallas_call | solution.py:213
  105.0 4.4 %collective-permute-done.19.moved_ref = bf16[128,1536]{1,0:T(8,128)(2,1)S(1)} collective-permute-done((bf16[128,1536]{1,0:T(8,128)(2,1)S(1)}, bf16[128,1536]{1,0:T(8,128)(2,1)S(1)}, u32[]{:S(2)}, u32[]{:S(2)}) %collective-permute-start.19) | collective-permute-done | bytes 393248 | tf_op jit(solution)/shard_map/ppermute | solution.py:37
  109.4 2.2 %shard_map.68.rest_0_ = bf16[2,512,1536]{2,1,0:T(8,128)(2,1)} custom-call(bf16[128,1536]{1,0:T(8,128)(2,1)S(1)} %get-tuple-element.58.after_ref, bf16[512,1536]{1,0:T(8,128)(2,1)S(1)} %get-tuple-element.33.start_ref.after_ref, bf16[2,1536,1536]{2,1,0:T(8,128)(2,1)S(1)} %get-tuple-element.34.w_ref, ...), custom_call_target="tpu_custom_call", output_to_operand_aliasing={{}: (8, {})} | custom-call | flops 1207959552 | bytes 1572864 | tf_op jit(solution)/shard_map/pallas_call | solution.py:213
  111.7 1.9 %collective-permute-done.18.moved_ref = bf16[128,1536]{1,0:T(8,128)(2,1)S(1)} collective-permute-done((bf16[128,1536]{1,0:T(8,128)(2,1)S(1)}, bf16[128,1536]{1,0:T(8,128)(2,1)S(1)}, u32[]{:S(2)}, u32[]{:S(2)}) %collective-permute-start.18) | collective-permute-done | bytes 393248 | tf_op jit(solution)/shard_map/ppermute | solution.py:37
  113.5 2.2 %shard_map.69 = bf16[2,512,1536]{2,1,0:T(8,128)(2,1)} custom-call(bf16[512,1536]{1,0:T(8,128)(2,1)S(1)} %get-tuple-element.33.start_ref.after_ref, bf16[512,1536]{1,0:T(8,128)(2,1)S(1)} %get-tuple-element.33.start_ref.after_ref, bf16[2,1536,1536]{2,1,0:T(8,128)(2,1)S(1)} %get-tuple-element.34.w_ref, ...), custom_call_target="tpu_custom_call", output_to_operand_aliasing={{}: (8, {})} | custom-call | flops 1207959552 | bytes 1572864 | tf_op jit(solution)/shard_map/pallas_call | solution.py:213
  (40 shorter events, 29.8 us)
Async XLA Ops:
  5.7 8.4 %collective-permute-start = (bf16[128,1536]{1,0:T(8,128)(2,1)S(1)}, bf16[128,1536]{1,0:T(8,128)(2,1)S(1)}, u32[]{:S(2)}, u32[]{:S(2)}) collective-permute-start(bf16[128,1536]{1,0:T(8,128)(2,1)S(1)} %get-tuple-element.36.after_ref), channel_id=1, source_target_pairs={{0,1},{1,2},{2,3},{3,4},{4,5},{5,6},{6,7},{7,8},{8,9},{9,10},{10,1... | collective-permute-start | bytes 1179656 | tf_op jit(solution)/shard_map/ppermute | solution.py:37
  10.8 12.3 %collective-permute-start.1 = (bf16[128,1536]{1,0:T(8,128)(2,1)S(1)}, bf16[128,1536]{1,0:T(8,128)(2,1)S(1)}, u32[]{:S(2)}, u32[]{:S(2)}) collective-permute-start(bf16[128,1536]{1,0:T(8,128)(2,1)S(1)} %shard_map.47.after_ref), channel_id=1, source_target_pairs={{0,1},{1,2},{2,3},{3,4},{4,5},{5,6},{6,7},{7,8},{8,9},{9,10},{10,1... | collective-permute-start | bytes 1179656 | tf_op jit(solution)/shard_map/ppermute | solution.py:37
  15.5 11.0 %collective-permute-start.2 = (bf16[128,1536]{1,0:T(8,128)(2,1)S(1)}, bf16[128,1536]{1,0:T(8,128)(2,1)S(1)}, u32[]{:S(2)}, u32[]{:S(2)}) collective-permute-start(bf16[128,1536]{1,0:T(8,128)(2,1)S(1)} %shard_map.48.after_ref), channel_id=1, source_target_pairs={{0,1},{1,2},{2,3},{3,4},{4,5},{5,6},{6,7},{7,8},{8,9},{9,10},{10,1... | collective-permute-start | bytes 1179656 | tf_op jit(solution)/shard_map/ppermute | solution.py:37
  24.6 14.7 %collective-permute-start.3 = (bf16[128,1536]{1,0:T(8,128)(2,1)S(1)}, bf16[128,1536]{1,0:T(8,128)(2,1)S(1)}, u32[]{:S(2)}, u32[]{:S(2)}) collective-permute-start(bf16[128,1536]{1,0:T(8,128)(2,1)S(1)} %shard_map.50.after_ref), channel_id=1, source_target_pairs={{0,1},{1,2},{2,3},{3,4},{4,5},{5,6},{6,7},{7,8},{8,9},{9,10},{10,1... | collective-permute-start | bytes 1179656 | tf_op jit(solution)/shard_map/ppermute | solution.py:37
  28.0 14.7 %collective-permute-start.4 = (bf16[128,1536]{1,0:T(8,128)(2,1)S(1)}, bf16[128,1536]{1,0:T(8,128)(2,1)S(1)}, u32[]{:S(2)}, u32[]{:S(2)}) collective-permute-start(bf16[128,1536]{1,0:T(8,128)(2,1)S(1)} %get-tuple-element.37.after_ref), channel_id=1, source_target_pairs={{0,1},{1,2},{2,3},{3,4},{4,5},{5,6},{6,7},{7,8},{8,9},{9,10},{10,1... | collective-permute-start | bytes 1179656 | tf_op jit(solution)/shard_map/ppermute | solution.py:37
  34.0 8.9 %collective-permute-start.5 = (bf16[128,1536]{1,0:T(8,128)(2,1)S(1)}, bf16[128,1536]{1,0:T(8,128)(2,1)S(1)}, u32[]{:S(2)}, u32[]{:S(2)}) collective-permute-start(bf16[128,1536]{1,0:T(8,128)(2,1)S(1)} %shard_map.49.after_ref), channel_id=1, source_target_pairs={{0,1},{1,2},{2,3},{3,4},{4,5},{5,6},{6,7},{7,8},{8,9},{9,10},{10,1... | collective-permute-start | bytes 1179656 | tf_op jit(solution)/shard_map/ppermute | solution.py:37
  37.4 14.5 %collective-permute-start.6 = (bf16[128,1536]{1,0:T(8,128)(2,1)S(1)}, bf16[128,1536]{1,0:T(8,128)(2,1)S(1)}, u32[]{:S(2)}, u32[]{:S(2)}) collective-permute-start(bf16[128,1536]{1,0:T(8,128)(2,1)S(1)} %shard_map.52.after_ref), channel_id=1, source_target_pairs={{0,1},{1,2},{2,3},{3,4},{4,5},{5,6},{6,7},{7,8},{8,9},{9,10},{10,1... | collective-permute-start | bytes 1179656 | tf_op jit(solution)/shard_map/ppermute | solution.py:37
  40.8 14.5 %collective-permute-start.8 = (bf16[128,1536]{1,0:T(8,128)(2,1)S(1)}, bf16[128,1536]{1,0:T(8,128)(2,1)S(1)}, u32[]{:S(2)}, u32[]{:S(2)}) collective-permute-start(bf16[128,1536]{1,0:T(8,128)(2,1)S(1)} %get-tuple-element.38.after_ref), channel_id=1, source_target_pairs={{0,1},{1,2},{2,3},{3,4},{4,5},{5,6},{6,7},{7,8},{8,9},{9,10},{10,1... | collective-permute-start | bytes 1179656 | tf_op jit(solution)/shard_map/ppermute | solution.py:37
  44.4 12.2 %collective-permute-start.9 = (bf16[128,1536]{1,0:T(8,128)(2,1)S(1)}, bf16[128,1536]{1,0:T(8,128)(2,1)S(1)}, u32[]{:S(2)}, u32[]{:S(2)}) collective-permute-start(bf16[128,1536]{1,0:T(8,128)(2,1)S(1)} %shard_map.55.after_ref), channel_id=1, source_target_pairs={{0,1},{1,2},{2,3},{3,4},{4,5},{5,6},{6,7},{7,8},{8,9},{9,10},{10,1... | collective-permute-start | bytes 1179656 | tf_op jit(solution)/shard_map/ppermute | solution.py:37
  50.6 17.8 %collective-permute-start.10 = (bf16[128,1536]{1,0:T(8,128)(2,1)S(1)}, bf16[128,1536]{1,0:T(8,128)(2,1)S(1)}, u32[]{:S(2)}, u32[]{:S(2)}) collective-permute-start(bf16[128,1536]{1,0:T(8,128)(2,1)S(1)} %get-tuple-element.40.after_ref), channel_id=1, source_target_pairs={{8,16},{9,17},{10,18},{11,19},{12,20},{13,21},{14,22},{15,23}} | collective-permute-start | bytes 1179656 | tf_op jit(solution)/shard_map/ppermute | solution.py:37
  53.3 15.9 %collective-permute-start.7 = (bf16[128,1536]{1,0:T(8,128)(2,1)S(1)}, bf16[128,1536]{1,0:T(8,128)(2,1)S(1)}, u32[]{:S(2)}, u32[]{:S(2)}) collective-permute-start(bf16[128,1536]{1,0:T(8,128)(2,1)S(1)} %shard_map.56.after_ref), channel_id=1, source_target_pairs={{0,1},{1,2},{2,3},{3,4},{4,5},{5,6},{6,7},{7,8},{8,9},{9,10},{10,1... | collective-permute-start | bytes 1179656 | tf_op jit(solution)/shard_map/ppermute | solution.py:37
  55.3 22.0 %collective-permute-start.13 = (bf16[128,1536]{1,0:T(8,128)(2,1)S(1)}, bf16[128,1536]{1,0:T(8,128)(2,1)S(1)}, u32[]{:S(2)}, u32[]{:S(2)}) collective-permute-start(bf16[128,1536]{1,0:T(8,128)(2,1)S(1)} %get-tuple-element.42.after_ref), channel_id=1, source_target_pairs={{8,16},{9,17},{10,18},{11,19},{12,20},{13,21},{14,22},{15,23}} | collective-permute-start | bytes 1179656 | tf_op jit(solution)/shard_map/ppermute | solution.py:37
  58.0 15.9 %collective-permute-start.12 = (bf16[128,1536]{1,0:T(8,128)(2,1)S(1)}, bf16[128,1536]{1,0:T(8,128)(2,1)S(1)}, u32[]{:S(2)}, u32[]{:S(2)}) collective-permute-start(bf16[128,1536]{1,0:T(8,128)(2,1)S(1)} %get-tuple-element.43.after_ref), channel_id=1, source_target_pairs={{0,1},{1,2},{2,3},{3,4},{4,5},{5,6},{6,7},{7,8},{8,9},{9,10},{10,1... | collective-permute-start | bytes 1179656 | tf_op jit(solution)/shard_map/ppermute | solution.py:37
  70.6 8.8 %collective-permute-start.11 = (bf16[128,1536]{1,0:T(8,128)(2,1)S(1)}, bf16[128,1536]{1,0:T(8,128)(2,1)S(1)}, u32[]{:S(2)}, u32[]{:S(2)}) collective-permute-start(bf16[128,1536]{1,0:T(8,128)(2,1)S(1)} %get-tuple-element.46.after_ref), channel_id=1, source_target_pairs={{0,1},{1,2},{2,3},{3,4},{4,5},{5,6},{6,7},{7,8},{8,9},{9,10},{10,1... | collective-permute-start | bytes 1179656 | tf_op jit(solution)/shard_map/ppermute | solution.py:37
  72.6 15.3 %collective-permute-start.14 = (bf16[128,1536]{1,0:T(8,128)(2,1)S(1)}, bf16[128,1536]{1,0:T(8,128)(2,1)S(1)}, u32[]{:S(2)}, u32[]{:S(2)}) collective-permute-start(bf16[128,1536]{1,0:T(8,128)(2,1)S(1)} %get-tuple-element.45.after_ref), channel_id=1, source_target_pairs={{16,24},{17,25},{18,26},{19,27},{20,28},{21,29},{22,30},{23,31}} | collective-permute-start | bytes 1179656 | tf_op jit(solution)/shard_map/ppermute | solution.py:37
  73.9 24.4 %collective-permute-start.15 = (bf16[128,1536]{1,0:T(8,128)(2,1)S(1)}, bf16[128,1536]{1,0:T(8,128)(2,1)S(1)}, u32[]{:S(2)}, u32[]{:S(2)}) collective-permute-start(bf16[128,1536]{1,0:T(8,128)(2,1)S(1)} %get-tuple-element.48.after_ref), channel_id=1, source_target_pairs={{8,16},{9,17},{10,18},{11,19},{12,20},{13,21},{14,22},{15,23}} | collective-permute-start | bytes 1179656 | tf_op jit(solution)/shard_map/ppermute | solution.py:37
  78.1 22.4 %collective-permute-start.16 = (bf16[128,1536]{1,0:T(8,128)(2,1)S(1)}, bf16[128,1536]{1,0:T(8,128)(2,1)S(1)}, u32[]{:S(2)}, u32[]{:S(2)}) collective-permute-start(bf16[128,1536]{1,0:T(8,128)(2,1)S(1)} %get-tuple-element.50.after_ref), channel_id=1, source_target_pairs={{16,24},{17,25},{18,26},{19,27},{20,28},{21,29},{22,30},{23,31}} | collective-permute-start | bytes 1179656 | tf_op jit(solution)/shard_map/ppermute | solution.py:37
  79.5 23.3 %collective-permute-start.17 = (bf16[128,1536]{1,0:T(8,128)(2,1)S(1)}, bf16[128,1536]{1,0:T(8,128)(2,1)S(1)}, u32[]{:S(2)}, u32[]{:S(2)}) collective-permute-start(bf16[128,1536]{1,0:T(8,128)(2,1)S(1)} %get-tuple-element.52.after_ref), channel_id=1, source_target_pairs={{8,16},{9,17},{10,18},{11,19},{12,20},{13,21},{14,22},{15,23}} | collective-permute-start | bytes 1179656 | tf_op jit(solution)/shard_map/ppermute | solution.py:37
  99.2 10.2 %collective-permute-start.19 = (bf16[128,1536]{1,0:T(8,128)(2,1)S(1)}, bf16[128,1536]{1,0:T(8,128)(2,1)S(1)}, u32[]{:S(2)}, u32[]{:S(2)}) collective-permute-start(bf16[128,1536]{1,0:T(8,128)(2,1)S(1)} %get-tuple-element.55.after_ref), channel_id=1, source_target_pairs={{16,24},{17,25},{18,26},{19,27},{20,28},{21,29},{22,30},{23,31}} | collective-permute-start | bytes 1179656 | tf_op jit(solution)/shard_map/ppermute | solution.py:37
  103.7 9.8 %collective-permute-start.18 = (bf16[128,1536]{1,0:T(8,128)(2,1)S(1)}, bf16[128,1536]{1,0:T(8,128)(2,1)S(1)}, u32[]{:S(2)}, u32[]{:S(2)}) collective-permute-start(bf16[128,1536]{1,0:T(8,128)(2,1)S(1)} %get-tuple-element.58.after_ref), channel_id=1, source_target_pairs={{16,24},{17,25},{18,26},{19,27},{20,28},{21,29},{22,30},{23,31}} | collective-permute-start | bytes 1179656 | tf_op jit(solution)/shard_map/ppermute | solution.py:37

commit v3 on v2

v3 whole, which is shorter than its diff:
```python
import functools

import jax
import jax.numpy as jnp
from jax import lax
from jax.experimental import pallas as pl
from jax.experimental.pallas import tpu as pltpu
from jax.sharding import PartitionSpec as P

LAY_DEV = 2
INTERVAL = 8

SHARES = (4, 5, 4, 3)
ORDER = (
    0, 20, 10, 1, 21, 11, 2, 30, 12, 3, 31, 22, 13, 17, 4, 32, 23, 14, 33, 5, 24, 34, 15, 25, 35,
)
RELAYS = {8: (0, 2), 6: (1, 6), 7: (2, 2)}
TILE = 512
VMEM_BYTES = 20 << 20
VMEM = pl.BlockSpec(memory_space=pltpu.VMEM)
ANY = pl.BlockSpec(memory_space=pl.ANY)
DMA = pltpu.SemaphoreType.DMA


def held(value):
    return pltpu.with_memory_space_constraint(value, pltpu.VMEM)


def kept(shape, kind):
    return pltpu.VMEM(shape, kind)


def in_hbm(value):
    return pltpu.with_memory_space_constraint(value, pltpu.HBM)


def passed_along(value, pairs):
    return lax.ppermute(value, "depth", pairs)


def tiles(width):
    tile = TILE if width % TILE == 0 else width
    return [slice(low, low + tile) for low in range(0, width, tile)]


def bend(state, w_ref, p_ref, layer, cols):
    pre = jnp.dot(state, w_ref[layer, :, cols], preferred_element_type=jnp.float32)
    return jnp.tanh(pre + p_ref[layer : layer + 1, cols])


def opening_kernel(rows, start_hbm, w_hbm, b_hbm, h_hbm, out_ref, w_ref, p_ref, start, state, rounded, b_ref, h_ref, w_sems, sems):
    width = w_hbm.shape[2]
    small = [
        pltpu.make_async_copy(start_hbm.at[rows, :], start, sems.at[0]),
        pltpu.make_async_copy(b_hbm, b_ref, sems.at[1]),
        pltpu.make_async_copy(h_hbm, h_ref, sems.at[2]),
    ]
    for copy in small:
        copy.start()
    copies = []
    for layer in range(LAY_DEV):
        for cols in tiles(width):
            copy = pltpu.make_async_copy(
                w_hbm.at[layer, :, cols], w_ref.at[layer, :, cols], w_sems.at[len(copies)]
            )
            copy.start()
            copies.append(copy)
    for copy in small:
        copy.wait()
    p_ref[0:2, :] = b_ref[...]
    for layer in range(LAY_DEV):
        p_ref[2 + layer : 3 + layer, :] = jnp.full((1, width), h_ref[layer], jnp.float32)
    p_ref[4:8, :] = jnp.zeros((4, width), jnp.float32)
    for index, cols in enumerate(tiles(width)):
        copies[index].wait()
        moved = start[:, cols].astype(jnp.float32) + p_ref[2:3, cols] * bend(start[...], w_ref, p_ref, 0, cols)
        state[:, cols] = moved
        rounded[:, cols] = moved.astype(jnp.bfloat16)
    for index, cols in enumerate(tiles(width)):
        copies[len(tiles(width)) + index].wait()
        bent = bend(rounded[...], w_ref, p_ref, 1, cols)
        out_ref[:, cols] = (state[:, cols] + p_ref[3:4, cols] * bent).astype(jnp.bfloat16)


def total_of(parts):
    return sum(part[...].astype(jnp.float32) for part in parts)


def pass_kernel(rows, parts, keep, extra, start_ref, w_ref, p_ref, *rest):
    arrived, rest = rest[:parts], rest[parts + extra :]
    if parts:
        if keep:
            out_ref, t_ref, entering, state, rounded = rest
        else:
            out_ref, entering, state, rounded = rest
        came = total_of(arrived).astype(jnp.bfloat16) if parts > 1 else arrived[0][...]
        entering[...] = jnp.where(lax.axis_index("depth") == 0, start_ref[rows, :], came)
    else:
        out_ref, state, rounded = rest
        entering = start_ref.at[rows, :]
    for cols in tiles(w_ref.shape[2]):
        bent = bend(entering[...], w_ref, p_ref, 0, cols)
        if keep:
            t_ref[:, cols] = bent
        moved = entering[:, cols].astype(jnp.float32) + p_ref[2:3, cols] * bent
        state[:, cols] = moved
        rounded[:, cols] = moved.astype(jnp.bfloat16)
    for cols in tiles(w_ref.shape[2]):
        bent = bend(rounded[...], w_ref, p_ref, 1, cols)
        out_ref[:, cols] = (state[:, cols] + p_ref[3:4, cols] * bent).astype(jnp.bfloat16)


def relay_kernel(place, extra, came_ref, *rest):
    (out_ref,) = rest[extra:]

    @pl.when(lax.axis_index("depth") % INTERVAL == place)
    def _():
        out_ref[...] = came_ref[...]


def correction_of(entry, fresh, moved_ref):
    total = fresh - entry
    if moved_ref is not None:
        total = moved_ref[...].astype(jnp.float32) + total
    return total.astype(jnp.bfloat16)


def coarse_kernel(group, extra, parts, t_ref, w_ref, p_ref, *rest):
    (entry_parts, fresh_parts), rest = parts, rest
    entry_refs, rest = rest[:entry_parts], rest[entry_parts:]
    fresh_refs, rest = rest[:fresh_parts], rest[fresh_parts:]
    moved_ref = None
    if group > 1:
        moved_ref, before_ref, *rest = rest
    out_ref, correction_ref, rounded = rest[extra:]

    here = lax.axis_index("depth") // INTERVAL == group
    if group > 1:

        @pl.when(jnp.logical_not(here))
        def _():
            correction_ref[...] = before_ref[...]

    @pl.when(here)
    def _():
        entry = total_of(entry_refs)
        correction = correction_of(entry, total_of(fresh_refs), moved_ref)
        correction_ref[...] = correction
        rounded[...] = (entry + correction.astype(jnp.float32)).astype(jnp.bfloat16)
        for cols in tiles(w_ref.shape[2]):
            bent = bend(rounded[...], w_ref, p_ref, 0, cols)
            change = (INTERVAL * LAY_DEV) * p_ref[2:3, cols] * (bent - t_ref[:, cols])
            out_ref[:, cols] = (correction_ref[:, cols].astype(jnp.float32) + change).astype(jnp.bfloat16)


def final_kernel(rows, groups, aliased, extra, parts, start_ref, w_ref, p_ref, moved_ref, correction_ref, *rest):
    entry_parts, fresh_parts = parts
    entry_refs, rest = rest[:entry_parts], rest[entry_parts:]
    fresh_refs, rest = rest[:fresh_parts], rest[fresh_parts + int(aliased) + extra :]
    states, token, state, first, second, sems = rest
    token[...] = jnp.zeros_like(token)
    device = lax.axis_index("depth")
    group = device // INTERVAL
    width = w_ref.shape[2]

    entry = total_of(entry_refs)

    @pl.when(group == 0)
    def _():
        state[...] = jnp.where(device == 0, start_ref[rows, :].astype(jnp.float32), entry)

    @pl.when((group > 0) & (group < groups - 1))
    def _():
        state[...] = entry + correction_ref[...].astype(jnp.float32)

    @pl.when((group > 0) & (group == groups - 1))
    def _():
        state[...] = entry + correction_of(entry, total_of(fresh_refs), moved_ref).astype(jnp.float32)

    second[...] = state[...].astype(jnp.bfloat16)
    copies = []
    for cols in tiles(width):
        moved = state[:, cols] + p_ref[2:3, cols] * bend(second[...], w_ref, p_ref, 0, cols)
        state[:, cols] = moved
        first[:, cols] = moved.astype(jnp.bfloat16)
        copy = pltpu.make_async_copy(first.at[:, cols], states.at[0, rows, cols], sems.at[len(copies)])
        copy.start()
        copies.append(copy)
    for cols in tiles(width):
        bent = bend(first[...], w_ref, p_ref, 1, cols)
        second[:, cols] = (state[:, cols] + p_ref[3:4, cols] * bent).astype(jnp.bfloat16)
        copy = pltpu.make_async_copy(second.at[:, cols], states.at[1, rows, cols], sems.at[len(copies)])
        copy.start()
        copies.append(copy)
    for copy in copies:
        copy.wait()


def order_of(groups):
    order, late = [], []
    for item in ORDER:
        chunk, step = divmod(item, 10)
        if step < 3:
            order.append(("pass", chunk, step))
        elif step in RELAYS:
            order.append(("relay", chunk, step))
        elif step < 5:
            if step - 2 < groups - 1:
                order.append(("coarse", chunk, step - 2))
        elif groups > 4:
            late.append(("final", chunk, 0))
        else:
            order.append(("final", chunk, 0))
    for group in range(3, groups - 1):
        order += [("coarse", chunk, group) for _, chunk, _ in late]
    return order + late


def local(initial, weights, biases, step_sizes):
    count = lax.axis_size("depth")
    groups = count // INTERVAL
    width = initial.shape[2]
    start = initial.reshape(-1, width)
    total = start.shape[0]
    bounds = [0]
    for share in SHARES:
        bounds.append(bounds[-1] + share * total // sum(SHARES))
    spans = [slice(low, high) for low, high in zip(bounds, bounds[1:])]
    sizes = [span.stop - span.start for span in spans]
    parts = len(tiles(width))
    one_on = [(source, source + 1) for source in range(count - 1)]
    ends = range(2 * INTERVAL - 1, count - 1, INTERVAL)
    straight = [pair for pair in one_on if pair[0] not in ends]

    def narrow(size):
        return kept((size, width), jnp.bfloat16)

    def call(body, outs, scratch, operands, specs=None, out_specs=None, aliases=None):
        specs = specs or [VMEM] * len(operands)
        return pl.pallas_call(
            body,
            out_shape=outs,
            in_specs=specs,
            out_specs=out_specs or jax.tree.map(lambda _: VMEM, outs),
            scratch_shapes=scratch,
            input_output_aliases=aliases or {},
            compiler_params=pltpu.CompilerParams(vmem_limit_bytes=VMEM_BYTES),
            cost_estimate=pl.CostEstimate(
                flops=2 * LAY_DEV * total * width * width, bytes_accessed=0, transcendentals=0
            ),
        )(*[held(value) if spec is VMEM else in_hbm(value) for value, spec in zip(operands, specs)])

    first = sizes[0]
    leaving, w, p = call(
        functools.partial(opening_kernel, spans[0]),
        (narrow(first), kept(weights.shape, jnp.bfloat16), kept((8, width), jnp.float32)),
        [
            pltpu.VMEM((first, width), jnp.bfloat16),
            pltpu.VMEM((first, width), jnp.float32), pltpu.VMEM((first, width), jnp.bfloat16),
            pltpu.VMEM(biases.shape, jnp.float32), pltpu.SMEM(step_sizes.shape, jnp.float32),
            DMA((LAY_DEV * parts,)), DMA((3,)),
        ],
        [start, weights, biases, step_sizes], [ANY] * 4,
    )
    chunks = len(SHARES)
    bent, correction, moved = [None] * chunks, [None] * chunks, [None] * chunks
    arrived = [[] for _ in range(chunks)]
    asides, underway = {}, []
    relayed = {(item // 10, RELAYS[item % 10][0]): item % 10 for item in ORDER if item % 10 in RELAYS}

    def sent(value, pairs):
        underway.append(passed_along(value, pairs))
        return underway[-1]

    def passed(value, chunk, step):
        kind = relayed.get((chunk, step))
        if kind is None:
            arrived[chunk].append([sent(value, one_on)])
        else:
            back = RELAYS[kind][1]
            arrived[chunk].append([sent(value, straight)])
            asides[chunk, step] = sent(value, [(end, end - back) for end in ends])

    def earlier(values):
        found = []
        for value in values:
            if any(value is other for other in underway):
                while True:
                    oldest = underway.pop(0)
                    if oldest is value:
                        break
                    found.append(oldest)
        return [other for other in found if not any(other is value for value in values)]

    passed(leaving, 0, 0)
    after, states = [leaving], None
    for kind, chunk, step in order_of(groups)[1:]:
        size = sizes[chunk]
        wide = pltpu.VMEM((size, width), jnp.float32)
        thin = pltpu.VMEM((size, width), jnp.bfloat16)
        if kind == "pass":
            keep = step == 2
            came = arrived[chunk][step - 1] if step else []
            extra = after + earlier(came)
            result = call(
                functools.partial(pass_kernel, spans[chunk], len(came), keep, len(extra)),
                (narrow(size), kept((size, width), jnp.float32)) if keep else narrow(size),
                [thin, wide, thin] if step else [wide, thin],
                [start, w, p] + came + extra,
            )
            if keep:
                leaving, bent[chunk] = result
            else:
                leaving = result
            passed(leaving, chunk, step)
            after = [leaving]
        elif kind == "relay":
            step, back = RELAYS[step]
            came = asides[chunk, step]
            extra = after + earlier([came])
            leaving = call(
                functools.partial(relay_kernel, INTERVAL - 1 - back, len(extra)), narrow(size), [], [came] + extra
            )
            arrived[chunk][step].append(sent(leaving, [(end - back, end + 1) for end in ends]))
            after = [leaving]
        elif kind == "coarse":
            _, entry, fresh = arrived[chunk]
            if step == 1:
                fresh = fresh[:1]
            operands = [bent[chunk], w, p] + entry + fresh
            needed = entry + fresh
            if step > 1:
                operands += [moved[chunk], correction[chunk]]
                needed = needed + [moved[chunk]]
            extra = after + earlier(needed)
            delta, correction[chunk] = call(
                functools.partial(coarse_kernel, step, len(extra), (len(entry), len(fresh))),
                (narrow(size), narrow(size)), [thin], operands + extra,
            )
            ahead = [(source, source + INTERVAL) for source in range(step * INTERVAL, (step + 1) * INTERVAL)]
            moved[chunk] = sent(delta, ahead)
            after = [delta]
        else:
            _, entry, fresh = arrived[chunk]
            extra = after + earlier([moved[chunk]])
            operands = [start, w, p, moved[chunk], correction[chunk]] + entry + fresh
            specs = [VMEM] * len(operands)
            aliases = None
            if states is not None:
                aliases = {len(operands): 0}
                operands.append(states)
                specs.append(ANY)
            states, token = call(
                functools.partial(
                    final_kernel, spans[chunk], groups, states is not None, len(extra), (len(entry), len(fresh))
                ),
                (jax.ShapeDtypeStruct((LAY_DEV, total, width), jnp.bfloat16), kept((8, 128), jnp.float32)),
                [wide, thin, thin, DMA((LAY_DEV * parts,))],
                operands + extra, specs + [VMEM] * len(extra), (ANY, VMEM), aliases,
            )
            after = [token]
    return states.reshape(LAY_DEV, initial.shape[0], -1, width)


def solution(mesh):
    placed = (P(), P("depth", None, None), P("depth", None), P("depth"))
    return jax.shard_map(
        local, mesh=mesh, in_specs=placed, out_specs=P("depth", None, None, None), check_vma=False
    )
```

time: 117 us -> 106 us (0.906)
  waiting for transfers between devices: 30.1 us -> 20.5 us
  starting transfers between devices: 51.2 us -> 46.4 us
  Pallas kernels: 34.1 us -> 36.8 us
    ppermute x20 -> x22, waiting for transfers between devices: 30.1 us -> 20.5 us  [passed_along(): return lax.ppermute(value, 'depth', pairs)]
    ppermute x20 -> x22, starting transfers between devices: 51.2 us -> 46.4 us  [passed_along(): return lax.ppermute(value, 'depth', pairs)]
    pallas_call x24 -> x25, Pallas kernels: 34.1 us -> 36.8 us  [call(): pl.pallas_call(body, out_shape=outs, in_specs=specs, out_specs=out_specs...]
  transfers between devices with their start and end apart: 20 -> 22, of which waited for: 7 -> 5; matrix products, arithmetic and copies ran while one was open for 0% -> 0% of each run, Pallas kernels for 23% -> 27%
where the time goes in v3:
time: 106 us; the launch traced here: 104 us
  starting transfers between devices  46.4 us (44%)
  Pallas kernels  36.8 us (35%)
  waiting for transfers between devices  20.5 us (19%)
    ppermute x22, starting transfers between devices, passed_along(): return lax.ppermute(value, 'depth', pairs)  46.4 us
    pallas_call x25, Pallas kernels, call(): pl.pallas_call(body, out_shape=outs, in_specs=specs, out_specs=out_specs...  36.8 us
    ppermute x22, waiting for transfers between devices, passed_along(): return lax.ppermute(value, 'depth', pairs)  20.5 us
  transfers between devices with their start and end apart: 22, of which 5 were waited for; matrix products, arithmetic and copies ran while one was open for 0% of the time, Pallas kernels for 27%

profile of v3, /device:TPU:23, one launch (start us, length us, event | category | flops | bytes accessed | tf_op | source)
XLA Modules:
  0.0 104.4 jit_solution(4362824917287905924)
XLA Ops:
  0.0 5.3 %shard_map.46 = (bf16[128,1536]{1,0:T(8,128)(2,1)S(1)}, bf16[2,1536,1536]{2,1,0:T(8,128)(2,1)S(1)}, f32[8,1536]{1,0:T(8,128)S(1)}) custom-call(bf16[512,1536]{1,0:T(8,128)(2,1)} %bitcast.2, bf16[2,1536,1536]{2,1,0:T(8,128)(2,1)} %w_hbm.1, f32[2,1536]{1,0:T(2,128)} %b_hbm.1, f32[2]{0:T(128)} %h_hbm.1), custom_call_target="tpu_custom_call" | custom-call | flops 4831838208 | tf_op jit(solution)/shard_map/pallas_call | solution.py:240
  5.3 3.7 %collective-permute-start = (bf16[128,1536]{1,0:T(8,128)(2,1)S(1)}, bf16[128,1536]{1,0:T(8,128)(2,1)S(1)}, u32[]{:S(2)}, u32[]{:S(2)}) collective-permute-start(bf16[128,1536]{1,0:T(8,128)(2,1)S(1)} %get-tuple-element.41.rest_0_), channel_id=1, source_target_pairs={{0,1},{1,2},{2,3},{3,4},{4,5},{5,6},{6,7},{7,8},{8,9},{9,10},{10,1... | collective-permute-start | bytes 1179656 | tf_op jit(solution)/shard_map/ppermute | solution.py:38
  10.4 1.9 %collective-permute-start.3 = (bf16[128,1536]{1,0:T(8,128)(2,1)S(1)}, bf16[128,1536]{1,0:T(8,128)(2,1)S(1)}, u32[]{:S(2)}, u32[]{:S(2)}) collective-permute-start(bf16[128,1536]{1,0:T(8,128)(2,1)S(1)} %shard_map.47.rest_0_), channel_id=1, source_target_pairs={{0,1},{1,2},{2,3},{3,4},{4,5},{5,6},{6,7},{7,8},{8,9},{9,10},{10,1... | collective-permute-start | bytes 1179656 | tf_op jit(solution)/shard_map/ppermute | solution.py:38
  12.4 1.7 %shard_map.48.rest_1_ = bf16[160,1536]{1,0:T(8,128)(2,1)S(1)} custom-call(bf16[512,1536]{1,0:T(8,128)(2,1)S(1)} %bitcast.4, bf16[2,1536,1536]{2,1,0:T(8,128)(2,1)S(1)} %get-tuple-element.39.w_ref, f32[8,1536]{1,0:T(8,128)S(1)} %get-tuple-element.40.p_ref, bf16[128,1536]{1,0:T(8,128)(2,1)S(1)} %shard_map.47.rest_0_), custom_call_target="tpu_custom_call" | custom-call | flops 4831838208 | tf_op jit(solution)/shard_map/pallas_call | solution.py:240
  14.1 3.5 %collective-permute-start.2 = (bf16[160,1536]{1,0:T(8,128)(2,1)S(1)}, bf16[160,1536]{1,0:T(8,128)(2,1)S(1)}, u32[]{:S(2)}, u32[]{:S(2)}) collective-permute-start(bf16[160,1536]{1,0:T(8,128)(2,1)S(1)} %shard_map.48.rest_1_), channel_id=1, source_target_pairs={{0,1},{1,2},{2,3},{3,4},{4,5},{5,6},{6,7},{7,8},{8,9},{9,10},{10,1... | collective-permute-start | bytes 1474568 | tf_op jit(solution)/shard_map/ppermute | solution.py:38
  19.1 2.3 %collective-permute-start.1 = (bf16[128,1536]{1,0:T(8,128)(2,1)S(1)}, bf16[128,1536]{1,0:T(8,128)(2,1)S(1)}, u32[]{:S(2)}, u32[]{:S(2)}) collective-permute-start(bf16[128,1536]{1,0:T(8,128)(2,1)S(1)} %shard_map.49.rest_1_), channel_id=1, source_target_pairs={{0,1},{1,2},{2,3},{3,4},{4,5},{5,6},{6,7},{7,8},{8,9},{9,10},{10,1... | collective-permute-start | bytes 1179656 | tf_op jit(solution)/shard_map/ppermute | solution.py:38
  22.8 3.1 %collective-permute-start.7 = (bf16[128,1536]{1,0:T(8,128)(2,1)S(1)}, bf16[128,1536]{1,0:T(8,128)(2,1)S(1)}, u32[]{:S(2)}, u32[]{:S(2)}) collective-permute-start(bf16[128,1536]{1,0:T(8,128)(2,1)S(1)} %shard_map.50.rest_1_), channel_id=1, source_target_pairs={{0,1},{1,2},{2,3},{3,4},{4,5},{5,6},{6,7},{7,8},{8,9},{9,10},{10,1... | collective-permute-start | bytes 1179656 | tf_op jit(solution)/shard_map/ppermute | solution.py:38
  25.9 1.7 %shard_map.51.rest_1_ = bf16[160,1536]{1,0:T(8,128)(2,1)S(1)} custom-call(bf16[512,1536]{1,0:T(8,128)(2,1)S(1)} %bitcast.7, bf16[2,1536,1536]{2,1,0:T(8,128)(2,1)S(1)} %get-tuple-element.39.w_ref, f32[8,1536]{1,0:T(8,128)S(1)} %get-tuple-element.40.p_ref, bf16[160,1536]{1,0:T(8,128)(2,1)S(1)} %collective-permute-done.2.rest_0_, ...), custom_call_target="tpu_custom_call" | custom-call | flops 4831838208 | tf_op jit(solution)/shard_map/pallas_call | solution.py:240
  27.7 3.6 %collective-permute-start.6 = (bf16[160,1536]{1,0:T(8,128)(2,1)S(1)}, bf16[160,1536]{1,0:T(8,128)(2,1)S(1)}, u32[]{:S(2)}, u32[]{:S(2)}) collective-permute-start(bf16[160,1536]{1,0:T(8,128)(2,1)S(1)} %shard_map.51.rest_1_), channel_id=1, source_target_pairs={{0,1},{1,2},{2,3},{3,4},{4,5},{5,6},{6,7},{7,8},{8,9},{9,10},{10,1... | collective-permute-start | bytes 1474568 | tf_op jit(solution)/shard_map/ppermute | solution.py:38
  32.7 2.5 %collective-permute-start.5 = (bf16[128,1536]{1,0:T(8,128)(2,1)S(1)}, bf16[128,1536]{1,0:T(8,128)(2,1)S(1)}, u32[]{:S(2)}, u32[]{:S(2)}) collective-permute-start(bf16[128,1536]{1,0:T(8,128)(2,1)S(1)} %get-tuple-element.42.rest_0_), channel_id=1, source_target_pairs={{0,1},{1,2},{2,3},{3,4},{4,5},{5,6},{6,7},{7,8},{8,9},{9,10},{10,1... | collective-permute-start | bytes 1179656 | tf_op jit(solution)/shard_map/ppermute | solution.py:38
  35.2 1.7 %shard_map.53.rest_1_ = bf16[96,1536]{1,0:T(8,128)(2,1)S(1)} custom-call(bf16[512,1536]{1,0:T(8,128)(2,1)S(1)} %bitcast.9, bf16[2,1536,1536]{2,1,0:T(8,128)(2,1)S(1)} %get-tuple-element.39.w_ref, f32[8,1536]{1,0:T(8,128)S(1)} %get-tuple-element.40.p_ref, bf16[128,1536]{1,0:T(8,128)(2,1)S(1)} %get-tuple-element.42.rest_0_), custom_call_target="tpu_custom_call" | custom-call | flops 4831838208 | tf_op jit(solution)/shard_map/pallas_call | solution.py:240
  36.9 2.1 %collective-permute-start.4 = (bf16[96,1536]{1,0:T(8,128)(2,1)S(1)}, bf16[96,1536]{1,0:T(8,128)(2,1)S(1)}, u32[]{:S(2)}, u32[]{:S(2)}) collective-permute-start(bf16[96,1536]{1,0:T(8,128)(2,1)S(1)} %shard_map.53.rest_1_), channel_id=1, source_target_pairs={{0,1},{1,2},{2,3},{3,4},{4,5},{5,6},{6,7},{7,8},{8,9},{9,10},{10,1... | collective-permute-start | bytes 884744 | tf_op jit(solution)/shard_map/ppermute | solution.py:38
  39.0 1.7 %shard_map.54 = (bf16[160,1536]{1,0:T(8,128)(2,1)S(1)}, f32[160,1536]{1,0:T(8,128)S(1)}) custom-call(bf16[512,1536]{1,0:T(8,128)(2,1)S(1)} %bitcast.10, bf16[2,1536,1536]{2,1,0:T(8,128)(2,1)S(1)} %get-tuple-element.39.w_ref, f32[8,1536]{1,0:T(8,128)S(1)} %get-tuple-element.40.p_ref, bf16[160,1536]{1,0:T(8,128)(2,1)S(1)} %collective-permute-done.6.rest_0_, ...), custom_call_target="tpu_custom_call" | custom-call | flops 4831838208 | tf_op jit(solution)/shard_map/pallas_call | solution.py:240
  42.0 4.4 %collective-permute-start.10 = (bf16[160,1536]{1,0:T(8,128)(2,1)S(1)}, bf16[160,1536]{1,0:T(8,128)(2,1)S(1)}, u32[]{:S(2)}, u32[]{:S(2)}) collective-permute-start(bf16[160,1536]{1,0:T(8,128)(2,1)S(1)} %get-tuple-element.44.rest_2_), channel_id=1, source_target_pairs={{15,13},{23,21}} | collective-permute-start | bytes 1474568 | tf_op jit(solution)/shard_map/ppermute | solution.py:38
  47.8 1.7 %shard_map.56.rest_1_ = bf16[96,1536]{1,0:T(8,128)(2,1)S(1)} custom-call(bf16[512,1536]{1,0:T(8,128)(2,1)S(1)} %bitcast.11, bf16[2,1536,1536]{2,1,0:T(8,128)(2,1)S(1)} %get-tuple-element.39.w_ref, f32[8,1536]{1,0:T(8,128)S(1)} %get-tuple-element.40.p_ref, bf16[96,1536]{1,0:T(8,128)(2,1)S(1)} %collective-permute-done.4.rest_0_, ...), custom_call_target="tpu_custom_call" | custom-call | flops 4831838208 | tf_op jit(solution)/shard_map/pallas_call | solution.py:240
  49.5 2.8 %collective-permute-start.8 = (bf16[96,1536]{1,0:T(8,128)(2,1)S(1)}, bf16[96,1536]{1,0:T(8,128)(2,1)S(1)}, u32[]{:S(2)}, u32[]{:S(2)}) collective-permute-start(bf16[96,1536]{1,0:T(8,128)(2,1)S(1)} %shard_map.56.rest_1_), channel_id=1, source_target_pairs={{0,1},{1,2},{2,3},{3,4},{4,5},{5,6},{6,7},{7,8},{8,9},{9,10},{10,1... | collective-permute-start | bytes 884744 | tf_op jit(solution)/shard_map/ppermute | solution.py:38
  53.7 1.9 %collective-permute-start.15 = (bf16[128,1536]{1,0:T(8,128)(2,1)S(1)}, bf16[128,1536]{1,0:T(8,128)(2,1)S(1)}, u32[]{:S(2)}, u32[]{:S(2)}) collective-permute-start(bf16[128,1536]{1,0:T(8,128)(2,1)S(1)} %get-tuple-element.48.rest_2_), channel_id=1, source_target_pairs={{0,1},{1,2},{2,3},{3,4},{4,5},{5,6},{6,7},{7,8},{8,9},{9,10},{10,1... | collective-permute-start | bytes 1179656 | tf_op jit(solution)/shard_map/ppermute | solution.py:38
  61.6 2.1 %collective-permute-start.12 = (bf16[96,1536]{1,0:T(8,128)(2,1)S(1)}, bf16[96,1536]{1,0:T(8,128)(2,1)S(1)}, u32[]{:S(2)}, u32[]{:S(2)}) collective-permute-start(bf16[96,1536]{1,0:T(8,128)(2,1)S(1)} %get-tuple-element.52.rest_2_), channel_id=1, source_target_pairs={{0,1},{1,2},{2,3},{3,4},{4,5},{5,6},{6,7},{7,8},{8,9},{9,10},{10,1... | collective-permute-start | bytes 884744 | tf_op jit(solution)/shard_map/ppermute | solution.py:38
  65.1 12.8 %collective-permute-done.14.rest_3_ = bf16[160,1536]{1,0:T(8,128)(2,1)S(1)} collective-permute-done((bf16[160,1536]{1,0:T(8,128)(2,1)S(1)}, bf16[160,1536]{1,0:T(8,128)(2,1)S(1)}, u32[]{:S(2)}, u32[]{:S(2)}) %collective-permute-start.14) | collective-permute-done | bytes 491552 | tf_op jit(solution)/shard_map/ppermute | solution.py:38
  81.7 2.5 %shard_map.65 = (bf16[2,512,1536]{2,1,0:T(8,128)(2,1)}, f32[8,128]{1,0:T(8,128)S(1)}) custom-call(bf16[512,1536]{1,0:T(8,128)(2,1)S(1)} %bitcast.14, bf16[2,1536,1536]{2,1,0:T(8,128)(2,1)S(1)} %get-tuple-element.39.w_ref, f32[8,1536]{1,0:T(8,128)S(1)} %get-tuple-element.40.p_ref, bf16[128,1536]{1,0:T(8,128)(2,1)S(1)} %collective-permute-done.16.rest_3_.moved_ref, ...), custom_call_target="tpu_custom_call" | custom-call | flops 4831838208 | tf_op jit(solution)/shard_map/pallas_call | solution.py:240
  84.2 5.5 %collective-permute-done.18.rest_2_ = bf16[128,1536]{1,0:T(8,128)(2,1)S(1)} collective-permute-done((bf16[128,1536]{1,0:T(8,128)(2,1)S(1)}, bf16[128,1536]{1,0:T(8,128)(2,1)S(1)}, u32[]{:S(2)}, u32[]{:S(2)}) %collective-permute-start.18) | collective-permute-done | bytes 393248 | tf_op jit(solution)/shard_map/ppermute | solution.py:38
  95.2 2.6 %shard_map.68 = (bf16[2,512,1536]{2,1,0:T(8,128)(2,1)}, f32[8,128]{1,0:T(8,128)S(1)}) custom-call(bf16[512,1536]{1,0:T(8,128)(2,1)S(1)} %bitcast.15, bf16[2,1536,1536]{2,1,0:T(8,128)(2,1)S(1)} %get-tuple-element.39.w_ref, f32[8,1536]{1,0:T(8,128)S(1)} %get-tuple-element.40.p_ref, ...), custom_call_target="tpu_custom_call", output_to_operand_aliasing={{0}: (8, {})} | custom-call | flops 4831838208 | tf_op jit(solution)/shard_map/pallas_call | solution.py:240
  98.0 2.3 %shard_map.69 = (bf16[2,512,1536]{2,1,0:T(8,128)(2,1)}, f32[8,128]{1,0:T(8,128)S(1)}) custom-call(bf16[512,1536]{1,0:T(8,128)(2,1)S(1)} %bitcast.16, bf16[2,1536,1536]{2,1,0:T(8,128)(2,1)S(1)} %get-tuple-element.39.w_ref, f32[8,1536]{1,0:T(8,128)S(1)} %get-tuple-element.40.p_ref, ...), custom_call_target="tpu_custom_call", output_to_operand_aliasing={{0}: (7, {})} | custom-call | flops 4831838208 | tf_op jit(solution)/shard_map/pallas_call | solution.py:240
  101.2 3.0 %shard_map.70 = (bf16[2,512,1536]{2,1,0:T(8,128)(2,1)}, f32[8,128]{1,0:T(8,128)}) custom-call(bf16[512,1536]{1,0:T(8,128)(2,1)S(1)} %bitcast.17, bf16[2,1536,1536]{2,1,0:T(8,128)(2,1)S(1)} %get-tuple-element.39.w_ref, f32[8,1536]{1,0:T(8,128)S(1)} %get-tuple-element.40.p_ref, ...), custom_call_target="tpu_custom_call", output_to_operand_aliasing={{0}: (7, {})} | custom-call | flops 4831838208 | tf_op jit(solution)/shard_map/pallas_call | solution.py:240
  (47 shorter events, 27.2 us)
Async XLA Ops:
  0.0 9.0 %copy-start = (bf16[2,256,1536]{2,1,0:T(8,128)(2,1)S(1)}, bf16[2,256,1536]{2,1,0:T(8,128)(2,1)}, u32[]{:S(2)}) copy-start(bf16[2,256,1536]{2,1,0:T(8,128)(2,1)} %param.4) | copy-start | bytes 4718596
  5.3 12.3 %collective-permute-start = (bf16[128,1536]{1,0:T(8,128)(2,1)S(1)}, bf16[128,1536]{1,0:T(8,128)(2,1)S(1)}, u32[]{:S(2)}, u32[]{:S(2)}) collective-permute-start(bf16[128,1536]{1,0:T(8,128)(2,1)S(1)} %get-tuple-element.41.rest_0_), channel_id=1, source_target_pairs={{0,1},{1,2},{2,3},{3,4},{4,5},{5,6},{6,7},{7,8},{8,9},{9,10},{10,1... | collective-permute-start | bytes 1179656 | tf_op jit(solution)/shard_map/ppermute | solution.py:38
  10.4 10.9 %collective-permute-start.3 = (bf16[128,1536]{1,0:T(8,128)(2,1)S(1)}, bf16[128,1536]{1,0:T(8,128)(2,1)S(1)}, u32[]{:S(2)}, u32[]{:S(2)}) collective-permute-start(bf16[128,1536]{1,0:T(8,128)(2,1)S(1)} %shard_map.47.rest_0_), channel_id=1, source_target_pairs={{0,1},{1,2},{2,3},{3,4},{4,5},{5,6},{6,7},{7,8},{8,9},{9,10},{10,1... | collective-permute-start | bytes 1179656 | tf_op jit(solution)/shard_map/ppermute | solution.py:38
  14.1 11.8 %collective-permute-start.2 = (bf16[160,1536]{1,0:T(8,128)(2,1)S(1)}, bf16[160,1536]{1,0:T(8,128)(2,1)S(1)}, u32[]{:S(2)}, u32[]{:S(2)}) collective-permute-start(bf16[160,1536]{1,0:T(8,128)(2,1)S(1)} %shard_map.48.rest_1_), channel_id=1, source_target_pairs={{0,1},{1,2},{2,3},{3,4},{4,5},{5,6},{6,7},{7,8},{8,9},{9,10},{10,1... | collective-permute-start | bytes 1474568 | tf_op jit(solution)/shard_map/ppermute | solution.py:38
  19.1 12.2 %collective-permute-start.1 = (bf16[128,1536]{1,0:T(8,128)(2,1)S(1)}, bf16[128,1536]{1,0:T(8,128)(2,1)S(1)}, u32[]{:S(2)}, u32[]{:S(2)}) collective-permute-start(bf16[128,1536]{1,0:T(8,128)(2,1)S(1)} %shard_map.49.rest_1_), channel_id=1, source_target_pairs={{0,1},{1,2},{2,3},{3,4},{4,5},{5,6},{6,7},{7,8},{8,9},{9,10},{10,1... | collective-permute-start | bytes 1179656 | tf_op jit(solution)/shard_map/ppermute | solution.py:38
  22.8 16.2 %collective-permute-start.7 = (bf16[128,1536]{1,0:T(8,128)(2,1)S(1)}, bf16[128,1536]{1,0:T(8,128)(2,1)S(1)}, u32[]{:S(2)}, u32[]{:S(2)}) collective-permute-start(bf16[128,1536]{1,0:T(8,128)(2,1)S(1)} %shard_map.50.rest_1_), channel_id=1, source_target_pairs={{0,1},{1,2},{2,3},{3,4},{4,5},{5,6},{6,7},{7,8},{8,9},{9,10},{10,1... | collective-permute-start | bytes 1179656 | tf_op jit(solution)/shard_map/ppermute | solution.py:38
  27.7 11.3 %collective-permute-start.6 = (bf16[160,1536]{1,0:T(8,128)(2,1)S(1)}, bf16[160,1536]{1,0:T(8,128)(2,1)S(1)}, u32[]{:S(2)}, u32[]{:S(2)}) collective-permute-start(bf16[160,1536]{1,0:T(8,128)(2,1)S(1)} %shard_map.51.rest_1_), channel_id=1, source_target_pairs={{0,1},{1,2},{2,3},{3,4},{4,5},{5,6},{6,7},{7,8},{8,9},{9,10},{10,1... | collective-permute-start | bytes 1474568 | tf_op jit(solution)/shard_map/ppermute | solution.py:38
  32.7 13.7 %collective-permute-start.5 = (bf16[128,1536]{1,0:T(8,128)(2,1)S(1)}, bf16[128,1536]{1,0:T(8,128)(2,1)S(1)}, u32[]{:S(2)}, u32[]{:S(2)}) collective-permute-start(bf16[128,1536]{1,0:T(8,128)(2,1)S(1)} %get-tuple-element.42.rest_0_), channel_id=1, source_target_pairs={{0,1},{1,2},{2,3},{3,4},{4,5},{5,6},{6,7},{7,8},{8,9},{9,10},{10,1... | collective-permute-start | bytes 1179656 | tf_op jit(solution)/shard_map/ppermute | solution.py:38
  36.9 10.9 %collective-permute-start.4 = (bf16[96,1536]{1,0:T(8,128)(2,1)S(1)}, bf16[96,1536]{1,0:T(8,128)(2,1)S(1)}, u32[]{:S(2)}, u32[]{:S(2)}) collective-permute-start(bf16[96,1536]{1,0:T(8,128)(2,1)S(1)} %shard_map.53.rest_1_), channel_id=1, source_target_pairs={{0,1},{1,2},{2,3},{3,4},{4,5},{5,6},{6,7},{7,8},{8,9},{9,10},{10,1... | collective-permute-start | bytes 884744 | tf_op jit(solution)/shard_map/ppermute | solution.py:38
  40.7 14.9 %collective-permute-start.11 = (bf16[160,1536]{1,0:T(8,128)(2,1)S(1)}, bf16[160,1536]{1,0:T(8,128)(2,1)S(1)}, u32[]{:S(2)}, u32[]{:S(2)}) collective-permute-start(bf16[160,1536]{1,0:T(8,128)(2,1)S(1)} %get-tuple-element.44.rest_2_), channel_id=1, source_target_pairs={{0,1},{1,2},{2,3},{3,4},{4,5},{5,6},{6,7},{7,8},{8,9},{9,10},{10,1... | collective-permute-start | bytes 1474568 | tf_op jit(solution)/shard_map/ppermute | solution.py:38
  42.0 15.0 %collective-permute-start.10 = (bf16[160,1536]{1,0:T(8,128)(2,1)S(1)}, bf16[160,1536]{1,0:T(8,128)(2,1)S(1)}, u32[]{:S(2)}, u32[]{:S(2)}) collective-permute-start(bf16[160,1536]{1,0:T(8,128)(2,1)S(1)} %get-tuple-element.44.rest_2_), channel_id=1, source_target_pairs={{15,13},{23,21}} | collective-permute-start | bytes 1474568 | tf_op jit(solution)/shard_map/ppermute | solution.py:38
  46.5 11.3 %collective-permute-start.9 = (bf16[128,1536]{1,0:T(8,128)(2,1)S(1)}, bf16[128,1536]{1,0:T(8,128)(2,1)S(1)}, u32[]{:S(2)}, u32[]{:S(2)}) collective-permute-start(bf16[128,1536]{1,0:T(8,128)(2,1)S(1)} %get-tuple-element.45.rest_1_), channel_id=1, source_target_pairs={{8,16},{9,17},{10,18},{11,19},{12,20},{13,21},{14,22},{15,23}} | collective-permute-start | bytes 1179656 | tf_op jit(solution)/shard_map/ppermute | solution.py:38
  49.5 10.5 %collective-permute-start.8 = (bf16[96,1536]{1,0:T(8,128)(2,1)S(1)}, bf16[96,1536]{1,0:T(8,128)(2,1)S(1)}, u32[]{:S(2)}, u32[]{:S(2)}) collective-permute-start(bf16[96,1536]{1,0:T(8,128)(2,1)S(1)} %shard_map.56.rest_1_), channel_id=1, source_target_pairs={{0,1},{1,2},{2,3},{3,4},{4,5},{5,6},{6,7},{7,8},{8,9},{9,10},{10,1... | collective-permute-start | bytes 884744 | tf_op jit(solution)/shard_map/ppermute | solution.py:38
  53.7 10.1 %collective-permute-start.15 = (bf16[128,1536]{1,0:T(8,128)(2,1)S(1)}, bf16[128,1536]{1,0:T(8,128)(2,1)S(1)}, u32[]{:S(2)}, u32[]{:S(2)}) collective-permute-start(bf16[128,1536]{1,0:T(8,128)(2,1)S(1)} %get-tuple-element.48.rest_2_), channel_id=1, source_target_pairs={{0,1},{1,2},{2,3},{3,4},{4,5},{5,6},{6,7},{7,8},{8,9},{9,10},{10,1... | collective-permute-start | bytes 1179656 | tf_op jit(solution)/shard_map/ppermute | solution.py:38
  55.7 22.3 %collective-permute-start.14 = (bf16[160,1536]{1,0:T(8,128)(2,1)S(1)}, bf16[160,1536]{1,0:T(8,128)(2,1)S(1)}, u32[]{:S(2)}, u32[]{:S(2)}) collective-permute-start(bf16[160,1536]{1,0:T(8,128)(2,1)S(1)} %get-tuple-element.49.rest_0_), channel_id=1, source_target_pairs={{8,16},{9,17},{10,18},{11,19},{12,20},{13,21},{14,22},{15,23}} | collective-permute-start | bytes 1474568 | tf_op jit(solution)/shard_map/ppermute | solution.py:38
  57.0 8.1 %collective-permute-start.13 = (bf16[160,1536]{1,0:T(8,128)(2,1)S(1)}, bf16[160,1536]{1,0:T(8,128)(2,1)S(1)}, u32[]{:S(2)}, u32[]{:S(2)}) collective-permute-start(bf16[160,1536]{1,0:T(8,128)(2,1)S(1)} %shard_map.59.rest_4_), channel_id=1, source_target_pairs={{13,16},{21,24}} | collective-permute-start | bytes 1474568 | tf_op jit(solution)/shard_map/ppermute | solution.py:38
  58.6 21.8 %collective-permute-start.16 = (bf16[128,1536]{1,0:T(8,128)(2,1)S(1)}, bf16[128,1536]{1,0:T(8,128)(2,1)S(1)}, u32[]{:S(2)}, u32[]{:S(2)}) collective-permute-start(bf16[128,1536]{1,0:T(8,128)(2,1)S(1)} %get-tuple-element.50.rest_1_), channel_id=1, source_target_pairs={{16,24},{17,25},{18,26},{19,27},{20,28},{21,29},{22,30},{23,31}} | collective-permute-start | bytes 1179656 | tf_op jit(solution)/shard_map/ppermute | solution.py:38
  61.6 18.7 %collective-permute-start.12 = (bf16[96,1536]{1,0:T(8,128)(2,1)S(1)}, bf16[96,1536]{1,0:T(8,128)(2,1)S(1)}, u32[]{:S(2)}, u32[]{:S(2)}) collective-permute-start(bf16[96,1536]{1,0:T(8,128)(2,1)S(1)} %get-tuple-element.52.rest_2_), channel_id=1, source_target_pairs={{0,1},{1,2},{2,3},{3,4},{4,5},{5,6},{6,7},{7,8},{8,9},{9,10},{10,1... | collective-permute-start | bytes 884744 | tf_op jit(solution)/shard_map/ppermute | solution.py:38
  63.8 25.9 %collective-permute-start.18 = (bf16[128,1536]{1,0:T(8,128)(2,1)S(1)}, bf16[128,1536]{1,0:T(8,128)(2,1)S(1)}, u32[]{:S(2)}, u32[]{:S(2)}) collective-permute-start(bf16[128,1536]{1,0:T(8,128)(2,1)S(1)} %get-tuple-element.55.rest_5_), channel_id=1, source_target_pairs={{8,16},{9,17},{10,18},{11,19},{12,20},{13,21},{14,22},{15,23}} | collective-permute-start | bytes 1179656 | tf_op jit(solution)/shard_map/ppermute | solution.py:38
  79.1 13.9 %collective-permute-start.19 = (bf16[160,1536]{1,0:T(8,128)(2,1)S(1)}, bf16[160,1536]{1,0:T(8,128)(2,1)S(1)}, u32[]{:S(2)}, u32[]{:S(2)}) collective-permute-start(bf16[160,1536]{1,0:T(8,128)(2,1)S(1)} %get-tuple-element.56.rest_2_), channel_id=1, source_target_pairs={{16,24},{17,25},{18,26},{19,27},{20,28},{21,29},{22,30},{23,31}} | collective-permute-start | bytes 1474568 | tf_op jit(solution)/shard_map/ppermute | solution.py:38
  80.4 12.5 %collective-permute-start.17 = (bf16[96,1536]{1,0:T(8,128)(2,1)S(1)}, bf16[96,1536]{1,0:T(8,128)(2,1)S(1)}, u32[]{:S(2)}, u32[]{:S(2)}) collective-permute-start(bf16[96,1536]{1,0:T(8,128)(2,1)S(1)} %get-tuple-element.57.rest_2_), channel_id=1, source_target_pairs={{8,16},{9,17},{10,18},{11,19},{12,20},{13,21},{14,22},{15,23}} | collective-permute-start | bytes 884744 | tf_op jit(solution)/shard_map/ppermute | solution.py:38
  90.6 7.4 %collective-permute-start.21 = (bf16[128,1536]{1,0:T(8,128)(2,1)S(1)}, bf16[128,1536]{1,0:T(8,128)(2,1)S(1)}, u32[]{:S(2)}, u32[]{:S(2)}) collective-permute-start(bf16[128,1536]{1,0:T(8,128)(2,1)S(1)} %get-tuple-element.62.rest_4_), channel_id=1, source_target_pairs={{16,24},{17,25},{18,26},{19,27},{20,28},{21,29},{22,30},{23,31}} | collective-permute-start | bytes 1179656 | tf_op jit(solution)/shard_map/ppermute | solution.py:38
  93.8 7.3 %collective-permute-start.20 = (bf16[96,1536]{1,0:T(8,128)(2,1)S(1)}, bf16[96,1536]{1,0:T(8,128)(2,1)S(1)}, u32[]{:S(2)}, u32[]{:S(2)}) collective-permute-start(bf16[96,1536]{1,0:T(8,128)(2,1)S(1)} %get-tuple-element.63.rest_4_), channel_id=1, source_target_pairs={{16,24},{17,25},{18,26},{19,27},{20,28},{21,29},{22,30},{23,31}} | collective-permute-start | bytes 884744 | tf_op jit(solution)/shard_map/ppermute | solution.py:38

commit v4 on v3

--- a/solution.py
+++ b/solution.py
@@ -10,12 +10,15 @@
 LAY_DEV = 2
 INTERVAL = 8
 
-SHARES = (4, 5, 4, 3)
+SHARES = (5, 4, 4, 3)
 ORDER = (
-    0, 20, 10, 1, 21, 11, 2, 30, 12, 3, 31, 22, 13, 17, 4, 32, 23, 14, 33, 5, 24, 34, 15, 25, 35,
+    0, 20, 10, 1, 21, 11, 2, 30, 12, 3, 31, 22, 13, 4, 23, 28, 32, 14, 5, 24, 33, 15, 34, 25, 35,
 )
-RELAYS = {8: (0, 2), 6: (1, 6), 7: (2, 2)}
+RELAYS = {7: 2, 8: 4}
+APART = ()
+UNDERWAY = 5
 TILE = 512
+ROWS_AT_ONCE = 128
 VMEM_BYTES = 20 << 20
 VMEM = pl.BlockSpec(memory_space=pltpu.VMEM)
 ANY = pl.BlockSpec(memory_space=pl.ANY)
@@ -43,13 +46,13 @@
     return [slice(low, low + tile) for low in range(0, width, tile)]
 
 
-def bend(state, w_ref, p_ref, layer, cols):
+def bend(state, size, w_ref, p_ref, layer, cols):
     pre = jnp.dot(state, w_ref[layer, :, cols], preferred_element_type=jnp.float32)
-    return jnp.tanh(pre + p_ref[layer : layer + 1, cols])
+    return jnp.tanh(pre[:size] + p_ref[layer : layer + 1, cols])
 
 
 def opening_kernel(rows, start_hbm, w_hbm, b_hbm, h_hbm, out_ref, w_ref, p_ref, start, state, rounded, b_ref, h_ref, w_sems, sems):
-    width = w_hbm.shape[2]
+    width, size = w_hbm.shape[2], out_ref.shape[0]
     small = [
         pltpu.make_async_copy(start_hbm.at[rows, :], start, sems.at[0]),
         pltpu.make_async_copy(b_hbm, b_ref, sems.at[1]),
@@ -73,12 +76,12 @@
     p_ref[4:8, :] = jnp.zeros((4, width), jnp.float32)
     for index, cols in enumerate(tiles(width)):
         copies[index].wait()
-        moved = start[:, cols].astype(jnp.float32) + p_ref[2:3, cols] * bend(start[...], w_ref, p_ref, 0, cols)
+        moved = start[:, cols].astype(jnp.float32) + p_ref[2:3, cols] * bend(start[...], size, w_ref, p_ref, 0, cols)
         state[:, cols] = moved
         rounded[:, cols] = moved.astype(jnp.bfloat16)
     for index, cols in enumerate(tiles(width)):
         copies[len(tiles(width)) + index].wait()
-        bent = bend(rounded[...], w_ref, p_ref, 1, cols)
+        bent = bend(rounded[...], size, w_ref, p_ref, 1, cols)
         out_ref[:, cols] = (state[:, cols] + p_ref[3:4, cols] * bent).astype(jnp.bfloat16)
 
 
@@ -88,25 +91,26 @@
 
 def pass_kernel(rows, parts, keep, extra, start_ref, w_ref, p_ref, *rest):
     arrived, rest = rest[:parts], rest[parts + extra :]
+    t_ref = None
+    if keep:
+        out_ref, t_ref, entering, state, rounded = rest
+    else:
+        out_ref, entering, state, rounded = rest
+    size = out_ref.shape[0]
     if parts:
-        if keep:
-            out_ref, t_ref, entering, state, rounded = rest
-        else:
-            out_ref, entering, state, rounded = rest
         came = total_of(arrived).astype(jnp.bfloat16) if parts > 1 else arrived[0][...]
-        entering[...] = jnp.where(lax.axis_index("depth") == 0, start_ref[rows, :], came)
+        entering[:size] = jnp.where(lax.axis_index("depth") == 0, start_ref[rows, :], came)
     else:
-        out_ref, state, rounded = rest
-        entering = start_ref.at[rows, :]
+        entering[:size] = start_ref[rows, :]
     for cols in tiles(w_ref.shape[2]):
-        bent = bend(entering[...], w_ref, p_ref, 0, cols)
+        bent = bend(entering[...], size, w_ref, p_ref, 0, cols)
         if keep:
             t_ref[:, cols] = bent
-        moved = entering[:, cols].astype(jnp.float32) + p_ref[2:3, cols] * bent
+        moved = entering[:size, cols].astype(jnp.float32) + p_ref[2:3, cols] * bent
         state[:, cols] = moved
-        rounded[:, cols] = moved.astype(jnp.bfloat16)
+        rounded[:size, cols] = moved.astype(jnp.bfloat16)
     for cols in tiles(w_ref.shape[2]):
-        bent = bend(rounded[...], w_ref, p_ref, 1, cols)
+        bent = bend(rounded[...], size, w_ref, p_ref, 1, cols)
         out_ref[:, cols] = (state[:, cols] + p_ref[3:4, cols] * bent).astype(jnp.bfloat16)
 
 
@@ -146,9 +150,10 @@
         entry = total_of(entry_refs)
         correction = correction_of(entry, total_of(fresh_refs), moved_ref)
         correction_ref[...] = correction
-        rounded[...] = (entry + correction.astype(jnp.float32)).astype(jnp.bfloat16)
+        size = out_ref.shape[0]
+        rounded[:size] = (entry + correction.astype(jnp.float32)).astype(jnp.bfloat16)
         for cols in tiles(w_ref.shape[2]):
-            bent = bend(rounded[...], w_ref, p_ref, 0, cols)
+            bent = bend(rounded[...], size, w_ref, p_ref, 0, cols)
             change = (INTERVAL * LAY_DEV) * p_ref[2:3, cols] * (bent - t_ref[:, cols])
             out_ref[:, cols] = (correction_ref[:, cols].astype(jnp.float32) + change).astype(jnp.bfloat16)
 
@@ -177,23 +182,30 @@
     def _():
         state[...] = entry + correction_of(entry, total_of(fresh_refs), moved_ref).astype(jnp.float32)
 
-    second[...] = state[...].astype(jnp.bfloat16)
+    size = state.shape[0]
+    second[:size] = state[...].astype(jnp.bfloat16)
     copies = []
-    for cols in tiles(width):
-        moved = state[:, cols] + p_ref[2:3, cols] * bend(second[...], w_ref, p_ref, 0, cols)
-        state[:, cols] = moved
-        first[:, cols] = moved.astype(jnp.bfloat16)
-        copy = pltpu.make_async_copy(first.at[:, cols], states.at[0, rows, cols], sems.at[len(copies)])
+
+    def written(ref, layer, cols):
+        copy = pltpu.make_async_copy(ref.at[:size, cols], states.at[layer, rows, cols], sems.at[len(copies)])
         copy.start()
         copies.append(copy)
+
     for cols in tiles(width):
-        bent = bend(first[...], w_ref, p_ref, 1, cols)
-        second[:, cols] = (state[:, cols] + p_ref[3:4, cols] * bent).astype(jnp.bfloat16)
-        copy = pltpu.make_async_copy(second.at[:, cols], states.at[1, rows, cols], sems.at[len(copies)])
-        copy.start()
-        copies.append(copy)
+        moved = state[:, cols] + p_ref[2:3, cols] * bend(second[...], size, w_ref, p_ref, 0, cols)
+        state[:, cols] = moved
+        first[:size, cols] = moved.astype(jnp.bfloat16)
+        written(first, 0, cols)
+    for cols in tiles(width):
+        bent = bend(first[...], size, w_ref, p_ref, 1, cols)
+        second[:size, cols] = (state[:, cols] + p_ref[3:4, cols] * bent).astype(jnp.bfloat16)
+        written(second, 1, cols)
     for copy in copies:
         copy.wait()
+
+
+def room_of(size):
+    return ROWS_AT_ONCE if ROWS_AT_ONCE // 2 < size < ROWS_AT_ONCE else size
 
 
 def order_of(groups):
@@ -265,48 +277,44 @@
     chunks = len(SHARES)
     bent, correction, moved = [None] * chunks, [None] * chunks, [None] * chunks
     arrived = [[] for _ in range(chunks)]
-    asides, underway = {}, []
-    relayed = {(item // 10, RELAYS[item % 10][0]): item % 10 for item in ORDER if item % 10 in RELAYS}
+    asides = {}
+    back = {item // 10: RELAYS[item % 10] for item in ORDER if item % 10 in RELAYS}
+    underway = []
 
     def sent(value, pairs):
         underway.append(passed_along(value, pairs))
         return underway[-1]
 
+    def waited(values, sends):
+        underway[:] = [other for other in underway if not any(other is value for value in values)]
+        surplus = max(0, len(underway) + sends - UNDERWAY)
+        oldest, underway[:] = underway[:surplus], underway[surplus:]
+        return oldest
+
     def passed(value, chunk, step):
-        kind = relayed.get((chunk, step))
-        if kind is None:
+        if step == 2 and chunk in back:
+            arrived[chunk].append([sent(value, straight)])
+            asides[chunk] = sent(value, [(end, end - back[chunk]) for end in ends])
+        elif step == 2 and chunk in APART:
+            arrived[chunk].append([sent(value, straight), sent(value, [(end, end + 1) for end in ends])])
+        else:
             arrived[chunk].append([sent(value, one_on)])
-        else:
-            back = RELAYS[kind][1]
-            arrived[chunk].append([sent(value, straight)])
-            asides[chunk, step] = sent(value, [(end, end - back) for end in ends])
-
-    def earlier(values):
-        found = []
-        for value in values:
-            if any(value is other for other in underway):
-                while True:
-                    oldest = underway.pop(0)
-                    if oldest is value:
-                        break
-                    found.append(oldest)
-        return [other for other in found if not any(other is value for value in values)]
 
     passed(leaving, 0, 0)
     after, states = [leaving], None
     for kind, chunk, step in order_of(groups)[1:]:
         size = sizes[chunk]
         wide = pltpu.VMEM((size, width), jnp.float32)
-        thin = pltpu.VMEM((size, width), jnp.bfloat16)
+        thin = pltpu.VMEM((room_of(size), width), jnp.bfloat16)
         if kind == "pass":
             keep = step == 2
             came = arrived[chunk][step - 1] if step else []
-            extra = after + earlier(came)
+            after += waited(came, 2 if keep and (chunk in back or chunk in APART) else 1)
             result = call(
-                functools.partial(pass_kernel, spans[chunk], len(came), keep, len(extra)),
+                functools.partial(pass_kernel, spans[chunk], len(came), keep, len(after)),
                 (narrow(size), kept((size, width), jnp.float32)) if keep else narrow(size),
-                [thin, wide, thin] if step else [wide, thin],
-                [start, w, p] + came + extra,
+                [thin, wide, thin],
+                [start, w, p] + came + after,
             )
             if keep:
                 leaving, bent[chunk] = result
@@ -315,35 +323,32 @@
             passed(leaving, chunk, step)
             after = [leaving]
         elif kind == "relay":
-            step, back = RELAYS[step]
-            came = asides[chunk, step]
-            extra = after + earlier([came])
+            came = [asides[chunk]]
+            after += waited(came, 1)
             leaving = call(
-                functools.partial(relay_kernel, INTERVAL - 1 - back, len(extra)), narrow(size), [], [came] + extra
-            )
-            arrived[chunk][step].append(sent(leaving, [(end - back, end + 1) for end in ends]))
+                functools.partial(relay_kernel, INTERVAL - 1 - back[chunk], len(after)), narrow(size), [], came + after
+            )
+            arrived[chunk][2].append(sent(leaving, [(end - back[chunk], end + 1) for end in ends]))
             after = [leaving]
         elif kind == "coarse":
             _, entry, fresh = arrived[chunk]
             if step == 1:
                 fresh = fresh[:1]
             operands = [bent[chunk], w, p] + entry + fresh
-            needed = entry + fresh
             if step > 1:
                 operands += [moved[chunk], correction[chunk]]
-                needed = needed + [moved[chunk]]
-            extra = after + earlier(needed)
+            after += waited(operands, 1)
             delta, correction[chunk] = call(
-                functools.partial(coarse_kernel, step, len(extra), (len(entry), len(fresh))),
-                (narrow(size), narrow(size)), [thin], operands + extra,
+                functools.partial(coarse_kernel, step, len(after), (len(entry), len(fresh))),
+                (narrow(size), narrow(size)), [thin], operands + after,
             )
             ahead = [(source, source + INTERVAL) for source in range(step * INTERVAL, (step + 1) * INTERVAL)]
             moved[chunk] = sent(delta, ahead)
             after = [delta]
         else:
             _, entry, fresh = arrived[chunk]
-            extra = after + earlier([moved[chunk]])
             operands = [start, w, p, moved[chunk], correction[chunk]] + entry + fresh
+            waited(operands, 0)
             specs = [VMEM] * len(operands)
             aliases = None
             if states is not None:
@@ -352,11 +357,11 @@
                 specs.append(ANY)
             states, token = call(
                 functools.partial(
-                    final_kernel, spans[chunk], groups, states is not None, len(extra), (len(entry), len(fresh))
+                    final_kernel, spans[chunk], groups, states is not None, len(after), (len(entry), len(fresh))
                 ),
                 (jax.ShapeDtypeStruct((LAY_DEV, total, width), jnp.bfloat16), kept((8, 128), jnp.float32)),
                 [wide, thin, thin, DMA((LAY_DEV * parts,))],
-                operands + extra, specs + [VMEM] * len(extra), (ANY, VMEM), aliases,
+                operands + after, specs + [VMEM] * len(after), (ANY, VMEM), aliases,
             )
             after = [token]
     return states.reshape(LAY_DEV, initial.shape[0], -1, width)

time: 106 us -> 107 us (level)
  starting transfers between devices: 46.4 us -> 48.8 us
    ppermute x22, starting transfers between devices: 46.4 us -> 48.8 us  [passed_along(): return lax.ppermute(value, 'depth', pairs)]
  transfers between devices with their start and end apart: 22 -> 22, of which waited for: 5 -> 6; matrix products, arithmetic and copies ran while one was open for 0% -> 0% of each run, Pallas kernels for 27% -> 26%
where the time goes in v4:
time: 107 us; the launch traced here: 105 us
  starting transfers between devices  48.8 us (46%)
  Pallas kernels  35.8 us (33%)
  waiting for transfers between devices  19.6 us (18%)
    ppermute x22, starting transfers between devices, passed_along(): return lax.ppermute(value, 'depth', pairs)  48.8 us
    pallas_call x25, Pallas kernels, call(): pl.pallas_call(body, out_shape=outs, in_specs=specs, out_specs=out_specs...  35.8 us
    ppermute x22, waiting for transfers between devices, passed_along(): return lax.ppermute(value, 'depth', pairs)  19.6 us
  transfers between devices with their start and end apart: 22, of which 6 were waited for; matrix products, arithmetic and copies ran while one was open for 0% of the time, Pallas kernels for 26%

profile of v4, /device:TPU:23, one launch (start us, length us, event | category | flops | bytes accessed | tf_op | source)
XLA Modules:
  0.0 105.0 jit_solution(5343635066831744538)
XLA Ops:
  0.0 5.6 %shard_map.46 = (bf16[160,1536]{1,0:T(8,128)(2,1)S(1)}, bf16[2,1536,1536]{2,1,0:T(8,128)(2,1)S(1)}, f32[8,1536]{1,0:T(8,128)S(1)}) custom-call(bf16[512,1536]{1,0:T(8,128)(2,1)} %bitcast.2, bf16[2,1536,1536]{2,1,0:T(8,128)(2,1)} %w_hbm.1, f32[2,1536]{1,0:T(2,128)} %b_hbm.1, f32[2]{0:T(128)} %h_hbm.1), custom_call_target="tpu_custom_call" | custom-call | flops 4831838208 | tf_op jit(solution)/shard_map/pallas_call | solution.py:252
  5.7 3.7 %collective-permute-start = (bf16[160,1536]{1,0:T(8,128)(2,1)S(1)}, bf16[160,1536]{1,0:T(8,128)(2,1)S(1)}, u32[]{:S(2)}, u32[]{:S(2)}) collective-permute-start(bf16[160,1536]{1,0:T(8,128)(2,1)S(1)} %get-tuple-element.41.rest_0_), channel_id=1, source_target_pairs={{0,1},{1,2},{2,3},{3,4},{4,5},{5,6},{6,7},{7,8},{8,9},{9,10},{10,1... | collective-permute-start | bytes 1474568 | tf_op jit(solution)/shard_map/ppermute | solution.py:41
  10.8 1.9 %collective-permute-start.3 = (bf16[128,1536]{1,0:T(8,128)(2,1)S(1)}, bf16[128,1536]{1,0:T(8,128)(2,1)S(1)}, u32[]{:S(2)}, u32[]{:S(2)}) collective-permute-start(bf16[128,1536]{1,0:T(8,128)(2,1)S(1)} %shard_map.47.rest_0_), channel_id=1, source_target_pairs={{0,1},{1,2},{2,3},{3,4},{4,5},{5,6},{6,7},{7,8},{8,9},{9,10},{10,1... | collective-permute-start | bytes 1179656 | tf_op jit(solution)/shard_map/ppermute | solution.py:41
  14.2 3.5 %collective-permute-start.2 = (bf16[128,1536]{1,0:T(8,128)(2,1)S(1)}, bf16[128,1536]{1,0:T(8,128)(2,1)S(1)}, u32[]{:S(2)}, u32[]{:S(2)}) collective-permute-start(bf16[128,1536]{1,0:T(8,128)(2,1)S(1)} %shard_map.48.rest_1_), channel_id=1, source_target_pairs={{0,1},{1,2},{2,3},{3,4},{4,5},{5,6},{6,7},{7,8},{8,9},{9,10},{10,1... | collective-permute-start | bytes 1179656 | tf_op jit(solution)/shard_map/ppermute | solution.py:41
  17.7 1.7 %shard_map.49.rest_1_ = bf16[160,1536]{1,0:T(8,128)(2,1)S(1)} custom-call(bf16[512,1536]{1,0:T(8,128)(2,1)S(1)} %bitcast.5, bf16[2,1536,1536]{2,1,0:T(8,128)(2,1)S(1)} %get-tuple-element.39.w_ref, f32[8,1536]{1,0:T(8,128)S(1)} %get-tuple-element.40.p_ref, bf16[160,1536]{1,0:T(8,128)(2,1)S(1)} %collective-permute-done.rest_0_, ...), custom_call_target="tpu_custom_call" | custom-call | flops 4831838208 | tf_op jit(solution)/shard_map/pallas_call | solution.py:252
  19.4 3.6 %collective-permute-start.1 = (bf16[160,1536]{1,0:T(8,128)(2,1)S(1)}, bf16[160,1536]{1,0:T(8,128)(2,1)S(1)}, u32[]{:S(2)}, u32[]{:S(2)}) collective-permute-start(bf16[160,1536]{1,0:T(8,128)(2,1)S(1)} %shard_map.49.rest_1_), channel_id=1, source_target_pairs={{0,1},{1,2},{2,3},{3,4},{4,5},{5,6},{6,7},{7,8},{8,9},{9,10},{10,1... | collective-permute-start | bytes 1474568 | tf_op jit(solution)/shard_map/ppermute | solution.py:41
  24.4 2.5 %collective-permute-start.8 = (bf16[128,1536]{1,0:T(8,128)(2,1)S(1)}, bf16[128,1536]{1,0:T(8,128)(2,1)S(1)}, u32[]{:S(2)}, u32[]{:S(2)}) collective-permute-start(bf16[128,1536]{1,0:T(8,128)(2,1)S(1)} %shard_map.50.rest_1_), channel_id=1, source_target_pairs={{0,1},{1,2},{2,3},{3,4},{4,5},{5,6},{6,7},{7,8},{8,9},{9,10},{10,1... | collective-permute-start | bytes 1179656 | tf_op jit(solution)/shard_map/ppermute | solution.py:41
  28.4 2.8 %collective-permute-start.6 = (bf16[128,1536]{1,0:T(8,128)(2,1)S(1)}, bf16[128,1536]{1,0:T(8,128)(2,1)S(1)}, u32[]{:S(2)}, u32[]{:S(2)}) collective-permute-start(bf16[128,1536]{1,0:T(8,128)(2,1)S(1)} %shard_map.51.rest_1_), channel_id=1, source_target_pairs={{0,1},{1,2},{2,3},{3,4},{4,5},{5,6},{6,7},{7,8},{8,9},{9,10},{10,1... | collective-permute-start | bytes 1179656 | tf_op jit(solution)/shard_map/ppermute | solution.py:41
  31.1 1.7 %shard_map.52 = (bf16[160,1536]{1,0:T(8,128)(2,1)S(1)}, f32[160,1536]{1,0:T(8,128)S(1)}) custom-call(bf16[512,1536]{1,0:T(8,128)(2,1)S(1)} %bitcast.8, bf16[2,1536,1536]{2,1,0:T(8,128)(2,1)S(1)} %get-tuple-element.39.w_ref, f32[8,1536]{1,0:T(8,128)S(1)} %get-tuple-element.40.p_ref, bf16[160,1536]{1,0:T(8,128)(2,1)S(1)} %collective-permute-done.1.rest_0_, ...), custom_call_target="tpu_custom_call" | custom-call | flops 4831838208 | tf_op jit(solution)/shard_map/pallas_call | solution.py:252
  32.9 3.8 %collective-permute-start.5 = (bf16[160,1536]{1,0:T(8,128)(2,1)S(1)}, bf16[160,1536]{1,0:T(8,128)(2,1)S(1)}, u32[]{:S(2)}, u32[]{:S(2)}) collective-permute-start(bf16[160,1536]{1,0:T(8,128)(2,1)S(1)} %get-tuple-element.42.rest_0_), channel_id=1, source_target_pairs={{0,1},{1,2},{2,3},{3,4},{4,5},{5,6},{6,7},{7,8},{8,9},{9,10},{10,1... | collective-permute-start | bytes 1474568 | tf_op jit(solution)/shard_map/ppermute | solution.py:41
  38.1 2.1 %collective-permute-start.4 = (bf16[96,1536]{1,0:T(8,128)(2,1)S(1)}, bf16[96,1536]{1,0:T(8,128)(2,1)S(1)}, u32[]{:S(2)}, u32[]{:S(2)}) collective-permute-start(bf16[96,1536]{1,0:T(8,128)(2,1)S(1)} %shard_map.53.rest_1_), channel_id=1, source_target_pairs={{0,1},{1,2},{2,3},{3,4},{4,5},{5,6},{6,7},{7,8},{8,9},{9,10},{10,1... | collective-permute-start | bytes 884744 | tf_op jit(solution)/shard_map/ppermute | solution.py:41
  41.7 3.1 %collective-permute-start.12 = (bf16[128,1536]{1,0:T(8,128)(2,1)S(1)}, bf16[128,1536]{1,0:T(8,128)(2,1)S(1)}, u32[]{:S(2)}, u32[]{:S(2)}) collective-permute-start(bf16[128,1536]{1,0:T(8,128)(2,1)S(1)} %get-tuple-element.44.rest_2_), channel_id=1, source_target_pairs={{0,1},{1,2},{2,3},{3,4},{4,5},{5,6},{6,7},{7,8},{8,9},{9,10},{10,1... | collective-permute-start | bytes 1179656 | tf_op jit(solution)/shard_map/ppermute | solution.py:41
  47.6 5.6 %collective-permute-start.7 = (bf16[96,1536]{1,0:T(8,128)(2,1)S(1)}, bf16[96,1536]{1,0:T(8,128)(2,1)S(1)}, u32[]{:S(2)}, u32[]{:S(2)}) collective-permute-start(bf16[96,1536]{1,0:T(8,128)(2,1)S(1)} %shard_map.56.rest_1_), channel_id=1, source_target_pairs={{0,1},{1,2},{2,3},{3,4},{4,5},{5,6},{6,7},{7,8},{8,9},{9,10},{10,1... | collective-permute-start | bytes 884744 | tf_op jit(solution)/shard_map/ppermute | solution.py:41
  56.0 1.9 %collective-permute-start.9 = (bf16[128,1536]{1,0:T(8,128)(2,1)S(1)}, bf16[128,1536]{1,0:T(8,128)(2,1)S(1)}, u32[]{:S(2)}, u32[]{:S(2)}) collective-permute-start(bf16[128,1536]{1,0:T(8,128)(2,1)S(1)} %get-tuple-element.46.rest_2_), channel_id=1, source_target_pairs={{15,11},{23,19}} | collective-permute-start | bytes 1179656 | tf_op jit(solution)/shard_map/ppermute | solution.py:41
  59.3 1.7 %collective-permute-done.11.rest_2_ = bf16[160,1536]{1,0:T(8,128)(2,1)S(1)} collective-permute-done((bf16[160,1536]{1,0:T(8,128)(2,1)S(1)}, bf16[160,1536]{1,0:T(8,128)(2,1)S(1)}, u32[]{:S(2)}, u32[]{:S(2)}) %collective-permute-start.11) | collective-permute-done | bytes 491552 | tf_op jit(solution)/shard_map/ppermute | solution.py:41
  66.9 1.9 %collective-permute-start.13 = (bf16[96,1536]{1,0:T(8,128)(2,1)S(1)}, bf16[96,1536]{1,0:T(8,128)(2,1)S(1)}, u32[]{:S(2)}, u32[]{:S(2)}) collective-permute-start(bf16[96,1536]{1,0:T(8,128)(2,1)S(1)} %get-tuple-element.54.rest_4_), channel_id=1, source_target_pairs={{0,1},{1,2},{2,3},{3,4},{4,5},{5,6},{6,7},{7,8},{8,9},{9,10},{10,1... | collective-permute-start | bytes 884744 | tf_op jit(solution)/shard_map/ppermute | solution.py:41
  68.8 5.5 %collective-permute-done.17.rest_2_ = bf16[128,1536]{1,0:T(8,128)(2,1)S(1)} collective-permute-done((bf16[128,1536]{1,0:T(8,128)(2,1)S(1)}, bf16[128,1536]{1,0:T(8,128)(2,1)S(1)}, u32[]{:S(2)}, u32[]{:S(2)}) %collective-permute-start.17) | collective-permute-done | bytes 393248 | tf_op jit(solution)/shard_map/ppermute | solution.py:41
  76.5 2.8 %shard_map.64 = (bf16[2,512,1536]{2,1,0:T(8,128)(2,1)}, f32[8,128]{1,0:T(8,128)S(1)}) custom-call(bf16[512,1536]{1,0:T(8,128)(2,1)S(1)} %bitcast.14, bf16[2,1536,1536]{2,1,0:T(8,128)(2,1)S(1)} %get-tuple-element.39.w_ref, f32[8,1536]{1,0:T(8,128)S(1)} %get-tuple-element.40.p_ref, bf16[160,1536]{1,0:T(8,128)(2,1)S(1)} %collective-permute-done.16.moved_ref, ...), custom_call_target="tpu_custom_call" | custom-call | flops 4831838208 | tf_op jit(solution)/shard_map/pallas_call | solution.py:252
  84.6 3.0 %collective-permute-done.19.moved_ref = bf16[128,1536]{1,0:T(8,128)(2,1)S(1)} collective-permute-done((bf16[128,1536]{1,0:T(8,128)(2,1)S(1)}, bf16[128,1536]{1,0:T(8,128)(2,1)S(1)}, u32[]{:S(2)}, u32[]{:S(2)}) %collective-permute-start.19) | collective-permute-done | bytes 393248 | tf_op jit(solution)/shard_map/ppermute | solution.py:41
  87.5 2.3 %shard_map.67 = (bf16[2,512,1536]{2,1,0:T(8,128)(2,1)}, f32[8,128]{1,0:T(8,128)S(1)}) custom-call(bf16[512,1536]{1,0:T(8,128)(2,1)S(1)} %bitcast.15, bf16[2,1536,1536]{2,1,0:T(8,128)(2,1)S(1)} %get-tuple-element.39.w_ref, f32[8,1536]{1,0:T(8,128)S(1)} %get-tuple-element.40.p_ref, ...), custom_call_target="tpu_custom_call", output_to_operand_aliasing={{0}: (7, {})} | custom-call | flops 4831838208 | tf_op jit(solution)/shard_map/pallas_call | solution.py:252
  89.8 3.8 %collective-permute-done.18.rest_2_ = bf16[96,1536]{1,0:T(8,128)(2,1)S(1)} collective-permute-done((bf16[96,1536]{1,0:T(8,128)(2,1)S(1)}, bf16[96,1536]{1,0:T(8,128)(2,1)S(1)}, u32[]{:S(2)}, u32[]{:S(2)}) %collective-permute-start.18) | collective-permute-done | bytes 294944 | tf_op jit(solution)/shard_map/ppermute | solution.py:41
  95.8 2.3 %shard_map.69 = (bf16[2,512,1536]{2,1,0:T(8,128)(2,1)}, f32[8,128]{1,0:T(8,128)S(1)}) custom-call(bf16[512,1536]{1,0:T(8,128)(2,1)S(1)} %bitcast.16, bf16[2,1536,1536]{2,1,0:T(8,128)(2,1)S(1)} %get-tuple-element.39.w_ref, f32[8,1536]{1,0:T(8,128)S(1)} %get-tuple-element.40.p_ref, ...), custom_call_target="tpu_custom_call", output_to_operand_aliasing={{0}: (8, {})} | custom-call | flops 4831838208 | tf_op jit(solution)/shard_map/pallas_call | solution.py:252
  98.0 4.0 %collective-permute-done.20.moved_ref = bf16[96,1536]{1,0:T(8,128)(2,1)S(1)} collective-permute-done((bf16[96,1536]{1,0:T(8,128)(2,1)S(1)}, bf16[96,1536]{1,0:T(8,128)(2,1)S(1)}, u32[]{:S(2)}, u32[]{:S(2)}) %collective-permute-start.20) | collective-permute-done | bytes 294944 | tf_op jit(solution)/shard_map/ppermute | solution.py:41
  102.0 2.8 %shard_map.70 = (bf16[2,512,1536]{2,1,0:T(8,128)(2,1)}, f32[8,128]{1,0:T(8,128)}) custom-call(bf16[512,1536]{1,0:T(8,128)(2,1)S(1)} %bitcast.17, bf16[2,1536,1536]{2,1,0:T(8,128)(2,1)S(1)} %get-tuple-element.39.w_ref, f32[8,1536]{1,0:T(8,128)S(1)} %get-tuple-element.40.p_ref, ...), custom_call_target="tpu_custom_call", output_to_operand_aliasing={{0}: (7, {})} | custom-call | flops 4831838208 | tf_op jit(solution)/shard_map/pallas_call | solution.py:252
  (47 shorter events, 30.7 us)
Async XLA Ops:
  0.0 9.3 %copy-start = (bf16[2,256,1536]{2,1,0:T(8,128)(2,1)S(1)}, bf16[2,256,1536]{2,1,0:T(8,128)(2,1)}, u32[]{:S(2)}) copy-start(bf16[2,256,1536]{2,1,0:T(8,128)(2,1)} %param.4) | copy-start | bytes 4718596
  5.7 12.0 %collective-permute-start = (bf16[160,1536]{1,0:T(8,128)(2,1)S(1)}, bf16[160,1536]{1,0:T(8,128)(2,1)S(1)}, u32[]{:S(2)}, u32[]{:S(2)}) collective-permute-start(bf16[160,1536]{1,0:T(8,128)(2,1)S(1)} %get-tuple-element.41.rest_0_), channel_id=1, source_target_pairs={{0,1},{1,2},{2,3},{3,4},{4,5},{5,6},{6,7},{7,8},{8,9},{9,10},{10,1... | collective-permute-start | bytes 1474568 | tf_op jit(solution)/shard_map/ppermute | solution.py:41
  10.8 12.2 %collective-permute-start.3 = (bf16[128,1536]{1,0:T(8,128)(2,1)S(1)}, bf16[128,1536]{1,0:T(8,128)(2,1)S(1)}, u32[]{:S(2)}, u32[]{:S(2)}) collective-permute-start(bf16[128,1536]{1,0:T(8,128)(2,1)S(1)} %shard_map.47.rest_0_), channel_id=1, source_target_pairs={{0,1},{1,2},{2,3},{3,4},{4,5},{5,6},{6,7},{7,8},{8,9},{9,10},{10,1... | collective-permute-start | bytes 1179656 | tf_op jit(solution)/shard_map/ppermute | solution.py:41
  14.2 12.8 %collective-permute-start.2 = (bf16[128,1536]{1,0:T(8,128)(2,1)S(1)}, bf16[128,1536]{1,0:T(8,128)(2,1)S(1)}, u32[]{:S(2)}, u32[]{:S(2)}) collective-permute-start(bf16[128,1536]{1,0:T(8,128)(2,1)S(1)} %shard_map.48.rest_1_), channel_id=1, source_target_pairs={{0,1},{1,2},{2,3},{3,4},{4,5},{5,6},{6,7},{7,8},{8,9},{9,10},{10,1... | collective-permute-start | bytes 1179656 | tf_op jit(solution)/shard_map/ppermute | solution.py:41
  19.4 11.8 %collective-permute-start.1 = (bf16[160,1536]{1,0:T(8,128)(2,1)S(1)}, bf16[160,1536]{1,0:T(8,128)(2,1)S(1)}, u32[]{:S(2)}, u32[]{:S(2)}) collective-permute-start(bf16[160,1536]{1,0:T(8,128)(2,1)S(1)} %shard_map.49.rest_1_), channel_id=1, source_target_pairs={{0,1},{1,2},{2,3},{3,4},{4,5},{5,6},{6,7},{7,8},{8,9},{9,10},{10,1... | collective-permute-start | bytes 1474568 | tf_op jit(solution)/shard_map/ppermute | solution.py:41
  24.4 28.8 %collective-permute-start.8 = (bf16[128,1536]{1,0:T(8,128)(2,1)S(1)}, bf16[128,1536]{1,0:T(8,128)(2,1)S(1)}, u32[]{:S(2)}, u32[]{:S(2)}) collective-permute-start(bf16[128,1536]{1,0:T(8,128)(2,1)S(1)} %shard_map.50.rest_1_), channel_id=1, source_target_pairs={{0,1},{1,2},{2,3},{3,4},{4,5},{5,6},{6,7},{7,8},{8,9},{9,10},{10,1... | collective-permute-start | bytes 1179656 | tf_op jit(solution)/shard_map/ppermute | solution.py:41
  28.4 11.9 %collective-permute-start.6 = (bf16[128,1536]{1,0:T(8,128)(2,1)S(1)}, bf16[128,1536]{1,0:T(8,128)(2,1)S(1)}, u32[]{:S(2)}, u32[]{:S(2)}) collective-permute-start(bf16[128,1536]{1,0:T(8,128)(2,1)S(1)} %shard_map.51.rest_1_), channel_id=1, source_target_pairs={{0,1},{1,2},{2,3},{3,4},{4,5},{5,6},{6,7},{7,8},{8,9},{9,10},{10,1... | collective-permute-start | bytes 1179656 | tf_op jit(solution)/shard_map/ppermute | solution.py:41
  32.9 12.0 %collective-permute-start.5 = (bf16[160,1536]{1,0:T(8,128)(2,1)S(1)}, bf16[160,1536]{1,0:T(8,128)(2,1)S(1)}, u32[]{:S(2)}, u32[]{:S(2)}) collective-permute-start(bf16[160,1536]{1,0:T(8,128)(2,1)S(1)} %get-tuple-element.42.rest_0_), channel_id=1, source_target_pairs={{0,1},{1,2},{2,3},{3,4},{4,5},{5,6},{6,7},{7,8},{8,9},{9,10},{10,1... | collective-permute-start | bytes 1474568 | tf_op jit(solution)/shard_map/ppermute | solution.py:41
  38.1 8.0 %collective-permute-start.4 = (bf16[96,1536]{1,0:T(8,128)(2,1)S(1)}, bf16[96,1536]{1,0:T(8,128)(2,1)S(1)}, u32[]{:S(2)}, u32[]{:S(2)}) collective-permute-start(bf16[96,1536]{1,0:T(8,128)(2,1)S(1)} %shard_map.53.rest_1_), channel_id=1, source_target_pairs={{0,1},{1,2},{2,3},{3,4},{4,5},{5,6},{6,7},{7,8},{8,9},{9,10},{10,1... | collective-permute-start | bytes 884744 | tf_op jit(solution)/shard_map/ppermute | solution.py:41
  41.7 16.2 %collective-permute-start.12 = (bf16[128,1536]{1,0:T(8,128)(2,1)S(1)}, bf16[128,1536]{1,0:T(8,128)(2,1)S(1)}, u32[]{:S(2)}, u32[]{:S(2)}) collective-permute-start(bf16[128,1536]{1,0:T(8,128)(2,1)S(1)} %get-tuple-element.44.rest_2_), channel_id=1, source_target_pairs={{0,1},{1,2},{2,3},{3,4},{4,5},{5,6},{6,7},{7,8},{8,9},{9,10},{10,1... | collective-permute-start | bytes 1179656 | tf_op jit(solution)/shard_map/ppermute | solution.py:41
  44.9 16.1 %collective-permute-start.11 = (bf16[160,1536]{1,0:T(8,128)(2,1)S(1)}, bf16[160,1536]{1,0:T(8,128)(2,1)S(1)}, u32[]{:S(2)}, u32[]{:S(2)}) collective-permute-start(bf16[160,1536]{1,0:T(8,128)(2,1)S(1)} %get-tuple-element.45.rest_1_), channel_id=1, source_target_pairs={{8,16},{9,17},{10,18},{11,19},{12,20},{13,21},{14,22},{15,23}} | collective-permute-start | bytes 1474568 | tf_op jit(solution)/shard_map/ppermute | solution.py:41
  47.6 17.8 %collective-permute-start.7 = (bf16[96,1536]{1,0:T(8,128)(2,1)S(1)}, bf16[96,1536]{1,0:T(8,128)(2,1)S(1)}, u32[]{:S(2)}, u32[]{:S(2)}) collective-permute-start(bf16[96,1536]{1,0:T(8,128)(2,1)S(1)} %shard_map.56.rest_1_), channel_id=1, source_target_pairs={{0,1},{1,2},{2,3},{3,4},{4,5},{5,6},{6,7},{7,8},{8,9},{9,10},{10,1... | collective-permute-start | bytes 884744 | tf_op jit(solution)/shard_map/ppermute | solution.py:41
  54.7 8.7 %collective-permute-start.10 = (bf16[128,1536]{1,0:T(8,128)(2,1)S(1)}, bf16[128,1536]{1,0:T(8,128)(2,1)S(1)}, u32[]{:S(2)}, u32[]{:S(2)}) collective-permute-start(bf16[128,1536]{1,0:T(8,128)(2,1)S(1)} %get-tuple-element.46.rest_2_), channel_id=1, source_target_pairs={{0,1},{1,2},{2,3},{3,4},{4,5},{5,6},{6,7},{7,8},{8,9},{9,10},{10,1... | collective-permute-start | bytes 1179656 | tf_op jit(solution)/shard_map/ppermute | solution.py:41
  56.0 8.7 %collective-permute-start.9 = (bf16[128,1536]{1,0:T(8,128)(2,1)S(1)}, bf16[128,1536]{1,0:T(8,128)(2,1)S(1)}, u32[]{:S(2)}, u32[]{:S(2)}) collective-permute-start(bf16[128,1536]{1,0:T(8,128)(2,1)S(1)} %get-tuple-element.46.rest_2_), channel_id=1, source_target_pairs={{15,11},{23,19}} | collective-permute-start | bytes 1179656 | tf_op jit(solution)/shard_map/ppermute | solution.py:41
  58.0 16.4 %collective-permute-start.17 = (bf16[128,1536]{1,0:T(8,128)(2,1)S(1)}, bf16[128,1536]{1,0:T(8,128)(2,1)S(1)}, u32[]{:S(2)}, u32[]{:S(2)}) collective-permute-start(bf16[128,1536]{1,0:T(8,128)(2,1)S(1)} %get-tuple-element.50.rest_4_), channel_id=1, source_target_pairs={{8,16},{9,17},{10,18},{11,19},{12,20},{13,21},{14,22},{15,23}} | collective-permute-start | bytes 1179656 | tf_op jit(solution)/shard_map/ppermute | solution.py:41
  62.0 14.5 %collective-permute-start.16 = (bf16[160,1536]{1,0:T(8,128)(2,1)S(1)}, bf16[160,1536]{1,0:T(8,128)(2,1)S(1)}, u32[]{:S(2)}, u32[]{:S(2)}) collective-permute-start(bf16[160,1536]{1,0:T(8,128)(2,1)S(1)} %get-tuple-element.51.rest_2_), channel_id=1, source_target_pairs={{16,24},{17,25},{18,26},{19,27},{20,28},{21,29},{22,30},{23,31}} | collective-permute-start | bytes 1474568 | tf_op jit(solution)/shard_map/ppermute | solution.py:41
  63.4 17.6 %collective-permute-start.15 = (bf16[128,1536]{1,0:T(8,128)(2,1)S(1)}, bf16[128,1536]{1,0:T(8,128)(2,1)S(1)}, u32[]{:S(2)}, u32[]{:S(2)}) collective-permute-start(bf16[128,1536]{1,0:T(8,128)(2,1)S(1)} %get-tuple-element.52.rest_0_), channel_id=1, source_target_pairs={{8,16},{9,17},{10,18},{11,19},{12,20},{13,21},{14,22},{15,23}} | collective-permute-start | bytes 1179656 | tf_op jit(solution)/shard_map/ppermute | solution.py:41
  64.7 14.6 %collective-permute-start.14 = (bf16[128,1536]{1,0:T(8,128)(2,1)S(1)}, bf16[128,1536]{1,0:T(8,128)(2,1)S(1)}, u32[]{:S(2)}, u32[]{:S(2)}) collective-permute-start(bf16[128,1536]{1,0:T(8,128)(2,1)S(1)} %shard_map.61.rest_1_), channel_id=1, source_target_pairs={{11,16},{19,24}} | collective-permute-start | bytes 1179656 | tf_op jit(solution)/shard_map/ppermute | solution.py:41
  66.9 16.3 %collective-permute-start.13 = (bf16[96,1536]{1,0:T(8,128)(2,1)S(1)}, bf16[96,1536]{1,0:T(8,128)(2,1)S(1)}, u32[]{:S(2)}, u32[]{:S(2)}) collective-permute-start(bf16[96,1536]{1,0:T(8,128)(2,1)S(1)} %get-tuple-element.54.rest_4_), channel_id=1, source_target_pairs={{0,1},{1,2},{2,3},{3,4},{4,5},{5,6},{6,7},{7,8},{8,9},{9,10},{10,1... | collective-permute-start | bytes 884744 | tf_op jit(solution)/shard_map/ppermute | solution.py:41
  75.2 12.3 %collective-permute-start.19 = (bf16[128,1536]{1,0:T(8,128)(2,1)S(1)}, bf16[128,1536]{1,0:T(8,128)(2,1)S(1)}, u32[]{:S(2)}, u32[]{:S(2)}) collective-permute-start(bf16[128,1536]{1,0:T(8,128)(2,1)S(1)} %get-tuple-element.58.rest_2_), channel_id=1, source_target_pairs={{16,24},{17,25},{18,26},{19,27},{20,28},{21,29},{22,30},{23,31}} | collective-permute-start | bytes 1179656 | tf_op jit(solution)/shard_map/ppermute | solution.py:41
  81.9 13.8 %collective-permute-start.21 = (bf16[128,1536]{1,0:T(8,128)(2,1)S(1)}, bf16[128,1536]{1,0:T(8,128)(2,1)S(1)}, u32[]{:S(2)}, u32[]{:S(2)}) collective-permute-start(bf16[128,1536]{1,0:T(8,128)(2,1)S(1)} %get-tuple-element.60.rest_2_), channel_id=1, source_target_pairs={{16,24},{17,25},{18,26},{19,27},{20,28},{21,29},{22,30},{23,31}} | collective-permute-start | bytes 1179656 | tf_op jit(solution)/shard_map/ppermute | solution.py:41
  83.3 10.3 %collective-permute-start.18 = (bf16[96,1536]{1,0:T(8,128)(2,1)S(1)}, bf16[96,1536]{1,0:T(8,128)(2,1)S(1)}, u32[]{:S(2)}, u32[]{:S(2)}) collective-permute-start(bf16[96,1536]{1,0:T(8,128)(2,1)S(1)} %get-tuple-element.61.rest_3_), channel_id=1, source_target_pairs={{8,16},{9,17},{10,18},{11,19},{12,20},{13,21},{14,22},{15,23}} | collective-permute-start | bytes 884744 | tf_op jit(solution)/shard_map/ppermute | solution.py:41
  94.4 7.6 %collective-permute-start.20 = (bf16[96,1536]{1,0:T(8,128)(2,1)S(1)}, bf16[96,1536]{1,0:T(8,128)(2,1)S(1)}, u32[]{:S(2)}, u32[]{:S(2)}) collective-permute-start(bf16[96,1536]{1,0:T(8,128)(2,1)S(1)} %get-tuple-element.66.rest_4_), channel_id=1, source_target_pairs={{16,24},{17,25},{18,26},{19,27},{20,28},{21,29},{22,30},{23,31}} | collective-permute-start | bytes 884744 | tf_op jit(solution)/shard_map/ppermute | solution.py:41

commit v5 on v4

--- a/solution.py
+++ b/solution.py
@@ -10,9 +10,9 @@
 LAY_DEV = 2
 INTERVAL = 8
 
-SHARES = (5, 4, 4, 3)
+SHARES = (4, 5, 4, 3)
 ORDER = (
-    0, 20, 10, 1, 21, 11, 2, 30, 12, 3, 31, 22, 13, 4, 23, 28, 32, 14, 5, 24, 33, 15, 34, 25, 35,
+    0, 20, 10, 1, 21, 11, 2, 30, 12, 3, 31, 22, 13, 17, 4, 32, 23, 14, 33, 5, 24, 34, 15, 25, 35,
 )
 RELAYS = {7: 2, 8: 4}
 APART = ()

time: 107 us -> 105 us (0.981)
  starting transfers between devices: 48.8 us -> 46.6 us
  waiting for transfers between devices: 19.6 us -> 20.7 us
    ppermute x22, starting transfers between devices: 48.8 us -> 46.6 us  [passed_along(): return lax.ppermute(value, 'depth', pairs)]
  transfers between devices with their start and end apart: 22 -> 22, of which waited for: 6 -> 5; matrix products, arithmetic and copies ran while one was open for 0% -> 0% of each run, Pallas kernels for 26% -> 27%
where the time goes in v5:
time: 105 us; the launch traced here: 104 us
  starting transfers between devices  46.6 us (44%)
  Pallas kernels  35.8 us (34%)
  waiting for transfers between devices  20.7 us (20%)
    ppermute x22, starting transfers between devices, passed_along(): return lax.ppermute(value, 'depth', pairs)  46.6 us
    pallas_call x25, Pallas kernels, call(): pl.pallas_call(body, out_shape=outs, in_specs=specs, out_specs=out_specs...  35.8 us
    ppermute x22, waiting for transfers between devices, passed_along(): return lax.ppermute(value, 'depth', pairs)  20.7 us
  transfers between devices with their start and end apart: 22, of which 5 were waited for; matrix products, arithmetic and copies ran while one was open for 0% of the time, Pallas kernels for 27%

profile of v5, /device:TPU:23, one launch (start us, length us, event | category | flops | bytes accessed | tf_op | source)
XLA Modules:
  0.0 103.8 jit_solution(7964145207107695537)
XLA Ops:
  0.0 5.3 %shard_map.46 = (bf16[128,1536]{1,0:T(8,128)(2,1)S(1)}, bf16[2,1536,1536]{2,1,0:T(8,128)(2,1)S(1)}, f32[8,1536]{1,0:T(8,128)S(1)}) custom-call(bf16[512,1536]{1,0:T(8,128)(2,1)} %bitcast.2, bf16[2,1536,1536]{2,1,0:T(8,128)(2,1)} %w_hbm.1, f32[2,1536]{1,0:T(2,128)} %b_hbm.1, f32[2]{0:T(128)} %h_hbm.1), custom_call_target="tpu_custom_call" | custom-call | flops 4831838208 | tf_op jit(solution)/shard_map/pallas_call | solution.py:252
  5.3 3.7 %collective-permute-start = (bf16[128,1536]{1,0:T(8,128)(2,1)S(1)}, bf16[128,1536]{1,0:T(8,128)(2,1)S(1)}, u32[]{:S(2)}, u32[]{:S(2)}) collective-permute-start(bf16[128,1536]{1,0:T(8,128)(2,1)S(1)} %get-tuple-element.41.rest_0_), channel_id=1, source_target_pairs={{0,1},{1,2},{2,3},{3,4},{4,5},{5,6},{6,7},{7,8},{8,9},{9,10},{10,1... | collective-permute-start | bytes 1179656 | tf_op jit(solution)/shard_map/ppermute | solution.py:41
  10.4 1.9 %collective-permute-start.3 = (bf16[128,1536]{1,0:T(8,128)(2,1)S(1)}, bf16[128,1536]{1,0:T(8,128)(2,1)S(1)}, u32[]{:S(2)}, u32[]{:S(2)}) collective-permute-start(bf16[128,1536]{1,0:T(8,128)(2,1)S(1)} %shard_map.47.rest_0_), channel_id=1, source_target_pairs={{0,1},{1,2},{2,3},{3,4},{4,5},{5,6},{6,7},{7,8},{8,9},{9,10},{10,1... | collective-permute-start | bytes 1179656 | tf_op jit(solution)/shard_map/ppermute | solution.py:41
  12.4 1.7 %shard_map.48.rest_1_ = bf16[160,1536]{1,0:T(8,128)(2,1)S(1)} custom-call(bf16[512,1536]{1,0:T(8,128)(2,1)S(1)} %bitcast.4, bf16[2,1536,1536]{2,1,0:T(8,128)(2,1)S(1)} %get-tuple-element.39.w_ref, f32[8,1536]{1,0:T(8,128)S(1)} %get-tuple-element.40.p_ref, bf16[128,1536]{1,0:T(8,128)(2,1)S(1)} %shard_map.47.rest_0_), custom_call_target="tpu_custom_call" | custom-call | flops 4831838208 | tf_op jit(solution)/shard_map/pallas_call | solution.py:252
  14.1 3.5 %collective-permute-start.2 = (bf16[160,1536]{1,0:T(8,128)(2,1)S(1)}, bf16[160,1536]{1,0:T(8,128)(2,1)S(1)}, u32[]{:S(2)}, u32[]{:S(2)}) collective-permute-start(bf16[160,1536]{1,0:T(8,128)(2,1)S(1)} %shard_map.48.rest_1_), channel_id=1, source_target_pairs={{0,1},{1,2},{2,3},{3,4},{4,5},{5,6},{6,7},{7,8},{8,9},{9,10},{10,1... | collective-permute-start | bytes 1474568 | tf_op jit(solution)/shard_map/ppermute | solution.py:41
  19.1 2.3 %collective-permute-start.1 = (bf16[128,1536]{1,0:T(8,128)(2,1)S(1)}, bf16[128,1536]{1,0:T(8,128)(2,1)S(1)}, u32[]{:S(2)}, u32[]{:S(2)}) collective-permute-start(bf16[128,1536]{1,0:T(8,128)(2,1)S(1)} %shard_map.49.rest_1_), channel_id=1, source_target_pairs={{0,1},{1,2},{2,3},{3,4},{4,5},{5,6},{6,7},{7,8},{8,9},{9,10},{10,1... | collective-permute-start | bytes 1179656 | tf_op jit(solution)/shard_map/ppermute | solution.py:41
  22.8 3.2 %collective-permute-start.11 = (bf16[128,1536]{1,0:T(8,128)(2,1)S(1)}, bf16[128,1536]{1,0:T(8,128)(2,1)S(1)}, u32[]{:S(2)}, u32[]{:S(2)}) collective-permute-start(bf16[128,1536]{1,0:T(8,128)(2,1)S(1)} %shard_map.50.rest_1_), channel_id=1, source_target_pairs={{0,1},{1,2},{2,3},{3,4},{4,5},{5,6},{6,7},{7,8},{8,9},{9,10},{10,1... | collective-permute-start | bytes 1179656 | tf_op jit(solution)/shard_map/ppermute | solution.py:41
  25.9 1.7 %shard_map.51.rest_1_ = bf16[160,1536]{1,0:T(8,128)(2,1)S(1)} custom-call(bf16[512,1536]{1,0:T(8,128)(2,1)S(1)} %bitcast.7, bf16[2,1536,1536]{2,1,0:T(8,128)(2,1)S(1)} %get-tuple-element.39.w_ref, f32[8,1536]{1,0:T(8,128)S(1)} %get-tuple-element.40.p_ref, bf16[160,1536]{1,0:T(8,128)(2,1)S(1)} %collective-permute-done.2.rest_0_, ...), custom_call_target="tpu_custom_call" | custom-call | flops 4831838208 | tf_op jit(solution)/shard_map/pallas_call | solution.py:252
  27.7 3.6 %collective-permute-start.6 = (bf16[160,1536]{1,0:T(8,128)(2,1)S(1)}, bf16[160,1536]{1,0:T(8,128)(2,1)S(1)}, u32[]{:S(2)}, u32[]{:S(2)}) collective-permute-start(bf16[160,1536]{1,0:T(8,128)(2,1)S(1)} %shard_map.51.rest_1_), channel_id=1, source_target_pairs={{0,1},{1,2},{2,3},{3,4},{4,5},{5,6},{6,7},{7,8},{8,9},{9,10},{10,1... | collective-permute-start | bytes 1474568 | tf_op jit(solution)/shard_map/ppermute | solution.py:41
  32.7 2.5 %collective-permute-start.5 = (bf16[128,1536]{1,0:T(8,128)(2,1)S(1)}, bf16[128,1536]{1,0:T(8,128)(2,1)S(1)}, u32[]{:S(2)}, u32[]{:S(2)}) collective-permute-start(bf16[128,1536]{1,0:T(8,128)(2,1)S(1)} %get-tuple-element.42.rest_0_), channel_id=1, source_target_pairs={{0,1},{1,2},{2,3},{3,4},{4,5},{5,6},{6,7},{7,8},{8,9},{9,10},{10,1... | collective-permute-start | bytes 1179656 | tf_op jit(solution)/shard_map/ppermute | solution.py:41
  35.2 1.4 %shard_map.53.rest_1_ = bf16[96,1536]{1,0:T(8,128)(2,1)S(1)} custom-call(bf16[512,1536]{1,0:T(8,128)(2,1)S(1)} %bitcast.9, bf16[2,1536,1536]{2,1,0:T(8,128)(2,1)S(1)} %get-tuple-element.39.w_ref, f32[8,1536]{1,0:T(8,128)S(1)} %get-tuple-element.40.p_ref, bf16[128,1536]{1,0:T(8,128)(2,1)S(1)} %get-tuple-element.42.rest_0_), custom_call_target="tpu_custom_call" | custom-call | flops 4831838208 | tf_op jit(solution)/shard_map/pallas_call | solution.py:252
  36.7 2.1 %collective-permute-start.4 = (bf16[96,1536]{1,0:T(8,128)(2,1)S(1)}, bf16[96,1536]{1,0:T(8,128)(2,1)S(1)}, u32[]{:S(2)}, u32[]{:S(2)}) collective-permute-start(bf16[96,1536]{1,0:T(8,128)(2,1)S(1)} %shard_map.53.rest_1_), channel_id=1, source_target_pairs={{0,1},{1,2},{2,3},{3,4},{4,5},{5,6},{6,7},{7,8},{8,9},{9,10},{10,1... | collective-permute-start | bytes 884744 | tf_op jit(solution)/shard_map/ppermute | solution.py:41
  38.8 1.7 %shard_map.54 = (bf16[160,1536]{1,0:T(8,128)(2,1)S(1)}, f32[160,1536]{1,0:T(8,128)S(1)}) custom-call(bf16[512,1536]{1,0:T(8,128)(2,1)S(1)} %bitcast.10, bf16[2,1536,1536]{2,1,0:T(8,128)(2,1)S(1)} %get-tuple-element.39.w_ref, f32[8,1536]{1,0:T(8,128)S(1)} %get-tuple-element.40.p_ref, bf16[160,1536]{1,0:T(8,128)(2,1)S(1)} %collective-permute-done.6.rest_0_, ...), custom_call_target="tpu_custom_call" | custom-call | flops 4831838208 | tf_op jit(solution)/shard_map/pallas_call | solution.py:252
  41.8 4.4 %collective-permute-start.9 = (bf16[160,1536]{1,0:T(8,128)(2,1)S(1)}, bf16[160,1536]{1,0:T(8,128)(2,1)S(1)}, u32[]{:S(2)}, u32[]{:S(2)}) collective-permute-start(bf16[160,1536]{1,0:T(8,128)(2,1)S(1)} %get-tuple-element.44.rest_2_), channel_id=1, source_target_pairs={{15,13},{23,21}} | collective-permute-start | bytes 1474568 | tf_op jit(solution)/shard_map/ppermute | solution.py:41
  49.0 3.1 %collective-permute-start.7 = (bf16[96,1536]{1,0:T(8,128)(2,1)S(1)}, bf16[96,1536]{1,0:T(8,128)(2,1)S(1)}, u32[]{:S(2)}, u32[]{:S(2)}) collective-permute-start(bf16[96,1536]{1,0:T(8,128)(2,1)S(1)} %shard_map.56.rest_1_), channel_id=1, source_target_pairs={{0,1},{1,2},{2,3},{3,4},{4,5},{5,6},{6,7},{7,8},{8,9},{9,10},{10,1... | collective-permute-start | bytes 884744 | tf_op jit(solution)/shard_map/ppermute | solution.py:41
  53.5 1.9 %collective-permute-start.15 = (bf16[128,1536]{1,0:T(8,128)(2,1)S(1)}, bf16[128,1536]{1,0:T(8,128)(2,1)S(1)}, u32[]{:S(2)}, u32[]{:S(2)}) collective-permute-start(bf16[128,1536]{1,0:T(8,128)(2,1)S(1)} %get-tuple-element.48.rest_2_), channel_id=1, source_target_pairs={{0,1},{1,2},{2,3},{3,4},{4,5},{5,6},{6,7},{7,8},{8,9},{9,10},{10,1... | collective-permute-start | bytes 1179656 | tf_op jit(solution)/shard_map/ppermute | solution.py:41
  59.8 1.4 %shard_map.61 = (bf16[96,1536]{1,0:T(8,128)(2,1)S(1)}, f32[96,1536]{1,0:T(8,128)S(1)}) custom-call(bf16[512,1536]{1,0:T(8,128)(2,1)S(1)} %bitcast.13, bf16[2,1536,1536]{2,1,0:T(8,128)(2,1)S(1)} %get-tuple-element.39.w_ref, f32[8,1536]{1,0:T(8,128)S(1)} %get-tuple-element.40.p_ref, bf16[96,1536]{1,0:T(8,128)(2,1)S(1)} %collective-permute-done.7.rest_0_, ...), custom_call_target="tpu_custom_call" | custom-call | flops 4831838208 | tf_op jit(solution)/shard_map/pallas_call | solution.py:252
  61.2 2.1 %collective-permute-start.12 = (bf16[96,1536]{1,0:T(8,128)(2,1)S(1)}, bf16[96,1536]{1,0:T(8,128)(2,1)S(1)}, u32[]{:S(2)}, u32[]{:S(2)}) collective-permute-start(bf16[96,1536]{1,0:T(8,128)(2,1)S(1)} %get-tuple-element.52.rest_2_), channel_id=1, source_target_pairs={{0,1},{1,2},{2,3},{3,4},{4,5},{5,6},{6,7},{7,8},{8,9},{9,10},{10,1... | collective-permute-start | bytes 884744 | tf_op jit(solution)/shard_map/ppermute | solution.py:41
  64.7 13.0 %collective-permute-done.14.rest_3_ = bf16[160,1536]{1,0:T(8,128)(2,1)S(1)} collective-permute-done((bf16[160,1536]{1,0:T(8,128)(2,1)S(1)}, bf16[160,1536]{1,0:T(8,128)(2,1)S(1)}, u32[]{:S(2)}, u32[]{:S(2)}) %collective-permute-start.14) | collective-permute-done | bytes 491552 | tf_op jit(solution)/shard_map/ppermute | solution.py:41
  81.5 2.5 %shard_map.65 = (bf16[2,512,1536]{2,1,0:T(8,128)(2,1)}, f32[8,128]{1,0:T(8,128)S(1)}) custom-call(bf16[512,1536]{1,0:T(8,128)(2,1)S(1)} %bitcast.14, bf16[2,1536,1536]{2,1,0:T(8,128)(2,1)S(1)} %get-tuple-element.39.w_ref, f32[8,1536]{1,0:T(8,128)S(1)} %get-tuple-element.40.p_ref, bf16[128,1536]{1,0:T(8,128)(2,1)S(1)} %collective-permute-done.18.moved_ref, ...), custom_call_target="tpu_custom_call" | custom-call | flops 4831838208 | tf_op jit(solution)/shard_map/pallas_call | solution.py:252
  84.0 5.5 %collective-permute-done.17.rest_2_ = bf16[128,1536]{1,0:T(8,128)(2,1)S(1)} collective-permute-done((bf16[128,1536]{1,0:T(8,128)(2,1)S(1)}, bf16[128,1536]{1,0:T(8,128)(2,1)S(1)}, u32[]{:S(2)}, u32[]{:S(2)}) %collective-permute-start.17) | collective-permute-done | bytes 393248 | tf_op jit(solution)/shard_map/ppermute | solution.py:41
  94.8 2.6 %shard_map.68 = (bf16[2,512,1536]{2,1,0:T(8,128)(2,1)}, f32[8,128]{1,0:T(8,128)S(1)}) custom-call(bf16[512,1536]{1,0:T(8,128)(2,1)S(1)} %bitcast.15, bf16[2,1536,1536]{2,1,0:T(8,128)(2,1)S(1)} %get-tuple-element.39.w_ref, f32[8,1536]{1,0:T(8,128)S(1)} %get-tuple-element.40.p_ref, ...), custom_call_target="tpu_custom_call", output_to_operand_aliasing={{0}: (8, {})} | custom-call | flops 4831838208 | tf_op jit(solution)/shard_map/pallas_call | solution.py:252
  97.7 2.3 %shard_map.69 = (bf16[2,512,1536]{2,1,0:T(8,128)(2,1)}, f32[8,128]{1,0:T(8,128)S(1)}) custom-call(bf16[512,1536]{1,0:T(8,128)(2,1)S(1)} %bitcast.16, bf16[2,1536,1536]{2,1,0:T(8,128)(2,1)S(1)} %get-tuple-element.39.w_ref, f32[8,1536]{1,0:T(8,128)S(1)} %get-tuple-element.40.p_ref, ...), custom_call_target="tpu_custom_call", output_to_operand_aliasing={{0}: (7, {})} | custom-call | flops 4831838208 | tf_op jit(solution)/shard_map/pallas_call | solution.py:252
  100.9 2.8 %shard_map.70 = (bf16[2,512,1536]{2,1,0:T(8,128)(2,1)}, f32[8,128]{1,0:T(8,128)}) custom-call(bf16[512,1536]{1,0:T(8,128)(2,1)S(1)} %bitcast.17, bf16[2,1536,1536]{2,1,0:T(8,128)(2,1)S(1)} %get-tuple-element.39.w_ref, f32[8,1536]{1,0:T(8,128)S(1)} %get-tuple-element.40.p_ref, ...), custom_call_target="tpu_custom_call", output_to_operand_aliasing={{0}: (7, {})} | custom-call | flops 4831838208 | tf_op jit(solution)/shard_map/pallas_call | solution.py:252
  (47 shorter events, 26.9 us)
Async XLA Ops:
  0.0 9.0 %copy-start = (bf16[2,256,1536]{2,1,0:T(8,128)(2,1)S(1)}, bf16[2,256,1536]{2,1,0:T(8,128)(2,1)}, u32[]{:S(2)}) copy-start(bf16[2,256,1536]{2,1,0:T(8,128)(2,1)} %param.4) | copy-start | bytes 4718596
  5.3 12.3 %collective-permute-start = (bf16[128,1536]{1,0:T(8,128)(2,1)S(1)}, bf16[128,1536]{1,0:T(8,128)(2,1)S(1)}, u32[]{:S(2)}, u32[]{:S(2)}) collective-permute-start(bf16[128,1536]{1,0:T(8,128)(2,1)S(1)} %get-tuple-element.41.rest_0_), channel_id=1, source_target_pairs={{0,1},{1,2},{2,3},{3,4},{4,5},{5,6},{6,7},{7,8},{8,9},{9,10},{10,1... | collective-permute-start | bytes 1179656 | tf_op jit(solution)/shard_map/ppermute | solution.py:41
  10.4 10.9 %collective-permute-start.3 = (bf16[128,1536]{1,0:T(8,128)(2,1)S(1)}, bf16[128,1536]{1,0:T(8,128)(2,1)S(1)}, u32[]{:S(2)}, u32[]{:S(2)}) collective-permute-start(bf16[128,1536]{1,0:T(8,128)(2,1)S(1)} %shard_map.47.rest_0_), channel_id=1, source_target_pairs={{0,1},{1,2},{2,3},{3,4},{4,5},{5,6},{6,7},{7,8},{8,9},{9,10},{10,1... | collective-permute-start | bytes 1179656 | tf_op jit(solution)/shard_map/ppermute | solution.py:41
  14.1 11.8 %collective-permute-start.2 = (bf16[160,1536]{1,0:T(8,128)(2,1)S(1)}, bf16[160,1536]{1,0:T(8,128)(2,1)S(1)}, u32[]{:S(2)}, u32[]{:S(2)}) collective-permute-start(bf16[160,1536]{1,0:T(8,128)(2,1)S(1)} %shard_map.48.rest_1_), channel_id=1, source_target_pairs={{0,1},{1,2},{2,3},{3,4},{4,5},{5,6},{6,7},{7,8},{8,9},{9,10},{10,1... | collective-permute-start | bytes 1474568 | tf_op jit(solution)/shard_map/ppermute | solution.py:41
  19.1 12.2 %collective-permute-start.1 = (bf16[128,1536]{1,0:T(8,128)(2,1)S(1)}, bf16[128,1536]{1,0:T(8,128)(2,1)S(1)}, u32[]{:S(2)}, u32[]{:S(2)}) collective-permute-start(bf16[128,1536]{1,0:T(8,128)(2,1)S(1)} %shard_map.49.rest_1_), channel_id=1, source_target_pairs={{0,1},{1,2},{2,3},{3,4},{4,5},{5,6},{6,7},{7,8},{8,9},{9,10},{10,1... | collective-permute-start | bytes 1179656 | tf_op jit(solution)/shard_map/ppermute | solution.py:41
  22.8 29.3 %collective-permute-start.11 = (bf16[128,1536]{1,0:T(8,128)(2,1)S(1)}, bf16[128,1536]{1,0:T(8,128)(2,1)S(1)}, u32[]{:S(2)}, u32[]{:S(2)}) collective-permute-start(bf16[128,1536]{1,0:T(8,128)(2,1)S(1)} %shard_map.50.rest_1_), channel_id=1, source_target_pairs={{0,1},{1,2},{2,3},{3,4},{4,5},{5,6},{6,7},{7,8},{8,9},{9,10},{10,1... | collective-permute-start | bytes 1179656 | tf_op jit(solution)/shard_map/ppermute | solution.py:41
  27.7 11.1 %collective-permute-start.6 = (bf16[160,1536]{1,0:T(8,128)(2,1)S(1)}, bf16[160,1536]{1,0:T(8,128)(2,1)S(1)}, u32[]{:S(2)}, u32[]{:S(2)}) collective-permute-start(bf16[160,1536]{1,0:T(8,128)(2,1)S(1)} %shard_map.51.rest_1_), channel_id=1, source_target_pairs={{0,1},{1,2},{2,3},{3,4},{4,5},{5,6},{6,7},{7,8},{8,9},{9,10},{10,1... | collective-permute-start | bytes 1474568 | tf_op jit(solution)/shard_map/ppermute | solution.py:41
  32.7 13.5 %collective-permute-start.5 = (bf16[128,1536]{1,0:T(8,128)(2,1)S(1)}, bf16[128,1536]{1,0:T(8,128)(2,1)S(1)}, u32[]{:S(2)}, u32[]{:S(2)}) collective-permute-start(bf16[128,1536]{1,0:T(8,128)(2,1)S(1)} %get-tuple-element.42.rest_0_), channel_id=1, source_target_pairs={{0,1},{1,2},{2,3},{3,4},{4,5},{5,6},{6,7},{7,8},{8,9},{9,10},{10,1... | collective-permute-start | bytes 1179656 | tf_op jit(solution)/shard_map/ppermute | solution.py:41
  36.7 10.9 %collective-permute-start.4 = (bf16[96,1536]{1,0:T(8,128)(2,1)S(1)}, bf16[96,1536]{1,0:T(8,128)(2,1)S(1)}, u32[]{:S(2)}, u32[]{:S(2)}) collective-permute-start(bf16[96,1536]{1,0:T(8,128)(2,1)S(1)} %shard_map.53.rest_1_), channel_id=1, source_target_pairs={{0,1},{1,2},{2,3},{3,4},{4,5},{5,6},{6,7},{7,8},{8,9},{9,10},{10,1... | collective-permute-start | bytes 884744 | tf_op jit(solution)/shard_map/ppermute | solution.py:41
  40.5 14.9 %collective-permute-start.10 = (bf16[160,1536]{1,0:T(8,128)(2,1)S(1)}, bf16[160,1536]{1,0:T(8,128)(2,1)S(1)}, u32[]{:S(2)}, u32[]{:S(2)}) collective-permute-start(bf16[160,1536]{1,0:T(8,128)(2,1)S(1)} %get-tuple-element.44.rest_2_), channel_id=1, source_target_pairs={{0,1},{1,2},{2,3},{3,4},{4,5},{5,6},{6,7},{7,8},{8,9},{9,10},{10,1... | collective-permute-start | bytes 1474568 | tf_op jit(solution)/shard_map/ppermute | solution.py:41
  41.8 15.0 %collective-permute-start.9 = (bf16[160,1536]{1,0:T(8,128)(2,1)S(1)}, bf16[160,1536]{1,0:T(8,128)(2,1)S(1)}, u32[]{:S(2)}, u32[]{:S(2)}) collective-permute-start(bf16[160,1536]{1,0:T(8,128)(2,1)S(1)} %get-tuple-element.44.rest_2_), channel_id=1, source_target_pairs={{15,13},{23,21}} | collective-permute-start | bytes 1474568 | tf_op jit(solution)/shard_map/ppermute | solution.py:41
  46.3 11.3 %collective-permute-start.8 = (bf16[128,1536]{1,0:T(8,128)(2,1)S(1)}, bf16[128,1536]{1,0:T(8,128)(2,1)S(1)}, u32[]{:S(2)}, u32[]{:S(2)}) collective-permute-start(bf16[128,1536]{1,0:T(8,128)(2,1)S(1)} %get-tuple-element.45.rest_1_), channel_id=1, source_target_pairs={{8,16},{9,17},{10,18},{11,19},{12,20},{13,21},{14,22},{15,23}} | collective-permute-start | bytes 1179656 | tf_op jit(solution)/shard_map/ppermute | solution.py:41
  49.0 10.7 %collective-permute-start.7 = (bf16[96,1536]{1,0:T(8,128)(2,1)S(1)}, bf16[96,1536]{1,0:T(8,128)(2,1)S(1)}, u32[]{:S(2)}, u32[]{:S(2)}) collective-permute-start(bf16[96,1536]{1,0:T(8,128)(2,1)S(1)} %shard_map.56.rest_1_), channel_id=1, source_target_pairs={{0,1},{1,2},{2,3},{3,4},{4,5},{5,6},{6,7},{7,8},{8,9},{9,10},{10,1... | collective-permute-start | bytes 884744 | tf_op jit(solution)/shard_map/ppermute | solution.py:41
  53.5 9.8 %collective-permute-start.15 = (bf16[128,1536]{1,0:T(8,128)(2,1)S(1)}, bf16[128,1536]{1,0:T(8,128)(2,1)S(1)}, u32[]{:S(2)}, u32[]{:S(2)}) collective-permute-start(bf16[128,1536]{1,0:T(8,128)(2,1)S(1)} %get-tuple-element.48.rest_2_), channel_id=1, source_target_pairs={{0,1},{1,2},{2,3},{3,4},{4,5},{5,6},{6,7},{7,8},{8,9},{9,10},{10,1... | collective-permute-start | bytes 1179656 | tf_op jit(solution)/shard_map/ppermute | solution.py:41
  55.5 22.2 %collective-permute-start.14 = (bf16[160,1536]{1,0:T(8,128)(2,1)S(1)}, bf16[160,1536]{1,0:T(8,128)(2,1)S(1)}, u32[]{:S(2)}, u32[]{:S(2)}) collective-permute-start(bf16[160,1536]{1,0:T(8,128)(2,1)S(1)} %get-tuple-element.49.rest_0_), channel_id=1, source_target_pairs={{8,16},{9,17},{10,18},{11,19},{12,20},{13,21},{14,22},{15,23}} | collective-permute-start | bytes 1474568 | tf_op jit(solution)/shard_map/ppermute | solution.py:41
  56.8 7.9 %collective-permute-start.13 = (bf16[160,1536]{1,0:T(8,128)(2,1)S(1)}, bf16[160,1536]{1,0:T(8,128)(2,1)S(1)}, u32[]{:S(2)}, u32[]{:S(2)}) collective-permute-start(bf16[160,1536]{1,0:T(8,128)(2,1)S(1)} %shard_map.59.rest_4_), channel_id=1, source_target_pairs={{13,16},{21,24}} | collective-permute-start | bytes 1474568 | tf_op jit(solution)/shard_map/ppermute | solution.py:41
  58.4 23.1 %collective-permute-start.18 = (bf16[128,1536]{1,0:T(8,128)(2,1)S(1)}, bf16[128,1536]{1,0:T(8,128)(2,1)S(1)}, u32[]{:S(2)}, u32[]{:S(2)}) collective-permute-start(bf16[128,1536]{1,0:T(8,128)(2,1)S(1)} %get-tuple-element.50.rest_1_), channel_id=1, source_target_pairs={{16,24},{17,25},{18,26},{19,27},{20,28},{21,29},{22,30},{23,31}} | collective-permute-start | bytes 1179656 | tf_op jit(solution)/shard_map/ppermute | solution.py:41
  61.2 18.9 %collective-permute-start.12 = (bf16[96,1536]{1,0:T(8,128)(2,1)S(1)}, bf16[96,1536]{1,0:T(8,128)(2,1)S(1)}, u32[]{:S(2)}, u32[]{:S(2)}) collective-permute-start(bf16[96,1536]{1,0:T(8,128)(2,1)S(1)} %get-tuple-element.52.rest_2_), channel_id=1, source_target_pairs={{0,1},{1,2},{2,3},{3,4},{4,5},{5,6},{6,7},{7,8},{8,9},{9,10},{10,1... | collective-permute-start | bytes 884744 | tf_op jit(solution)/shard_map/ppermute | solution.py:41
  63.4 26.1 %collective-permute-start.17 = (bf16[128,1536]{1,0:T(8,128)(2,1)S(1)}, bf16[128,1536]{1,0:T(8,128)(2,1)S(1)}, u32[]{:S(2)}, u32[]{:S(2)}) collective-permute-start(bf16[128,1536]{1,0:T(8,128)(2,1)S(1)} %get-tuple-element.55.rest_5_), channel_id=1, source_target_pairs={{8,16},{9,17},{10,18},{11,19},{12,20},{13,21},{14,22},{15,23}} | collective-permute-start | bytes 1179656 | tf_op jit(solution)/shard_map/ppermute | solution.py:41
  78.8 16.0 %collective-permute-start.21 = (bf16[160,1536]{1,0:T(8,128)(2,1)S(1)}, bf16[160,1536]{1,0:T(8,128)(2,1)S(1)}, u32[]{:S(2)}, u32[]{:S(2)}) collective-permute-start(bf16[160,1536]{1,0:T(8,128)(2,1)S(1)} %get-tuple-element.56.rest_2_), channel_id=1, source_target_pairs={{16,24},{17,25},{18,26},{19,27},{20,28},{21,29},{22,30},{23,31}} | collective-permute-start | bytes 1474568 | tf_op jit(solution)/shard_map/ppermute | solution.py:41
  80.2 12.5 %collective-permute-start.16 = (bf16[96,1536]{1,0:T(8,128)(2,1)S(1)}, bf16[96,1536]{1,0:T(8,128)(2,1)S(1)}, u32[]{:S(2)}, u32[]{:S(2)}) collective-permute-start(bf16[96,1536]{1,0:T(8,128)(2,1)S(1)} %get-tuple-element.57.rest_2_), channel_id=1, source_target_pairs={{8,16},{9,17},{10,18},{11,19},{12,20},{13,21},{14,22},{15,23}} | collective-permute-start | bytes 884744 | tf_op jit(solution)/shard_map/ppermute | solution.py:41
  90.4 7.3 %collective-permute-start.20 = (bf16[128,1536]{1,0:T(8,128)(2,1)S(1)}, bf16[128,1536]{1,0:T(8,128)(2,1)S(1)}, u32[]{:S(2)}, u32[]{:S(2)}) collective-permute-start(bf16[128,1536]{1,0:T(8,128)(2,1)S(1)} %get-tuple-element.62.rest_4_), channel_id=1, source_target_pairs={{16,24},{17,25},{18,26},{19,27},{20,28},{21,29},{22,30},{23,31}} | collective-permute-start | bytes 1179656 | tf_op jit(solution)/shard_map/ppermute | solution.py:41
  93.5 7.4 %collective-permute-start.19 = (bf16[96,1536]{1,0:T(8,128)(2,1)S(1)}, bf16[96,1536]{1,0:T(8,128)(2,1)S(1)}, u32[]{:S(2)}, u32[]{:S(2)}) collective-permute-start(bf16[96,1536]{1,0:T(8,128)(2,1)S(1)} %get-tuple-element.63.rest_4_), channel_id=1, source_target_pairs={{16,24},{17,25},{18,26},{19,27},{20,28},{21,29},{22,30},{23,31}} | collective-permute-start | bytes 884744 | tf_op jit(solution)/shard_map/ppermute | solution.py:41

commit v6 on v5

--- a/solution.py
+++ b/solution.py
@@ -17,7 +17,7 @@
 RELAYS = {7: 2, 8: 4}
 APART = ()
 UNDERWAY = 5
-TILE = 512
+TILE = 256
 ROWS_AT_ONCE = 128
 VMEM_BYTES = 20 << 20
 VMEM = pl.BlockSpec(memory_space=pltpu.VMEM)

time: 105 us -> 108 us (1.029)
  Pallas kernels: 35.8 us -> 38.6 us
    pallas_call x25, Pallas kernels: 35.8 us -> 38.6 us  [call(): pl.pallas_call(body, out_shape=outs, in_specs=specs, out_specs=out_specs...]
  transfers between devices with their start and end apart: 22 -> 22, of which waited for: 5 -> 5; matrix products, arithmetic and copies ran while one was open for 0% -> 0% of each run, Pallas kernels for 27% -> 26%
where the time goes in v6:
time: 108 us; the launch traced here: 106 us
  starting transfers between devices  46.6 us (43%)
  Pallas kernels  38.6 us (36%)
  waiting for transfers between devices  20.6 us (19%)
    ppermute x22, starting transfers between devices, passed_along(): return lax.ppermute(value, 'depth', pairs)  46.6 us
    pallas_call x25, Pallas kernels, call(): pl.pallas_call(body, out_shape=outs, in_specs=specs, out_specs=out_specs...  38.6 us
    ppermute x22, waiting for transfers between devices, passed_along(): return lax.ppermute(value, 'depth', pairs)  20.6 us
  transfers between devices with their start and end apart: 22, of which 5 were waited for; matrix products, arithmetic and copies ran while one was open for 0% of the time, Pallas kernels for 26%

profile of v6, /device:TPU:23, one launch (start us, length us, event | category | flops | bytes accessed | tf_op | source)
XLA Modules:
  0.0 106.5 jit_solution(10291592260784599915)
XLA Ops:
  0.0 7.9 %shard_map.46 = (bf16[128,1536]{1,0:T(8,128)(2,1)S(1)}, bf16[2,1536,1536]{2,1,0:T(8,128)(2,1)S(1)}, f32[8,1536]{1,0:T(8,128)S(1)}) custom-call(bf16[512,1536]{1,0:T(8,128)(2,1)} %bitcast.2, bf16[2,1536,1536]{2,1,0:T(8,128)(2,1)} %w_hbm.1, f32[2,1536]{1,0:T(2,128)} %b_hbm.1, f32[2]{0:T(128)} %h_hbm.1), custom_call_target="tpu_custom_call" | custom-call | flops 4831838208 | tf_op jit(solution)/shard_map/pallas_call | solution.py:252
  7.9 3.7 %collective-permute-start = (bf16[128,1536]{1,0:T(8,128)(2,1)S(1)}, bf16[128,1536]{1,0:T(8,128)(2,1)S(1)}, u32[]{:S(2)}, u32[]{:S(2)}) collective-permute-start(bf16[128,1536]{1,0:T(8,128)(2,1)S(1)} %get-tuple-element.41.rest_0_), channel_id=1, source_target_pairs={{0,1},{1,2},{2,3},{3,4},{4,5},{5,6},{6,7},{7,8},{8,9},{9,10},{10,1... | collective-permute-start | bytes 1179656 | tf_op jit(solution)/shard_map/ppermute | solution.py:41
  11.6 1.4 %shard_map.47.rest_0_ = bf16[128,1536]{1,0:T(8,128)(2,1)S(1)} custom-call(bf16[512,1536]{1,0:T(8,128)(2,1)S(1)} %bitcast.3, bf16[2,1536,1536]{2,1,0:T(8,128)(2,1)S(1)} %get-tuple-element.39.w_ref, f32[8,1536]{1,0:T(8,128)S(1)} %get-tuple-element.40.p_ref, bf16[128,1536]{1,0:T(8,128)(2,1)S(1)} %get-tuple-element.41.rest_0_), custom_call_target="tpu_custom_call" | custom-call | flops 4831838208 | tf_op jit(solution)/shard_map/pallas_call | solution.py:252
  13.0 1.9 %collective-permute-start.3 = (bf16[128,1536]{1,0:T(8,128)(2,1)S(1)}, bf16[128,1536]{1,0:T(8,128)(2,1)S(1)}, u32[]{:S(2)}, u32[]{:S(2)}) collective-permute-start(bf16[128,1536]{1,0:T(8,128)(2,1)S(1)} %shard_map.47.rest_0_), channel_id=1, source_target_pairs={{0,1},{1,2},{2,3},{3,4},{4,5},{5,6},{6,7},{7,8},{8,9},{9,10},{10,1... | collective-permute-start | bytes 1179656 | tf_op jit(solution)/shard_map/ppermute | solution.py:41
  15.0 1.7 %shard_map.48.rest_1_ = bf16[160,1536]{1,0:T(8,128)(2,1)S(1)} custom-call(bf16[512,1536]{1,0:T(8,128)(2,1)S(1)} %bitcast.4, bf16[2,1536,1536]{2,1,0:T(8,128)(2,1)S(1)} %get-tuple-element.39.w_ref, f32[8,1536]{1,0:T(8,128)S(1)} %get-tuple-element.40.p_ref, bf16[128,1536]{1,0:T(8,128)(2,1)S(1)} %shard_map.47.rest_0_), custom_call_target="tpu_custom_call" | custom-call | flops 4831838208 | tf_op jit(solution)/shard_map/pallas_call | solution.py:252
  16.7 3.5 %collective-permute-start.2 = (bf16[160,1536]{1,0:T(8,128)(2,1)S(1)}, bf16[160,1536]{1,0:T(8,128)(2,1)S(1)}, u32[]{:S(2)}, u32[]{:S(2)}) collective-permute-start(bf16[160,1536]{1,0:T(8,128)(2,1)S(1)} %shard_map.48.rest_1_), channel_id=1, source_target_pairs={{0,1},{1,2},{2,3},{3,4},{4,5},{5,6},{6,7},{7,8},{8,9},{9,10},{10,1... | collective-permute-start | bytes 1474568 | tf_op jit(solution)/shard_map/ppermute | solution.py:41
  21.6 2.3 %collective-permute-start.1 = (bf16[128,1536]{1,0:T(8,128)(2,1)S(1)}, bf16[128,1536]{1,0:T(8,128)(2,1)S(1)}, u32[]{:S(2)}, u32[]{:S(2)}) collective-permute-start(bf16[128,1536]{1,0:T(8,128)(2,1)S(1)} %shard_map.49.rest_1_), channel_id=1, source_target_pairs={{0,1},{1,2},{2,3},{3,4},{4,5},{5,6},{6,7},{7,8},{8,9},{9,10},{10,1... | collective-permute-start | bytes 1179656 | tf_op jit(solution)/shard_map/ppermute | solution.py:41
  25.3 3.2 %collective-permute-start.11 = (bf16[128,1536]{1,0:T(8,128)(2,1)S(1)}, bf16[128,1536]{1,0:T(8,128)(2,1)S(1)}, u32[]{:S(2)}, u32[]{:S(2)}) collective-permute-start(bf16[128,1536]{1,0:T(8,128)(2,1)S(1)} %shard_map.50.rest_1_), channel_id=1, source_target_pairs={{0,1},{1,2},{2,3},{3,4},{4,5},{5,6},{6,7},{7,8},{8,9},{9,10},{10,1... | collective-permute-start | bytes 1179656 | tf_op jit(solution)/shard_map/ppermute | solution.py:41
  28.5 1.7 %shard_map.51.rest_1_ = bf16[160,1536]{1,0:T(8,128)(2,1)S(1)} custom-call(bf16[512,1536]{1,0:T(8,128)(2,1)S(1)} %bitcast.7, bf16[2,1536,1536]{2,1,0:T(8,128)(2,1)S(1)} %get-tuple-element.39.w_ref, f32[8,1536]{1,0:T(8,128)S(1)} %get-tuple-element.40.p_ref, bf16[160,1536]{1,0:T(8,128)(2,1)S(1)} %collective-permute-done.2.rest_0_, ...), custom_call_target="tpu_custom_call" | custom-call | flops 4831838208 | tf_op jit(solution)/shard_map/pallas_call | solution.py:252
  30.2 3.6 %collective-permute-start.6 = (bf16[160,1536]{1,0:T(8,128)(2,1)S(1)}, bf16[160,1536]{1,0:T(8,128)(2,1)S(1)}, u32[]{:S(2)}, u32[]{:S(2)}) collective-permute-start(bf16[160,1536]{1,0:T(8,128)(2,1)S(1)} %shard_map.51.rest_1_), channel_id=1, source_target_pairs={{0,1},{1,2},{2,3},{3,4},{4,5},{5,6},{6,7},{7,8},{8,9},{9,10},{10,1... | collective-permute-start | bytes 1474568 | tf_op jit(solution)/shard_map/ppermute | solution.py:41
  35.3 2.7 %collective-permute-start.5 = (bf16[128,1536]{1,0:T(8,128)(2,1)S(1)}, bf16[128,1536]{1,0:T(8,128)(2,1)S(1)}, u32[]{:S(2)}, u32[]{:S(2)}) collective-permute-start(bf16[128,1536]{1,0:T(8,128)(2,1)S(1)} %get-tuple-element.42.rest_0_), channel_id=1, source_target_pairs={{0,1},{1,2},{2,3},{3,4},{4,5},{5,6},{6,7},{7,8},{8,9},{9,10},{10,1... | collective-permute-start | bytes 1179656 | tf_op jit(solution)/shard_map/ppermute | solution.py:41
  39.4 1.9 %collective-permute-start.4 = (bf16[96,1536]{1,0:T(8,128)(2,1)S(1)}, bf16[96,1536]{1,0:T(8,128)(2,1)S(1)}, u32[]{:S(2)}, u32[]{:S(2)}) collective-permute-start(bf16[96,1536]{1,0:T(8,128)(2,1)S(1)} %shard_map.53.rest_1_), channel_id=1, source_target_pairs={{0,1},{1,2},{2,3},{3,4},{4,5},{5,6},{6,7},{7,8},{8,9},{9,10},{10,1... | collective-permute-start | bytes 884744 | tf_op jit(solution)/shard_map/ppermute | solution.py:41
  41.3 1.7 %shard_map.54 = (bf16[160,1536]{1,0:T(8,128)(2,1)S(1)}, f32[160,1536]{1,0:T(8,128)S(1)}) custom-call(bf16[512,1536]{1,0:T(8,128)(2,1)S(1)} %bitcast.10, bf16[2,1536,1536]{2,1,0:T(8,128)(2,1)S(1)} %get-tuple-element.39.w_ref, f32[8,1536]{1,0:T(8,128)S(1)} %get-tuple-element.40.p_ref, bf16[160,1536]{1,0:T(8,128)(2,1)S(1)} %collective-permute-done.6.rest_0_, ...), custom_call_target="tpu_custom_call" | custom-call | flops 4831838208 | tf_op jit(solution)/shard_map/pallas_call | solution.py:252
  44.4 4.4 %collective-permute-start.9 = (bf16[160,1536]{1,0:T(8,128)(2,1)S(1)}, bf16[160,1536]{1,0:T(8,128)(2,1)S(1)}, u32[]{:S(2)}, u32[]{:S(2)}) collective-permute-start(bf16[160,1536]{1,0:T(8,128)(2,1)S(1)} %get-tuple-element.44.rest_2_), channel_id=1, source_target_pairs={{15,13},{23,21}} | collective-permute-start | bytes 1474568 | tf_op jit(solution)/shard_map/ppermute | solution.py:41
  51.6 3.1 %collective-permute-start.7 = (bf16[96,1536]{1,0:T(8,128)(2,1)S(1)}, bf16[96,1536]{1,0:T(8,128)(2,1)S(1)}, u32[]{:S(2)}, u32[]{:S(2)}) collective-permute-start(bf16[96,1536]{1,0:T(8,128)(2,1)S(1)} %shard_map.56.rest_1_), channel_id=1, source_target_pairs={{0,1},{1,2},{2,3},{3,4},{4,5},{5,6},{6,7},{7,8},{8,9},{9,10},{10,1... | collective-permute-start | bytes 884744 | tf_op jit(solution)/shard_map/ppermute | solution.py:41
  56.1 1.9 %collective-permute-start.15 = (bf16[128,1536]{1,0:T(8,128)(2,1)S(1)}, bf16[128,1536]{1,0:T(8,128)(2,1)S(1)}, u32[]{:S(2)}, u32[]{:S(2)}) collective-permute-start(bf16[128,1536]{1,0:T(8,128)(2,1)S(1)} %get-tuple-element.48.rest_2_), channel_id=1, source_target_pairs={{0,1},{1,2},{2,3},{3,4},{4,5},{5,6},{6,7},{7,8},{8,9},{9,10},{10,1... | collective-permute-start | bytes 1179656 | tf_op jit(solution)/shard_map/ppermute | solution.py:41
  62.3 1.4 %shard_map.61 = (bf16[96,1536]{1,0:T(8,128)(2,1)S(1)}, f32[96,1536]{1,0:T(8,128)S(1)}) custom-call(bf16[512,1536]{1,0:T(8,128)(2,1)S(1)} %bitcast.13, bf16[2,1536,1536]{2,1,0:T(8,128)(2,1)S(1)} %get-tuple-element.39.w_ref, f32[8,1536]{1,0:T(8,128)S(1)} %get-tuple-element.40.p_ref, bf16[96,1536]{1,0:T(8,128)(2,1)S(1)} %collective-permute-done.7.rest_0_, ...), custom_call_target="tpu_custom_call" | custom-call | flops 4831838208 | tf_op jit(solution)/shard_map/pallas_call | solution.py:252
  63.8 2.1 %collective-permute-start.12 = (bf16[96,1536]{1,0:T(8,128)(2,1)S(1)}, bf16[96,1536]{1,0:T(8,128)(2,1)S(1)}, u32[]{:S(2)}, u32[]{:S(2)}) collective-permute-start(bf16[96,1536]{1,0:T(8,128)(2,1)S(1)} %get-tuple-element.52.rest_2_), channel_id=1, source_target_pairs={{0,1},{1,2},{2,3},{3,4},{4,5},{5,6},{6,7},{7,8},{8,9},{9,10},{10,1... | collective-permute-start | bytes 884744 | tf_op jit(solution)/shard_map/ppermute | solution.py:41
  67.3 13.0 %collective-permute-done.14.rest_3_ = bf16[160,1536]{1,0:T(8,128)(2,1)S(1)} collective-permute-done((bf16[160,1536]{1,0:T(8,128)(2,1)S(1)}, bf16[160,1536]{1,0:T(8,128)(2,1)S(1)}, u32[]{:S(2)}, u32[]{:S(2)}) %collective-permute-start.14) | collective-permute-done | bytes 491552 | tf_op jit(solution)/shard_map/ppermute | solution.py:41
  84.3 2.3 %shard_map.65 = (bf16[2,512,1536]{2,1,0:T(8,128)(2,1)}, f32[8,128]{1,0:T(8,128)S(1)}) custom-call(bf16[512,1536]{1,0:T(8,128)(2,1)S(1)} %bitcast.14, bf16[2,1536,1536]{2,1,0:T(8,128)(2,1)S(1)} %get-tuple-element.39.w_ref, f32[8,1536]{1,0:T(8,128)S(1)} %get-tuple-element.40.p_ref, bf16[128,1536]{1,0:T(8,128)(2,1)S(1)} %collective-permute-done.18.moved_ref, ...), custom_call_target="tpu_custom_call" | custom-call | flops 4831838208 | tf_op jit(solution)/shard_map/pallas_call | solution.py:252
  86.6 5.5 %collective-permute-done.17.rest_2_ = bf16[128,1536]{1,0:T(8,128)(2,1)S(1)} collective-permute-done((bf16[128,1536]{1,0:T(8,128)(2,1)S(1)}, bf16[128,1536]{1,0:T(8,128)(2,1)S(1)}, u32[]{:S(2)}, u32[]{:S(2)}) %collective-permute-start.17) | collective-permute-done | bytes 393248 | tf_op jit(solution)/shard_map/ppermute | solution.py:41
  97.4 2.6 %shard_map.68 = (bf16[2,512,1536]{2,1,0:T(8,128)(2,1)}, f32[8,128]{1,0:T(8,128)S(1)}) custom-call(bf16[512,1536]{1,0:T(8,128)(2,1)S(1)} %bitcast.15, bf16[2,1536,1536]{2,1,0:T(8,128)(2,1)S(1)} %get-tuple-element.39.w_ref, f32[8,1536]{1,0:T(8,128)S(1)} %get-tuple-element.40.p_ref, ...), custom_call_target="tpu_custom_call", output_to_operand_aliasing={{0}: (8, {})} | custom-call | flops 4831838208 | tf_op jit(solution)/shard_map/pallas_call | solution.py:252
  100.3 2.3 %shard_map.69 = (bf16[2,512,1536]{2,1,0:T(8,128)(2,1)}, f32[8,128]{1,0:T(8,128)S(1)}) custom-call(bf16[512,1536]{1,0:T(8,128)(2,1)S(1)} %bitcast.16, bf16[2,1536,1536]{2,1,0:T(8,128)(2,1)S(1)} %get-tuple-element.39.w_ref, f32[8,1536]{1,0:T(8,128)S(1)} %get-tuple-element.40.p_ref, ...), custom_call_target="tpu_custom_call", output_to_operand_aliasing={{0}: (7, {})} | custom-call | flops 4831838208 | tf_op jit(solution)/shard_map/pallas_call | solution.py:252
  103.4 2.8 %shard_map.70 = (bf16[2,512,1536]{2,1,0:T(8,128)(2,1)}, f32[8,128]{1,0:T(8,128)}) custom-call(bf16[512,1536]{1,0:T(8,128)(2,1)S(1)} %bitcast.17, bf16[2,1536,1536]{2,1,0:T(8,128)(2,1)S(1)} %get-tuple-element.39.w_ref, f32[8,1536]{1,0:T(8,128)S(1)} %get-tuple-element.40.p_ref, ...), custom_call_target="tpu_custom_call", output_to_operand_aliasing={{0}: (7, {})} | custom-call | flops 4831838208 | tf_op jit(solution)/shard_map/pallas_call | solution.py:252
  (47 shorter events, 27.0 us)
Async XLA Ops:
  0.0 11.6 %copy-start = (bf16[2,256,1536]{2,1,0:T(8,128)(2,1)S(1)}, bf16[2,256,1536]{2,1,0:T(8,128)(2,1)}, u32[]{:S(2)}) copy-start(bf16[2,256,1536]{2,1,0:T(8,128)(2,1)} %param.4) | copy-start | bytes 4718596
  7.9 12.3 %collective-permute-start = (bf16[128,1536]{1,0:T(8,128)(2,1)S(1)}, bf16[128,1536]{1,0:T(8,128)(2,1)S(1)}, u32[]{:S(2)}, u32[]{:S(2)}) collective-permute-start(bf16[128,1536]{1,0:T(8,128)(2,1)S(1)} %get-tuple-element.41.rest_0_), channel_id=1, source_target_pairs={{0,1},{1,2},{2,3},{3,4},{4,5},{5,6},{6,7},{7,8},{8,9},{9,10},{10,1... | collective-permute-start | bytes 1179656 | tf_op jit(solution)/shard_map/ppermute | solution.py:41
  13.0 10.9 %collective-permute-start.3 = (bf16[128,1536]{1,0:T(8,128)(2,1)S(1)}, bf16[128,1536]{1,0:T(8,128)(2,1)S(1)}, u32[]{:S(2)}, u32[]{:S(2)}) collective-permute-start(bf16[128,1536]{1,0:T(8,128)(2,1)S(1)} %shard_map.47.rest_0_), channel_id=1, source_target_pairs={{0,1},{1,2},{2,3},{3,4},{4,5},{5,6},{6,7},{7,8},{8,9},{9,10},{10,1... | collective-permute-start | bytes 1179656 | tf_op jit(solution)/shard_map/ppermute | solution.py:41
  16.7 11.8 %collective-permute-start.2 = (bf16[160,1536]{1,0:T(8,128)(2,1)S(1)}, bf16[160,1536]{1,0:T(8,128)(2,1)S(1)}, u32[]{:S(2)}, u32[]{:S(2)}) collective-permute-start(bf16[160,1536]{1,0:T(8,128)(2,1)S(1)} %shard_map.48.rest_1_), channel_id=1, source_target_pairs={{0,1},{1,2},{2,3},{3,4},{4,5},{5,6},{6,7},{7,8},{8,9},{9,10},{10,1... | collective-permute-start | bytes 1474568 | tf_op jit(solution)/shard_map/ppermute | solution.py:41
  21.6 12.2 %collective-permute-start.1 = (bf16[128,1536]{1,0:T(8,128)(2,1)S(1)}, bf16[128,1536]{1,0:T(8,128)(2,1)S(1)}, u32[]{:S(2)}, u32[]{:S(2)}) collective-permute-start(bf16[128,1536]{1,0:T(8,128)(2,1)S(1)} %shard_map.49.rest_1_), channel_id=1, source_target_pairs={{0,1},{1,2},{2,3},{3,4},{4,5},{5,6},{6,7},{7,8},{8,9},{9,10},{10,1... | collective-permute-start | bytes 1179656 | tf_op jit(solution)/shard_map/ppermute | solution.py:41
  25.3 29.3 %collective-permute-start.11 = (bf16[128,1536]{1,0:T(8,128)(2,1)S(1)}, bf16[128,1536]{1,0:T(8,128)(2,1)S(1)}, u32[]{:S(2)}, u32[]{:S(2)}) collective-permute-start(bf16[128,1536]{1,0:T(8,128)(2,1)S(1)} %shard_map.50.rest_1_), channel_id=1, source_target_pairs={{0,1},{1,2},{2,3},{3,4},{4,5},{5,6},{6,7},{7,8},{8,9},{9,10},{10,1... | collective-permute-start | bytes 1179656 | tf_op jit(solution)/shard_map/ppermute | solution.py:41
  30.2 11.1 %collective-permute-start.6 = (bf16[160,1536]{1,0:T(8,128)(2,1)S(1)}, bf16[160,1536]{1,0:T(8,128)(2,1)S(1)}, u32[]{:S(2)}, u32[]{:S(2)}) collective-permute-start(bf16[160,1536]{1,0:T(8,128)(2,1)S(1)} %shard_map.51.rest_1_), channel_id=1, source_target_pairs={{0,1},{1,2},{2,3},{3,4},{4,5},{5,6},{6,7},{7,8},{8,9},{9,10},{10,1... | collective-permute-start | bytes 1474568 | tf_op jit(solution)/shard_map/ppermute | solution.py:41
  35.3 13.5 %collective-permute-start.5 = (bf16[128,1536]{1,0:T(8,128)(2,1)S(1)}, bf16[128,1536]{1,0:T(8,128)(2,1)S(1)}, u32[]{:S(2)}, u32[]{:S(2)}) collective-permute-start(bf16[128,1536]{1,0:T(8,128)(2,1)S(1)} %get-tuple-element.42.rest_0_), channel_id=1, source_target_pairs={{0,1},{1,2},{2,3},{3,4},{4,5},{5,6},{6,7},{7,8},{8,9},{9,10},{10,1... | collective-permute-start | bytes 1179656 | tf_op jit(solution)/shard_map/ppermute | solution.py:41
  39.4 10.7 %collective-permute-start.4 = (bf16[96,1536]{1,0:T(8,128)(2,1)S(1)}, bf16[96,1536]{1,0:T(8,128)(2,1)S(1)}, u32[]{:S(2)}, u32[]{:S(2)}) collective-permute-start(bf16[96,1536]{1,0:T(8,128)(2,1)S(1)} %shard_map.53.rest_1_), channel_id=1, source_target_pairs={{0,1},{1,2},{2,3},{3,4},{4,5},{5,6},{6,7},{7,8},{8,9},{9,10},{10,1... | collective-permute-start | bytes 884744 | tf_op jit(solution)/shard_map/ppermute | solution.py:41
  43.1 14.9 %collective-permute-start.10 = (bf16[160,1536]{1,0:T(8,128)(2,1)S(1)}, bf16[160,1536]{1,0:T(8,128)(2,1)S(1)}, u32[]{:S(2)}, u32[]{:S(2)}) collective-permute-start(bf16[160,1536]{1,0:T(8,128)(2,1)S(1)} %get-tuple-element.44.rest_2_), channel_id=1, source_target_pairs={{0,1},{1,2},{2,3},{3,4},{4,5},{5,6},{6,7},{7,8},{8,9},{9,10},{10,1... | collective-permute-start | bytes 1474568 | tf_op jit(solution)/shard_map/ppermute | solution.py:41
  44.4 15.0 %collective-permute-start.9 = (bf16[160,1536]{1,0:T(8,128)(2,1)S(1)}, bf16[160,1536]{1,0:T(8,128)(2,1)S(1)}, u32[]{:S(2)}, u32[]{:S(2)}) collective-permute-start(bf16[160,1536]{1,0:T(8,128)(2,1)S(1)} %get-tuple-element.44.rest_2_), channel_id=1, source_target_pairs={{15,13},{23,21}} | collective-permute-start | bytes 1474568 | tf_op jit(solution)/shard_map/ppermute | solution.py:41
  48.8 11.3 %collective-permute-start.8 = (bf16[128,1536]{1,0:T(8,128)(2,1)S(1)}, bf16[128,1536]{1,0:T(8,128)(2,1)S(1)}, u32[]{:S(2)}, u32[]{:S(2)}) collective-permute-start(bf16[128,1536]{1,0:T(8,128)(2,1)S(1)} %get-tuple-element.45.rest_1_), channel_id=1, source_target_pairs={{8,16},{9,17},{10,18},{11,19},{12,20},{13,21},{14,22},{15,23}} | collective-permute-start | bytes 1179656 | tf_op jit(solution)/shard_map/ppermute | solution.py:41
  51.6 10.8 %collective-permute-start.7 = (bf16[96,1536]{1,0:T(8,128)(2,1)S(1)}, bf16[96,1536]{1,0:T(8,128)(2,1)S(1)}, u32[]{:S(2)}, u32[]{:S(2)}) collective-permute-start(bf16[96,1536]{1,0:T(8,128)(2,1)S(1)} %shard_map.56.rest_1_), channel_id=1, source_target_pairs={{0,1},{1,2},{2,3},{3,4},{4,5},{5,6},{6,7},{7,8},{8,9},{9,10},{10,1... | collective-permute-start | bytes 884744 | tf_op jit(solution)/shard_map/ppermute | solution.py:41
  56.1 9.8 %collective-permute-start.15 = (bf16[128,1536]{1,0:T(8,128)(2,1)S(1)}, bf16[128,1536]{1,0:T(8,128)(2,1)S(1)}, u32[]{:S(2)}, u32[]{:S(2)}) collective-permute-start(bf16[128,1536]{1,0:T(8,128)(2,1)S(1)} %get-tuple-element.48.rest_2_), channel_id=1, source_target_pairs={{0,1},{1,2},{2,3},{3,4},{4,5},{5,6},{6,7},{7,8},{8,9},{9,10},{10,1... | collective-permute-start | bytes 1179656 | tf_op jit(solution)/shard_map/ppermute | solution.py:41
  58.0 22.3 %collective-permute-start.14 = (bf16[160,1536]{1,0:T(8,128)(2,1)S(1)}, bf16[160,1536]{1,0:T(8,128)(2,1)S(1)}, u32[]{:S(2)}, u32[]{:S(2)}) collective-permute-start(bf16[160,1536]{1,0:T(8,128)(2,1)S(1)} %get-tuple-element.49.rest_0_), channel_id=1, source_target_pairs={{8,16},{9,17},{10,18},{11,19},{12,20},{13,21},{14,22},{15,23}} | collective-permute-start | bytes 1474568 | tf_op jit(solution)/shard_map/ppermute | solution.py:41
  59.4 7.9 %collective-permute-start.13 = (bf16[160,1536]{1,0:T(8,128)(2,1)S(1)}, bf16[160,1536]{1,0:T(8,128)(2,1)S(1)}, u32[]{:S(2)}, u32[]{:S(2)}) collective-permute-start(bf16[160,1536]{1,0:T(8,128)(2,1)S(1)} %shard_map.59.rest_4_), channel_id=1, source_target_pairs={{13,16},{21,24}} | collective-permute-start | bytes 1474568 | tf_op jit(solution)/shard_map/ppermute | solution.py:41
  61.0 23.3 %collective-permute-start.18 = (bf16[128,1536]{1,0:T(8,128)(2,1)S(1)}, bf16[128,1536]{1,0:T(8,128)(2,1)S(1)}, u32[]{:S(2)}, u32[]{:S(2)}) collective-permute-start(bf16[128,1536]{1,0:T(8,128)(2,1)S(1)} %get-tuple-element.50.rest_1_), channel_id=1, source_target_pairs={{16,24},{17,25},{18,26},{19,27},{20,28},{21,29},{22,30},{23,31}} | collective-permute-start | bytes 1179656 | tf_op jit(solution)/shard_map/ppermute | solution.py:41
  63.8 18.9 %collective-permute-start.12 = (bf16[96,1536]{1,0:T(8,128)(2,1)S(1)}, bf16[96,1536]{1,0:T(8,128)(2,1)S(1)}, u32[]{:S(2)}, u32[]{:S(2)}) collective-permute-start(bf16[96,1536]{1,0:T(8,128)(2,1)S(1)} %get-tuple-element.52.rest_2_), channel_id=1, source_target_pairs={{0,1},{1,2},{2,3},{3,4},{4,5},{5,6},{6,7},{7,8},{8,9},{9,10},{10,1... | collective-permute-start | bytes 884744 | tf_op jit(solution)/shard_map/ppermute | solution.py:41
  66.0 26.1 %collective-permute-start.17 = (bf16[128,1536]{1,0:T(8,128)(2,1)S(1)}, bf16[128,1536]{1,0:T(8,128)(2,1)S(1)}, u32[]{:S(2)}, u32[]{:S(2)}) collective-permute-start(bf16[128,1536]{1,0:T(8,128)(2,1)S(1)} %get-tuple-element.55.rest_5_), channel_id=1, source_target_pairs={{8,16},{9,17},{10,18},{11,19},{12,20},{13,21},{14,22},{15,23}} | collective-permute-start | bytes 1179656 | tf_op jit(solution)/shard_map/ppermute | solution.py:41
  81.4 16.0 %collective-permute-start.21 = (bf16[160,1536]{1,0:T(8,128)(2,1)S(1)}, bf16[160,1536]{1,0:T(8,128)(2,1)S(1)}, u32[]{:S(2)}, u32[]{:S(2)}) collective-permute-start(bf16[160,1536]{1,0:T(8,128)(2,1)S(1)} %get-tuple-element.56.rest_2_), channel_id=1, source_target_pairs={{16,24},{17,25},{18,26},{19,27},{20,28},{21,29},{22,30},{23,31}} | collective-permute-start | bytes 1474568 | tf_op jit(solution)/shard_map/ppermute | solution.py:41
  83.0 12.3 %collective-permute-start.16 = (bf16[96,1536]{1,0:T(8,128)(2,1)S(1)}, bf16[96,1536]{1,0:T(8,128)(2,1)S(1)}, u32[]{:S(2)}, u32[]{:S(2)}) collective-permute-start(bf16[96,1536]{1,0:T(8,128)(2,1)S(1)} %get-tuple-element.57.rest_2_), channel_id=1, source_target_pairs={{8,16},{9,17},{10,18},{11,19},{12,20},{13,21},{14,22},{15,23}} | collective-permute-start | bytes 884744 | tf_op jit(solution)/shard_map/ppermute | solution.py:41
  93.0 7.3 %collective-permute-start.20 = (bf16[128,1536]{1,0:T(8,128)(2,1)S(1)}, bf16[128,1536]{1,0:T(8,128)(2,1)S(1)}, u32[]{:S(2)}, u32[]{:S(2)}) collective-permute-start(bf16[128,1536]{1,0:T(8,128)(2,1)S(1)} %get-tuple-element.62.rest_4_), channel_id=1, source_target_pairs={{16,24},{17,25},{18,26},{19,27},{20,28},{21,29},{22,30},{23,31}} | collective-permute-start | bytes 1179656 | tf_op jit(solution)/shard_map/ppermute | solution.py:41
  96.1 7.4 %collective-permute-start.19 = (bf16[96,1536]{1,0:T(8,128)(2,1)S(1)}, bf16[96,1536]{1,0:T(8,128)(2,1)S(1)}, u32[]{:S(2)}, u32[]{:S(2)}) collective-permute-start(bf16[96,1536]{1,0:T(8,128)(2,1)S(1)} %get-tuple-element.63.rest_4_), channel_id=1, source_target_pairs={{16,24},{17,25},{18,26},{19,27},{20,28},{21,29},{22,30},{23,31}} | collective-permute-start | bytes 884744 | tf_op jit(solution)/shard_map/ppermute | solution.py:41

commit v7 on v5

--- a/solution.py
+++ b/solution.py
@@ -18,6 +18,7 @@
 APART = ()
 UNDERWAY = 5
 TILE = 512
+WEIGHT_TILE = 768
 ROWS_AT_ONCE = 128
 VMEM_BYTES = 20 << 20
 VMEM = pl.BlockSpec(memory_space=pltpu.VMEM)
@@ -41,8 +42,8 @@
     return lax.ppermute(value, "depth", pairs)
 
 
-def tiles(width):
-    tile = TILE if width % TILE == 0 else width
+def tiles(width, most=TILE):
+    tile = most if width % most == 0 else width
     return [slice(low, low + tile) for low in range(0, width, tile)]
 
 
@@ -62,7 +63,7 @@
         copy.start()
     copies = []
     for layer in range(LAY_DEV):
-        for cols in tiles(width):
+        for cols in tiles(width, WEIGHT_TILE):
             copy = pltpu.make_async_copy(
                 w_hbm.at[layer, :, cols], w_ref.at[layer, :, cols], w_sems.at[len(copies)]
             )
@@ -74,13 +75,13 @@
     for layer in range(LAY_DEV):
         p_ref[2 + layer : 3 + layer, :] = jnp.full((1, width), h_ref[layer], jnp.float32)
     p_ref[4:8, :] = jnp.zeros((4, width), jnp.float32)
-    for index, cols in enumerate(tiles(width)):
+    for index, cols in enumerate(tiles(width, WEIGHT_TILE)):
         copies[index].wait()
         moved = start[:, cols].astype(jnp.float32) + p_ref[2:3, cols] * bend(start[...], size, w_ref, p_ref, 0, cols)
         state[:, cols] = moved
         rounded[:, cols] = moved.astype(jnp.bfloat16)
-    for index, cols in enumerate(tiles(width)):
-        copies[len(tiles(width)) + index].wait()
+    for index, cols in enumerate(tiles(width, WEIGHT_TILE)):
+        copies[len(tiles(width, WEIGHT_TILE)) + index].wait()
         bent = bend(rounded[...], size, w_ref, p_ref, 1, cols)
         out_ref[:, cols] = (state[:, cols] + p_ref[3:4, cols] * bent).astype(jnp.bfloat16)
 

time: 105 us -> 105 us (level)
  no operation moved by 1% of the time
where the time goes in v7:
time: 105 us; the launch traced here: 103 us
  starting transfers between devices  46.6 us (44%)
  Pallas kernels  35.4 us (34%)
  waiting for transfers between devices  20.7 us (20%)
    ppermute x22, starting transfers between devices, passed_along(): return lax.ppermute(value, 'depth', pairs)  46.6 us
    pallas_call x25, Pallas kernels, call(): pl.pallas_call(body, out_shape=outs, in_specs=specs, out_specs=out_specs...  35.4 us
    ppermute x22, waiting for transfers between devices, passed_along(): return lax.ppermute(value, 'depth', pairs)  20.7 us
  transfers between devices with their start and end apart: 22, of which 5 were waited for; matrix products, arithmetic and copies ran while one was open for 0% of the time, Pallas kernels for 27%

profile of v7, /device:TPU:23, one launch (start us, length us, event | category | flops | bytes accessed | tf_op | source)
XLA Modules:
  0.0 103.4 jit_solution(3675238006448614959)
XLA Ops:
  0.0 4.9 %shard_map.46 = (bf16[128,1536]{1,0:T(8,128)(2,1)S(1)}, bf16[2,1536,1536]{2,1,0:T(8,128)(2,1)S(1)}, f32[8,1536]{1,0:T(8,128)S(1)}) custom-call(bf16[512,1536]{1,0:T(8,128)(2,1)} %bitcast.2, bf16[2,1536,1536]{2,1,0:T(8,128)(2,1)} %w_hbm.1, f32[2,1536]{1,0:T(2,128)} %b_hbm.1, f32[2]{0:T(128)} %h_hbm.1), custom_call_target="tpu_custom_call" | custom-call | flops 4831838208 | tf_op jit(solution)/shard_map/pallas_call | solution.py:253
  4.9 3.7 %collective-permute-start = (bf16[128,1536]{1,0:T(8,128)(2,1)S(1)}, bf16[128,1536]{1,0:T(8,128)(2,1)S(1)}, u32[]{:S(2)}, u32[]{:S(2)}) collective-permute-start(bf16[128,1536]{1,0:T(8,128)(2,1)S(1)} %get-tuple-element.41.rest_0_), channel_id=1, source_target_pairs={{0,1},{1,2},{2,3},{3,4},{4,5},{5,6},{6,7},{7,8},{8,9},{9,10},{10,1... | collective-permute-start | bytes 1179656 | tf_op jit(solution)/shard_map/ppermute | solution.py:42
  10.0 1.9 %collective-permute-start.3 = (bf16[128,1536]{1,0:T(8,128)(2,1)S(1)}, bf16[128,1536]{1,0:T(8,128)(2,1)S(1)}, u32[]{:S(2)}, u32[]{:S(2)}) collective-permute-start(bf16[128,1536]{1,0:T(8,128)(2,1)S(1)} %shard_map.47.rest_0_), channel_id=1, source_target_pairs={{0,1},{1,2},{2,3},{3,4},{4,5},{5,6},{6,7},{7,8},{8,9},{9,10},{10,1... | collective-permute-start | bytes 1179656 | tf_op jit(solution)/shard_map/ppermute | solution.py:42
  11.9 1.7 %shard_map.48.rest_1_ = bf16[160,1536]{1,0:T(8,128)(2,1)S(1)} custom-call(bf16[512,1536]{1,0:T(8,128)(2,1)S(1)} %bitcast.4, bf16[2,1536,1536]{2,1,0:T(8,128)(2,1)S(1)} %get-tuple-element.39.w_ref, f32[8,1536]{1,0:T(8,128)S(1)} %get-tuple-element.40.p_ref, bf16[128,1536]{1,0:T(8,128)(2,1)S(1)} %shard_map.47.rest_0_), custom_call_target="tpu_custom_call" | custom-call | flops 4831838208 | tf_op jit(solution)/shard_map/pallas_call | solution.py:253
  13.7 3.5 %collective-permute-start.2 = (bf16[160,1536]{1,0:T(8,128)(2,1)S(1)}, bf16[160,1536]{1,0:T(8,128)(2,1)S(1)}, u32[]{:S(2)}, u32[]{:S(2)}) collective-permute-start(bf16[160,1536]{1,0:T(8,128)(2,1)S(1)} %shard_map.48.rest_1_), channel_id=1, source_target_pairs={{0,1},{1,2},{2,3},{3,4},{4,5},{5,6},{6,7},{7,8},{8,9},{9,10},{10,1... | collective-permute-start | bytes 1474568 | tf_op jit(solution)/shard_map/ppermute | solution.py:42
  18.6 2.3 %collective-permute-start.1 = (bf16[128,1536]{1,0:T(8,128)(2,1)S(1)}, bf16[128,1536]{1,0:T(8,128)(2,1)S(1)}, u32[]{:S(2)}, u32[]{:S(2)}) collective-permute-start(bf16[128,1536]{1,0:T(8,128)(2,1)S(1)} %shard_map.49.rest_1_), channel_id=1, source_target_pairs={{0,1},{1,2},{2,3},{3,4},{4,5},{5,6},{6,7},{7,8},{8,9},{9,10},{10,1... | collective-permute-start | bytes 1179656 | tf_op jit(solution)/shard_map/ppermute | solution.py:42
  22.3 3.2 %collective-permute-start.11 = (bf16[128,1536]{1,0:T(8,128)(2,1)S(1)}, bf16[128,1536]{1,0:T(8,128)(2,1)S(1)}, u32[]{:S(2)}, u32[]{:S(2)}) collective-permute-start(bf16[128,1536]{1,0:T(8,128)(2,1)S(1)} %shard_map.50.rest_1_), channel_id=1, source_target_pairs={{0,1},{1,2},{2,3},{3,4},{4,5},{5,6},{6,7},{7,8},{8,9},{9,10},{10,1... | collective-permute-start | bytes 1179656 | tf_op jit(solution)/shard_map/ppermute | solution.py:42
  25.5 1.7 %shard_map.51.rest_1_ = bf16[160,1536]{1,0:T(8,128)(2,1)S(1)} custom-call(bf16[512,1536]{1,0:T(8,128)(2,1)S(1)} %bitcast.7, bf16[2,1536,1536]{2,1,0:T(8,128)(2,1)S(1)} %get-tuple-element.39.w_ref, f32[8,1536]{1,0:T(8,128)S(1)} %get-tuple-element.40.p_ref, bf16[160,1536]{1,0:T(8,128)(2,1)S(1)} %collective-permute-done.2.rest_0_, ...), custom_call_target="tpu_custom_call" | custom-call | flops 4831838208 | tf_op jit(solution)/shard_map/pallas_call | solution.py:253
  27.3 3.6 %collective-permute-start.6 = (bf16[160,1536]{1,0:T(8,128)(2,1)S(1)}, bf16[160,1536]{1,0:T(8,128)(2,1)S(1)}, u32[]{:S(2)}, u32[]{:S(2)}) collective-permute-start(bf16[160,1536]{1,0:T(8,128)(2,1)S(1)} %shard_map.51.rest_1_), channel_id=1, source_target_pairs={{0,1},{1,2},{2,3},{3,4},{4,5},{5,6},{6,7},{7,8},{8,9},{9,10},{10,1... | collective-permute-start | bytes 1474568 | tf_op jit(solution)/shard_map/ppermute | solution.py:42
  32.3 2.5 %collective-permute-start.5 = (bf16[128,1536]{1,0:T(8,128)(2,1)S(1)}, bf16[128,1536]{1,0:T(8,128)(2,1)S(1)}, u32[]{:S(2)}, u32[]{:S(2)}) collective-permute-start(bf16[128,1536]{1,0:T(8,128)(2,1)S(1)} %get-tuple-element.42.rest_0_), channel_id=1, source_target_pairs={{0,1},{1,2},{2,3},{3,4},{4,5},{5,6},{6,7},{7,8},{8,9},{9,10},{10,1... | collective-permute-start | bytes 1179656 | tf_op jit(solution)/shard_map/ppermute | solution.py:42
  34.8 1.4 %shard_map.53.rest_1_ = bf16[96,1536]{1,0:T(8,128)(2,1)S(1)} custom-call(bf16[512,1536]{1,0:T(8,128)(2,1)S(1)} %bitcast.9, bf16[2,1536,1536]{2,1,0:T(8,128)(2,1)S(1)} %get-tuple-element.39.w_ref, f32[8,1536]{1,0:T(8,128)S(1)} %get-tuple-element.40.p_ref, bf16[128,1536]{1,0:T(8,128)(2,1)S(1)} %get-tuple-element.42.rest_0_), custom_call_target="tpu_custom_call" | custom-call | flops 4831838208 | tf_op jit(solution)/shard_map/pallas_call | solution.py:253
  36.2 2.1 %collective-permute-start.4 = (bf16[96,1536]{1,0:T(8,128)(2,1)S(1)}, bf16[96,1536]{1,0:T(8,128)(2,1)S(1)}, u32[]{:S(2)}, u32[]{:S(2)}) collective-permute-start(bf16[96,1536]{1,0:T(8,128)(2,1)S(1)} %shard_map.53.rest_1_), channel_id=1, source_target_pairs={{0,1},{1,2},{2,3},{3,4},{4,5},{5,6},{6,7},{7,8},{8,9},{9,10},{10,1... | collective-permute-start | bytes 884744 | tf_op jit(solution)/shard_map/ppermute | solution.py:42
  38.4 1.7 %shard_map.54 = (bf16[160,1536]{1,0:T(8,128)(2,1)S(1)}, f32[160,1536]{1,0:T(8,128)S(1)}) custom-call(bf16[512,1536]{1,0:T(8,128)(2,1)S(1)} %bitcast.10, bf16[2,1536,1536]{2,1,0:T(8,128)(2,1)S(1)} %get-tuple-element.39.w_ref, f32[8,1536]{1,0:T(8,128)S(1)} %get-tuple-element.40.p_ref, bf16[160,1536]{1,0:T(8,128)(2,1)S(1)} %collective-permute-done.6.rest_0_, ...), custom_call_target="tpu_custom_call" | custom-call | flops 4831838208 | tf_op jit(solution)/shard_map/pallas_call | solution.py:253
  41.4 4.4 %collective-permute-start.9 = (bf16[160,1536]{1,0:T(8,128)(2,1)S(1)}, bf16[160,1536]{1,0:T(8,128)(2,1)S(1)}, u32[]{:S(2)}, u32[]{:S(2)}) collective-permute-start(bf16[160,1536]{1,0:T(8,128)(2,1)S(1)} %get-tuple-element.44.rest_2_), channel_id=1, source_target_pairs={{15,13},{23,21}} | collective-permute-start | bytes 1474568 | tf_op jit(solution)/shard_map/ppermute | solution.py:42
  48.6 3.1 %collective-permute-start.7 = (bf16[96,1536]{1,0:T(8,128)(2,1)S(1)}, bf16[96,1536]{1,0:T(8,128)(2,1)S(1)}, u32[]{:S(2)}, u32[]{:S(2)}) collective-permute-start(bf16[96,1536]{1,0:T(8,128)(2,1)S(1)} %shard_map.56.rest_1_), channel_id=1, source_target_pairs={{0,1},{1,2},{2,3},{3,4},{4,5},{5,6},{6,7},{7,8},{8,9},{9,10},{10,1... | collective-permute-start | bytes 884744 | tf_op jit(solution)/shard_map/ppermute | solution.py:42
  53.1 1.9 %collective-permute-start.15 = (bf16[128,1536]{1,0:T(8,128)(2,1)S(1)}, bf16[128,1536]{1,0:T(8,128)(2,1)S(1)}, u32[]{:S(2)}, u32[]{:S(2)}) collective-permute-start(bf16[128,1536]{1,0:T(8,128)(2,1)S(1)} %get-tuple-element.48.rest_2_), channel_id=1, source_target_pairs={{0,1},{1,2},{2,3},{3,4},{4,5},{5,6},{6,7},{7,8},{8,9},{9,10},{10,1... | collective-permute-start | bytes 1179656 | tf_op jit(solution)/shard_map/ppermute | solution.py:42
  59.3 1.4 %shard_map.61 = (bf16[96,1536]{1,0:T(8,128)(2,1)S(1)}, f32[96,1536]{1,0:T(8,128)S(1)}) custom-call(bf16[512,1536]{1,0:T(8,128)(2,1)S(1)} %bitcast.13, bf16[2,1536,1536]{2,1,0:T(8,128)(2,1)S(1)} %get-tuple-element.39.w_ref, f32[8,1536]{1,0:T(8,128)S(1)} %get-tuple-element.40.p_ref, bf16[96,1536]{1,0:T(8,128)(2,1)S(1)} %collective-permute-done.7.rest_0_, ...), custom_call_target="tpu_custom_call" | custom-call | flops 4831838208 | tf_op jit(solution)/shard_map/pallas_call | solution.py:253
  60.8 2.1 %collective-permute-start.12 = (bf16[96,1536]{1,0:T(8,128)(2,1)S(1)}, bf16[96,1536]{1,0:T(8,128)(2,1)S(1)}, u32[]{:S(2)}, u32[]{:S(2)}) collective-permute-start(bf16[96,1536]{1,0:T(8,128)(2,1)S(1)} %get-tuple-element.52.rest_2_), channel_id=1, source_target_pairs={{0,1},{1,2},{2,3},{3,4},{4,5},{5,6},{6,7},{7,8},{8,9},{9,10},{10,1... | collective-permute-start | bytes 884744 | tf_op jit(solution)/shard_map/ppermute | solution.py:42
  64.3 13.0 %collective-permute-done.14.rest_3_ = bf16[160,1536]{1,0:T(8,128)(2,1)S(1)} collective-permute-done((bf16[160,1536]{1,0:T(8,128)(2,1)S(1)}, bf16[160,1536]{1,0:T(8,128)(2,1)S(1)}, u32[]{:S(2)}, u32[]{:S(2)}) %collective-permute-start.14) | collective-permute-done | bytes 491552 | tf_op jit(solution)/shard_map/ppermute | solution.py:42
  81.1 2.5 %shard_map.65 = (bf16[2,512,1536]{2,1,0:T(8,128)(2,1)}, f32[8,128]{1,0:T(8,128)S(1)}) custom-call(bf16[512,1536]{1,0:T(8,128)(2,1)S(1)} %bitcast.14, bf16[2,1536,1536]{2,1,0:T(8,128)(2,1)S(1)} %get-tuple-element.39.w_ref, f32[8,1536]{1,0:T(8,128)S(1)} %get-tuple-element.40.p_ref, bf16[128,1536]{1,0:T(8,128)(2,1)S(1)} %collective-permute-done.18.moved_ref, ...), custom_call_target="tpu_custom_call" | custom-call | flops 4831838208 | tf_op jit(solution)/shard_map/pallas_call | solution.py:253
  83.6 5.5 %collective-permute-done.17.rest_2_ = bf16[128,1536]{1,0:T(8,128)(2,1)S(1)} collective-permute-done((bf16[128,1536]{1,0:T(8,128)(2,1)S(1)}, bf16[128,1536]{1,0:T(8,128)(2,1)S(1)}, u32[]{:S(2)}, u32[]{:S(2)}) %collective-permute-start.17) | collective-permute-done | bytes 393248 | tf_op jit(solution)/shard_map/ppermute | solution.py:42
  94.4 2.6 %shard_map.68 = (bf16[2,512,1536]{2,1,0:T(8,128)(2,1)}, f32[8,128]{1,0:T(8,128)S(1)}) custom-call(bf16[512,1536]{1,0:T(8,128)(2,1)S(1)} %bitcast.15, bf16[2,1536,1536]{2,1,0:T(8,128)(2,1)S(1)} %get-tuple-element.39.w_ref, f32[8,1536]{1,0:T(8,128)S(1)} %get-tuple-element.40.p_ref, ...), custom_call_target="tpu_custom_call", output_to_operand_aliasing={{0}: (8, {})} | custom-call | flops 4831838208 | tf_op jit(solution)/shard_map/pallas_call | solution.py:253
  97.3 2.3 %shard_map.69 = (bf16[2,512,1536]{2,1,0:T(8,128)(2,1)}, f32[8,128]{1,0:T(8,128)S(1)}) custom-call(bf16[512,1536]{1,0:T(8,128)(2,1)S(1)} %bitcast.16, bf16[2,1536,1536]{2,1,0:T(8,128)(2,1)S(1)} %get-tuple-element.39.w_ref, f32[8,1536]{1,0:T(8,128)S(1)} %get-tuple-element.40.p_ref, ...), custom_call_target="tpu_custom_call", output_to_operand_aliasing={{0}: (7, {})} | custom-call | flops 4831838208 | tf_op jit(solution)/shard_map/pallas_call | solution.py:253
  100.5 2.8 %shard_map.70 = (bf16[2,512,1536]{2,1,0:T(8,128)(2,1)}, f32[8,128]{1,0:T(8,128)}) custom-call(bf16[512,1536]{1,0:T(8,128)(2,1)S(1)} %bitcast.17, bf16[2,1536,1536]{2,1,0:T(8,128)(2,1)S(1)} %get-tuple-element.39.w_ref, f32[8,1536]{1,0:T(8,128)S(1)} %get-tuple-element.40.p_ref, ...), custom_call_target="tpu_custom_call", output_to_operand_aliasing={{0}: (7, {})} | custom-call | flops 4831838208 | tf_op jit(solution)/shard_map/pallas_call | solution.py:253
  (47 shorter events, 26.9 us)
Async XLA Ops:
  0.0 8.6 %copy-start = (bf16[2,256,1536]{2,1,0:T(8,128)(2,1)S(1)}, bf16[2,256,1536]{2,1,0:T(8,128)(2,1)}, u32[]{:S(2)}) copy-start(bf16[2,256,1536]{2,1,0:T(8,128)(2,1)} %param.4) | copy-start | bytes 4718596
  4.9 12.3 %collective-permute-start = (bf16[128,1536]{1,0:T(8,128)(2,1)S(1)}, bf16[128,1536]{1,0:T(8,128)(2,1)S(1)}, u32[]{:S(2)}, u32[]{:S(2)}) collective-permute-start(bf16[128,1536]{1,0:T(8,128)(2,1)S(1)} %get-tuple-element.41.rest_0_), channel_id=1, source_target_pairs={{0,1},{1,2},{2,3},{3,4},{4,5},{5,6},{6,7},{7,8},{8,9},{9,10},{10,1... | collective-permute-start | bytes 1179656 | tf_op jit(solution)/shard_map/ppermute | solution.py:42
  10.0 10.9 %collective-permute-start.3 = (bf16[128,1536]{1,0:T(8,128)(2,1)S(1)}, bf16[128,1536]{1,0:T(8,128)(2,1)S(1)}, u32[]{:S(2)}, u32[]{:S(2)}) collective-permute-start(bf16[128,1536]{1,0:T(8,128)(2,1)S(1)} %shard_map.47.rest_0_), channel_id=1, source_target_pairs={{0,1},{1,2},{2,3},{3,4},{4,5},{5,6},{6,7},{7,8},{8,9},{9,10},{10,1... | collective-permute-start | bytes 1179656 | tf_op jit(solution)/shard_map/ppermute | solution.py:42
  13.7 11.9 %collective-permute-start.2 = (bf16[160,1536]{1,0:T(8,128)(2,1)S(1)}, bf16[160,1536]{1,0:T(8,128)(2,1)S(1)}, u32[]{:S(2)}, u32[]{:S(2)}) collective-permute-start(bf16[160,1536]{1,0:T(8,128)(2,1)S(1)} %shard_map.48.rest_1_), channel_id=1, source_target_pairs={{0,1},{1,2},{2,3},{3,4},{4,5},{5,6},{6,7},{7,8},{8,9},{9,10},{10,1... | collective-permute-start | bytes 1474568 | tf_op jit(solution)/shard_map/ppermute | solution.py:42
  18.6 12.2 %collective-permute-start.1 = (bf16[128,1536]{1,0:T(8,128)(2,1)S(1)}, bf16[128,1536]{1,0:T(8,128)(2,1)S(1)}, u32[]{:S(2)}, u32[]{:S(2)}) collective-permute-start(bf16[128,1536]{1,0:T(8,128)(2,1)S(1)} %shard_map.49.rest_1_), channel_id=1, source_target_pairs={{0,1},{1,2},{2,3},{3,4},{4,5},{5,6},{6,7},{7,8},{8,9},{9,10},{10,1... | collective-permute-start | bytes 1179656 | tf_op jit(solution)/shard_map/ppermute | solution.py:42
  22.3 29.3 %collective-permute-start.11 = (bf16[128,1536]{1,0:T(8,128)(2,1)S(1)}, bf16[128,1536]{1,0:T(8,128)(2,1)S(1)}, u32[]{:S(2)}, u32[]{:S(2)}) collective-permute-start(bf16[128,1536]{1,0:T(8,128)(2,1)S(1)} %shard_map.50.rest_1_), channel_id=1, source_target_pairs={{0,1},{1,2},{2,3},{3,4},{4,5},{5,6},{6,7},{7,8},{8,9},{9,10},{10,1... | collective-permute-start | bytes 1179656 | tf_op jit(solution)/shard_map/ppermute | solution.py:42
  27.3 11.1 %collective-permute-start.6 = (bf16[160,1536]{1,0:T(8,128)(2,1)S(1)}, bf16[160,1536]{1,0:T(8,128)(2,1)S(1)}, u32[]{:S(2)}, u32[]{:S(2)}) collective-permute-start(bf16[160,1536]{1,0:T(8,128)(2,1)S(1)} %shard_map.51.rest_1_), channel_id=1, source_target_pairs={{0,1},{1,2},{2,3},{3,4},{4,5},{5,6},{6,7},{7,8},{8,9},{9,10},{10,1... | collective-permute-start | bytes 1474568 | tf_op jit(solution)/shard_map/ppermute | solution.py:42
  32.3 13.5 %collective-permute-start.5 = (bf16[128,1536]{1,0:T(8,128)(2,1)S(1)}, bf16[128,1536]{1,0:T(8,128)(2,1)S(1)}, u32[]{:S(2)}, u32[]{:S(2)}) collective-permute-start(bf16[128,1536]{1,0:T(8,128)(2,1)S(1)} %get-tuple-element.42.rest_0_), channel_id=1, source_target_pairs={{0,1},{1,2},{2,3},{3,4},{4,5},{5,6},{6,7},{7,8},{8,9},{9,10},{10,1... | collective-permute-start | bytes 1179656 | tf_op jit(solution)/shard_map/ppermute | solution.py:42
  36.2 10.9 %collective-permute-start.4 = (bf16[96,1536]{1,0:T(8,128)(2,1)S(1)}, bf16[96,1536]{1,0:T(8,128)(2,1)S(1)}, u32[]{:S(2)}, u32[]{:S(2)}) collective-permute-start(bf16[96,1536]{1,0:T(8,128)(2,1)S(1)} %shard_map.53.rest_1_), channel_id=1, source_target_pairs={{0,1},{1,2},{2,3},{3,4},{4,5},{5,6},{6,7},{7,8},{8,9},{9,10},{10,1... | collective-permute-start | bytes 884744 | tf_op jit(solution)/shard_map/ppermute | solution.py:42
  40.1 14.9 %collective-permute-start.10 = (bf16[160,1536]{1,0:T(8,128)(2,1)S(1)}, bf16[160,1536]{1,0:T(8,128)(2,1)S(1)}, u32[]{:S(2)}, u32[]{:S(2)}) collective-permute-start(bf16[160,1536]{1,0:T(8,128)(2,1)S(1)} %get-tuple-element.44.rest_2_), channel_id=1, source_target_pairs={{0,1},{1,2},{2,3},{3,4},{4,5},{5,6},{6,7},{7,8},{8,9},{9,10},{10,1... | collective-permute-start | bytes 1474568 | tf_op jit(solution)/shard_map/ppermute | solution.py:42
  41.4 15.0 %collective-permute-start.9 = (bf16[160,1536]{1,0:T(8,128)(2,1)S(1)}, bf16[160,1536]{1,0:T(8,128)(2,1)S(1)}, u32[]{:S(2)}, u32[]{:S(2)}) collective-permute-start(bf16[160,1536]{1,0:T(8,128)(2,1)S(1)} %get-tuple-element.44.rest_2_), channel_id=1, source_target_pairs={{15,13},{23,21}} | collective-permute-start | bytes 1474568 | tf_op jit(solution)/shard_map/ppermute | solution.py:42
  45.8 11.3 %collective-permute-start.8 = (bf16[128,1536]{1,0:T(8,128)(2,1)S(1)}, bf16[128,1536]{1,0:T(8,128)(2,1)S(1)}, u32[]{:S(2)}, u32[]{:S(2)}) collective-permute-start(bf16[128,1536]{1,0:T(8,128)(2,1)S(1)} %get-tuple-element.45.rest_1_), channel_id=1, source_target_pairs={{8,16},{9,17},{10,18},{11,19},{12,20},{13,21},{14,22},{15,23}} | collective-permute-start | bytes 1179656 | tf_op jit(solution)/shard_map/ppermute | solution.py:42
  48.6 10.7 %collective-permute-start.7 = (bf16[96,1536]{1,0:T(8,128)(2,1)S(1)}, bf16[96,1536]{1,0:T(8,128)(2,1)S(1)}, u32[]{:S(2)}, u32[]{:S(2)}) collective-permute-start(bf16[96,1536]{1,0:T(8,128)(2,1)S(1)} %shard_map.56.rest_1_), channel_id=1, source_target_pairs={{0,1},{1,2},{2,3},{3,4},{4,5},{5,6},{6,7},{7,8},{8,9},{9,10},{10,1... | collective-permute-start | bytes 884744 | tf_op jit(solution)/shard_map/ppermute | solution.py:42
  53.1 9.8 %collective-permute-start.15 = (bf16[128,1536]{1,0:T(8,128)(2,1)S(1)}, bf16[128,1536]{1,0:T(8,128)(2,1)S(1)}, u32[]{:S(2)}, u32[]{:S(2)}) collective-permute-start(bf16[128,1536]{1,0:T(8,128)(2,1)S(1)} %get-tuple-element.48.rest_2_), channel_id=1, source_target_pairs={{0,1},{1,2},{2,3},{3,4},{4,5},{5,6},{6,7},{7,8},{8,9},{9,10},{10,1... | collective-permute-start | bytes 1179656 | tf_op jit(solution)/shard_map/ppermute | solution.py:42
  55.1 22.2 %collective-permute-start.14 = (bf16[160,1536]{1,0:T(8,128)(2,1)S(1)}, bf16[160,1536]{1,0:T(8,128)(2,1)S(1)}, u32[]{:S(2)}, u32[]{:S(2)}) collective-permute-start(bf16[160,1536]{1,0:T(8,128)(2,1)S(1)} %get-tuple-element.49.rest_0_), channel_id=1, source_target_pairs={{8,16},{9,17},{10,18},{11,19},{12,20},{13,21},{14,22},{15,23}} | collective-permute-start | bytes 1474568 | tf_op jit(solution)/shard_map/ppermute | solution.py:42
  56.4 7.9 %collective-permute-start.13 = (bf16[160,1536]{1,0:T(8,128)(2,1)S(1)}, bf16[160,1536]{1,0:T(8,128)(2,1)S(1)}, u32[]{:S(2)}, u32[]{:S(2)}) collective-permute-start(bf16[160,1536]{1,0:T(8,128)(2,1)S(1)} %shard_map.59.rest_4_), channel_id=1, source_target_pairs={{13,16},{21,24}} | collective-permute-start | bytes 1474568 | tf_op jit(solution)/shard_map/ppermute | solution.py:42
  58.0 23.1 %collective-permute-start.18 = (bf16[128,1536]{1,0:T(8,128)(2,1)S(1)}, bf16[128,1536]{1,0:T(8,128)(2,1)S(1)}, u32[]{:S(2)}, u32[]{:S(2)}) collective-permute-start(bf16[128,1536]{1,0:T(8,128)(2,1)S(1)} %get-tuple-element.50.rest_1_), channel_id=1, source_target_pairs={{16,24},{17,25},{18,26},{19,27},{20,28},{21,29},{22,30},{23,31}} | collective-permute-start | bytes 1179656 | tf_op jit(solution)/shard_map/ppermute | solution.py:42
  60.8 18.9 %collective-permute-start.12 = (bf16[96,1536]{1,0:T(8,128)(2,1)S(1)}, bf16[96,1536]{1,0:T(8,128)(2,1)S(1)}, u32[]{:S(2)}, u32[]{:S(2)}) collective-permute-start(bf16[96,1536]{1,0:T(8,128)(2,1)S(1)} %get-tuple-element.52.rest_2_), channel_id=1, source_target_pairs={{0,1},{1,2},{2,3},{3,4},{4,5},{5,6},{6,7},{7,8},{8,9},{9,10},{10,1... | collective-permute-start | bytes 884744 | tf_op jit(solution)/shard_map/ppermute | solution.py:42
  63.0 26.1 %collective-permute-start.17 = (bf16[128,1536]{1,0:T(8,128)(2,1)S(1)}, bf16[128,1536]{1,0:T(8,128)(2,1)S(1)}, u32[]{:S(2)}, u32[]{:S(2)}) collective-permute-start(bf16[128,1536]{1,0:T(8,128)(2,1)S(1)} %get-tuple-element.55.rest_5_), channel_id=1, source_target_pairs={{8,16},{9,17},{10,18},{11,19},{12,20},{13,21},{14,22},{15,23}} | collective-permute-start | bytes 1179656 | tf_op jit(solution)/shard_map/ppermute | solution.py:42
  78.4 16.0 %collective-permute-start.21 = (bf16[160,1536]{1,0:T(8,128)(2,1)S(1)}, bf16[160,1536]{1,0:T(8,128)(2,1)S(1)}, u32[]{:S(2)}, u32[]{:S(2)}) collective-permute-start(bf16[160,1536]{1,0:T(8,128)(2,1)S(1)} %get-tuple-element.56.rest_2_), channel_id=1, source_target_pairs={{16,24},{17,25},{18,26},{19,27},{20,28},{21,29},{22,30},{23,31}} | collective-permute-start | bytes 1474568 | tf_op jit(solution)/shard_map/ppermute | solution.py:42
  79.8 12.5 %collective-permute-start.16 = (bf16[96,1536]{1,0:T(8,128)(2,1)S(1)}, bf16[96,1536]{1,0:T(8,128)(2,1)S(1)}, u32[]{:S(2)}, u32[]{:S(2)}) collective-permute-start(bf16[96,1536]{1,0:T(8,128)(2,1)S(1)} %get-tuple-element.57.rest_2_), channel_id=1, source_target_pairs={{8,16},{9,17},{10,18},{11,19},{12,20},{13,21},{14,22},{15,23}} | collective-permute-start | bytes 884744 | tf_op jit(solution)/shard_map/ppermute | solution.py:42
  90.0 7.3 %collective-permute-start.20 = (bf16[128,1536]{1,0:T(8,128)(2,1)S(1)}, bf16[128,1536]{1,0:T(8,128)(2,1)S(1)}, u32[]{:S(2)}, u32[]{:S(2)}) collective-permute-start(bf16[128,1536]{1,0:T(8,128)(2,1)S(1)} %get-tuple-element.62.rest_4_), channel_id=1, source_target_pairs={{16,24},{17,25},{18,26},{19,27},{20,28},{21,29},{22,30},{23,31}} | collective-permute-start | bytes 1179656 | tf_op jit(solution)/shard_map/ppermute | solution.py:42
  93.1 7.4 %collective-permute-start.19 = (bf16[96,1536]{1,0:T(8,128)(2,1)S(1)}, bf16[96,1536]{1,0:T(8,128)(2,1)S(1)}, u32[]{:S(2)}, u32[]{:S(2)}) collective-permute-start(bf16[96,1536]{1,0:T(8,128)(2,1)S(1)} %get-tuple-element.63.rest_4_), channel_id=1, source_target_pairs={{16,24},{17,25},{18,26},{19,27},{20,28},{21,29},{22,30},{23,31}} | collective-permute-start | bytes 884744 | tf_op jit(solution)/shard_map/ppermute | solution.py:42
